TPU v7x, 32 devices: a whole 2x2x4 slice. The times are simulated.
32 devices in a mesh: grp: 4 (over y, x), dev: 8 (over z, core).
Axes of the slice: x: 2, y: 2, z: 4, core: 2. Of those that a mesh axis runs over, the one named last changes fastest.
Arguments:
- rhs: float32 [16, 32768], P(None, ('grp', 'dev')), may hold values from -6 to 6
- leaf_basis: float32 [64, 32768], P(None, ('grp', 'dev'))
- near_blocks: float32 [64, 65536], P(None, ('grp', 'dev')), may hold values from -0.75 to 0.75
- near_partner: int32 [512], P(('grp', 'dev')), may hold values from 0 to 511, as said below
- local_transfer: float32 [64, 61440], P(None, ('grp', 'dev'))
- local_coupling: float32 [64, 61440], P(None, ('grp', 'dev')), may hold values from -0.75 to 0.75
- far_partner: int32 [32, 30], P(('grp', 'dev')), may hold values from 0 to 511, as said below
- dev_transfer: float32 [4, 64, 896], P('grp')
- dev_coupling: float32 [4, 64, 896], P('grp'), may hold values from -4 to 4
- grp_transfer: float32 [64, 384], replicated
- grp_coupling: float32 [64, 384], replicated, may hold values from -6 to 6
Outputs:
- product: float32 [16, 32768], P(None, ('grp', 'dev'))
- root_factor: float32 [64, 64], replicated
Inputs may be any that keep to these rules, and one draw needn't show every extreme that they name: near_partner[l] is a leaf other than l, at most 16 leaves away; some leaf's partner is exactly 16 leaves away. `far_partner`: in row s, entry 2 * 16 - 2 * m + j (m = 16 >> k, level k, 0 <= j < m) names a node of level k other than node s * m + j and at most m nodes from it; at every level some entry is exactly m nodes away.
All inputs are finite; a program needn't handle non-finite values.
Results may differ from a plain program's by a relative error of at most 0.0001.
Values sent between devices are 32-bit elements; how exact they have to be, the bound alone decides.
No kernel may reach another device: no remote copies, remote signals or barrier semaphores. Data moves between devices by JAX's collectives and lax.ppermute only.
A program may use at most 64 MiB of HBM per device.

v0:
```python
import functools

import jax
import jax.numpy as jnp
from jax import lax
from jax.experimental import pallas as pl
from jax.experimental.pallas import tpu as pltpu
from jax.sharding import PartitionSpec as P

RANK = 64
LEAF = 64
NRHS = 16
LOC = 4
LEAF_DEV = 16
LOCAL_NODES = 30
PAIR = 2 * RANK
LANES = 128
BATCH = 32
ROWS = RANK + NRHS
PAIRS = LOCAL_NODES // 2
POINT_SPAN = LEAF_DEV * LEAF
NODE_SPAN = LOCAL_NODES * RANK
OFFSETS = [2 * LEAF_DEV - 2 * (LEAF_DEV >> level) for level in range(LOC)]
MIB = 1 << 20

precise = lax.Precision.HIGHEST


def mm(a, b):
    return lax.dot_general(
        a, b, (((1,), (0,)), ((), ())), precision=precise, preferred_element_type=jnp.float32
    )


def mm_t(a, b):
    return lax.dot_general(
        a, b, (((1,), (1,)), ((), ())), precision=precise, preferred_element_type=jnp.float32
    )


def low_half(rows):
    return lax.broadcasted_iota(jnp.int32, (rows, PAIR), 1) < RANK


def swap_halves(x):
    return pltpu.roll(x, RANK, 1)


def spread_pair(pair):
    low = low_half(pair.shape[0])
    return jnp.concatenate([jnp.where(low, pair, 0.0), jnp.where(low, 0.0, pair)], axis=0)


def stack_low(pair):
    low = low_half(pair.shape[0])
    return jnp.concatenate(
        [jnp.where(low, pair, 0.0), jnp.where(low, swap_halves(pair), 0.0)], axis=0
    )


def stack_high(pair):
    low = low_half(pair.shape[0])
    return jnp.concatenate(
        [jnp.where(low, 0.0, swap_halves(pair)), jnp.where(low, 0.0, pair)], axis=0
    )


def factor_batch(a, m):
    blocks = RANK // 8
    sub = lax.broadcasted_iota(jnp.int32, (8, LANES), 0)
    for kb in range(blocks):
        k0 = 8 * kb
        rows = [a[k0 + k, k0:RANK, :] for k in range(8)]
        mrows = []
        for k in range(8):
            unit = (sub == k).astype(jnp.float32)
            mrows.append(jnp.concatenate([m[k0 + k, 0:k0, :], unit], axis=0) if kb else unit)
        for k in range(8):
            scale = lax.rsqrt(rows[k][k : k + 1, :])
            rows[k] = rows[k] * scale
            mrows[k] = mrows[k] * scale
            for k2 in range(k + 1, 8):
                f = rows[k][k2 : k2 + 1, :]
                rows[k2] = rows[k2] - f * rows[k]
                mrows[k2] = mrows[k2] - f * mrows[k]
        for k in range(8):
            a[k0 + k, k0:RANK, :] = rows[k]
            m[k0 + k, 0 : k0 + 8, :] = mrows[k]
            if kb + 1 < blocks:
                m[k0 + k, k0 + 8 : RANK, :] = jnp.zeros((RANK - k0 - 8, LANES), jnp.float32)
        for ib in range(kb + 1, blocks):
            for i in range(8 * ib, 8 * ib + 8):
                acc = a[i, 8 * ib : RANK, :]
                old = m[i, 0:k0, :] if kb else None
                new = None
                for k in range(8):
                    f = a[k0 + k, i : i + 1, :]
                    acc = acc - f * a[k0 + k, 8 * ib : RANK, :]
                    part = f * m[k0 + k, 0 : k0 + 8, :]
                    if kb:
                        old = old - part[0:k0]
                    tail = part[k0 : k0 + 8]
                    new = -tail if new is None else new - tail
                a[i, 8 * ib : RANK, :] = acc
                if kb:
                    m[i, 0:k0, :] = old
                m[i, k0 : k0 + 8, :] = new


def invert_nodes(d, a, m, inv, count):
    for i in range(RANK):
        rows = d[pl.ds(i, count, stride=RANK), :]
        a[i, :, 0:count] = rows.T[0:RANK]
    factor_batch(a, m)
    for i in range(RANK):
        inv[pl.ds(i, count, stride=RANK), :] = m[i, :, 0:count].T


def gram_kernel(basis, rhs, transfer, gram, z_out, top):
    blocks = []
    zs = []
    for p in range(LEAF_DEV // 2):
        lanes = slice(PAIR * p, PAIR * (p + 1))
        u = basis[:, lanes]
        spread = spread_pair(u)
        full = mm(u.T, u)
        low = low_half(RANK)
        blocks.append(
            jnp.concatenate(
                [jnp.where(low, full[:RANK], 0.0), jnp.where(low, 0.0, full[RANK:])], axis=0
            )
        )
        zs.append(mm(rhs[:, lanes], spread))
    tile = 0
    for level in range(LOC):
        pairs = len(blocks)
        for p in range(pairs):
            gram[tile + p] = blocks[p]
            z_out[:, PAIR * (tile + p) : PAIR * (tile + p + 1)] = zs[p]
        next_blocks = []
        next_zs = []
        for q in range((pairs + 1) // 2):
            first = transfer[:, PAIR * (tile + 2 * q) : PAIR * (tile + 2 * q + 1)]
            f = stack_low(first)
            h = mm(blocks[2 * q], f)
            z = mm(zs[2 * q], f)
            parent = mm(f.T, h)
            if pairs > 1:
                second = transfer[:, PAIR * (tile + 2 * q + 1) : PAIR * (tile + 2 * q + 2)]
                f = stack_high(second)
                h = mm(blocks[2 * q + 1], f)
                z = z + mm(zs[2 * q + 1], f)
                parent = parent + mm(f.T, h)
            next_blocks.append(parent)
            next_zs.append(z)
        tile += pairs
        blocks = next_blocks
        zs = next_zs
    top[0:RANK, :] = blocks[0][0:RANK, 0:RANK]
    top[RANK:ROWS, :] = zs[0][:, 0:RANK]


def local_kernel(gram, z, rhs, inv, packed, d, a, m):
    for p in range(PAIRS):
        d[PAIR * p : PAIR * p + RANK, :] = gram[p, 0:RANK, :]
        d[PAIR * p + RANK : PAIR * (p + 1), :] = swap_halves(gram[p, RANK:PAIR, :])
    invert_nodes(d, a, m, inv, BATCH)
    packed[:, 0:POINT_SPAN] = rhs[...]
    for p in range(PAIRS):
        pair = z[:, PAIR * p : PAIR * (p + 1)]
        even = mm_t(pair[:, 0:RANK], inv[PAIR * p : PAIR * p + RANK, :])
        odd = mm_t(pair[:, RANK:PAIR], inv[PAIR * p + RANK : PAIR * (p + 1), :])
        packed[:, POINT_SPAN + PAIR * p : POINT_SPAN + PAIR * (p + 1)] = jnp.concatenate(
            [even, odd], axis=1
        )


def merge(nodes, tile, transfer):
    parents = []
    for p in range(len(nodes) // 2):
        pair = transfer[:, pl.ds(pl.multiple_of(PAIR * (tile + p), PAIR), PAIR)]
        even, odd = pair[:, 0:RANK], pair[:, RANK:PAIR]
        he, ho = mm(nodes[2 * p], even), mm(nodes[2 * p + 1], odd)
        g = mm(even.T, he[0:RANK]) + mm(odd.T, ho[0:RANK])
        parents.append(jnp.concatenate([g, he[RANK:] + ho[RANK:]], axis=0))
    return parents


def climb(blocks, place, start, bits, count, transfer, stack, records, first_record):
    for k, block in enumerate(blocks):
        stack[k] = block[...]
    here = lax.shift_right_logical(place, start)
    low = here & (2**bits - 1)
    base = here - low
    nodes = [stack[c ^ low] for c in range(2**bits)]
    for level in range(start, start + bits):
        m = count >> level
        own, sibling = (0, 1) if level == start else (low, low ^ 1)
        records[2 * (first_record + level - start)] = stack[own]
        records[2 * (first_record + level - start) + 1] = stack[sibling]
        tile = (2 * count - 2 * m + base) // 2
        nodes = merge(nodes, tile, transfer)
        low = lax.shift_right_logical(low, 1)
        base = lax.shift_right_logical(base, 1)
        for c, node in enumerate(nodes):
            stack[c] = node
    return nodes[0]


def climb_kernel(start, bits, count, place, transfer, *refs):
    blocks = refs[: 2**bits]
    top, records, stack = refs[2**bits :]
    top[...] = climb(blocks, place[0], start, bits, count, transfer, stack, records, 0)


def couple_kernel(
    place,
    near_partner,
    far_partner,
    own,
    lower,
    upper,
    inv,
    coupling,
    transfer,
    basis,
    near,
    base,
    lift,
    window,
):
    packed_tiles = (POINT_SPAN + NODE_SPAN) // PAIR
    point_tiles = POINT_SPAN // PAIR
    starts = [point_tiles + OFFSETS[level] // 2 for level in range(LOC)]
    spans = [(0, point_tiles)] + [(starts[level], (LEAF_DEV >> level) // 2) for level in range(LOC)]
    firsts = []
    slot = 0
    for start, span in spans:
        firsts.append(slot)
        for source in (lower, own, upper):
            for t in range(span):
                tile = source[:, PAIR * (start + t) : PAIR * (start + t + 1)]
                window[0, slot] = tile
                window[1, slot] = swap_halves(tile)
                slot += 1

    def pick(first, index, parity):
        return window[(index & 1) ^ parity, first + lax.shift_right_logical(index, 1)]

    low16 = low_half(NRHS)
    lifted = []
    for level in range(LOC):
        m = LEAF_DEV >> level
        tiles = []
        for p in range(m // 2):
            node = OFFSETS[level] + 2 * p
            sides = []
            for side in range(2):
                index = far_partner[0, node + side] - (place[0] - 1) * m
                value = pick(firsts[level + 1], index, 0)[:, 0:RANK]
                s = coupling[:, PAIR * (node // 2) : PAIR * (node // 2 + 1)]
                y = mm_t(value, s[:, RANK * side : RANK * (side + 1)])
                rows = slice(RANK * (node + side), RANK * (node + side + 1))
                sides.append(mm(y, inv[rows, :]))
            tiles.append(jnp.concatenate(sides, axis=1))
        lifted.append(tiles)

    state = None
    for level in reversed(range(LOC)):
        m = LEAF_DEV >> level
        tile = OFFSETS[level] // 2
        next_state = []
        for p in range(m // 2):
            pair = transfer[:, PAIR * (tile + p) : PAIR * (tile + p + 1)]
            if state is None:
                f = stack_low(pair)
                rows = f[:, 0:RANK].T
                next_state.append(jnp.concatenate([lifted[level][p], rows], axis=0))
                continue
            f = stack_high(pair) if p % 2 else stack_low(pair)
            rows = mm_t(state[p // 2], f)
            next_state.append(
                jnp.concatenate([rows[0:NRHS] + lifted[level][p], rows[NRHS:]], axis=0)
            )
        state = next_state

    for p in range(LEAF_DEV // 2):
        lanes = slice(PAIR * p, PAIR * (p + 1))
        out = mm_t(state[p], spread_pair(basis[:, lanes]))
        own_points = own[:, lanes]
        swapped = swap_halves(own_points)
        inputs = []
        for side in range(2):
            index = near_partner[2 * p + side] - (place[0] - 1) * LEAF_DEV
            value = pick(0, index, 1)
            inputs.append(jnp.where(low16, swapped if side else own_points, value))
        weights = jnp.concatenate(
            [
                near[:, 2 * PAIR * p : 2 * PAIR * p + PAIR],
                near[:, 2 * PAIR * p + PAIR : 2 * PAIR * (p + 1)],
            ],
            axis=0,
        )
        near_out = mm_t(jnp.concatenate(inputs, axis=0), weights)
        base[:, lanes] = out[0:NRHS] + jnp.where(low16, near_out[0:NRHS], near_out[NRHS:])
        lift[:, lanes] = out[NRHS:]


def half_of(array, index):
    pair = array[:, pl.ds(pl.multiple_of(PAIR * (index // 2), PAIR), PAIR)]
    return jnp.where(index % 2 == 1, pair[:, RANK:], pair[:, 0:RANK])


def top_kernel(
    grp_count,
    dev_count,
    start,
    bits,
    record_spans,
    place,
    grp_transfer,
    grp_coupling,
    dev_transfer,
    dev_coupling,
    base,
    lift,
    *refs,
):
    blocks = refs[: 2**bits]
    refs = refs[2**bits :]
    earlier = refs[: len(record_spans)]
    product, root, stack, records, d, a, m, inv = refs[len(record_spans) :]
    level = 0
    for ref, span in zip(earlier, record_spans):
        for r in range(2 * span):
            records[2 * level + r] = ref[r]
        level += span
    top = climb(
        blocks, place[0], start, bits, grp_count, grp_transfer, stack, records, level
    )
    levels = level + bits
    batch = inv.shape[0] // RANK
    for r in range(2 * levels):
        d[RANK * r : RANK * (r + 1), 0:RANK] = records[r, 0:RANK]
    d[RANK * 2 * levels : RANK * (2 * levels + 1), 0:RANK] = top[0:RANK]
    invert_nodes(d, a, m, inv, batch)
    root_inverse = inv[RANK * 2 * levels : RANK * (2 * levels + 1), :]
    keep = lax.broadcasted_iota(jnp.int32, (RANK, RANK), 0) >= lax.broadcasted_iota(
        jnp.int32, (RANK, RANK), 1
    )
    root[...] = jnp.where(keep, mm_t(top[0:RANK], root_inverse), 0.0)
    dev_levels = dev_count.bit_length() - 1
    terms = []
    for n in range(levels):
        if n < dev_levels:
            count, shift, spot = dev_count, n, place[1]
            transfer, coupling = dev_transfer, dev_coupling
        else:
            count, shift, spot = grp_count, n - dev_levels, place[0]
            transfer, coupling = grp_transfer, grp_coupling
        index = 2 * count - 2 * (count >> shift) + lax.shift_right_logical(spot, shift)
        other = records[2 * n + 1, RANK:ROWS]
        xhat = mm_t(other, inv[RANK * (2 * n + 1) : RANK * (2 * n + 2), :])
        yhat = mm_t(xhat, half_of(coupling, index))
        terms.append((mm(yhat, inv[RANK * 2 * n : RANK * (2 * n + 1), :]), half_of(transfer, index)))
    value = None
    for term, transfer in reversed(terms):
        value = term if value is None else term + mm_t(value, transfer)
    product[...] = base[...] + mm(value, lift[...])


def vmem(count):
    return [pl.BlockSpec(memory_space=pltpu.VMEM)] * count


def smem(count):
    return [pl.BlockSpec(memory_space=pltpu.SMEM)] * count


def f32(*shape):
    return jax.ShapeDtypeStruct(shape, jnp.float32)


def params(mib):
    return pltpu.CompilerParams(vmem_limit_bytes=mib * MIB)


def cost(flops, size):
    return pl.CostEstimate(flops=flops, bytes_accessed=size, transcendentals=0)


def exchange(block, axis, start, bits):
    count = lax.axis_size(axis)
    return [block] + [
        lax.ppermute(block, axis, [(i, i ^ (k << start)) for i in range(count)])
        for k in range(1, 2**bits)
    ]


def chunks(levels, first):
    out = []
    start = 0
    while start < levels:
        bits = min(first if start == 0 else 2, levels - start)
        out.append((start, bits))
        start += bits
    return out


def climb_call(blocks, place, start, bits, count, transfer):
    return pl.pallas_call(
        functools.partial(climb_kernel, start, bits, count),
        out_shape=[f32(ROWS, RANK), f32(2 * bits, ROWS, RANK)],
        in_specs=smem(1) + vmem(1 + 2**bits),
        out_specs=vmem(2),
        scratch_shapes=[pltpu.VMEM((2**bits, ROWS, RANK), jnp.float32)],
        compiler_params=params(8),
        name="climb",
    )(place, transfer, *blocks)


def shards(
    rhs,
    leaf_basis,
    near_blocks,
    near_partner,
    local_transfer,
    local_coupling,
    far_partner,
    dev_transfer,
    dev_coupling,
    grp_transfer,
    grp_coupling,
):
    dev_count = lax.axis_size("dev")
    grp_count = lax.axis_size("grp")
    dev_place = lax.axis_index("dev").astype(jnp.int32)
    grp_place = lax.axis_index("grp").astype(jnp.int32)
    places = jnp.stack([grp_place, dev_place])
    dev_spot = dev_place[None]
    device_spot = (grp_place * dev_count + dev_place)[None]

    gram, z, top = pl.pallas_call(
        gram_kernel,
        out_shape=[f32(PAIRS, PAIR, PAIR), f32(NRHS, NODE_SPAN), f32(ROWS, RANK)],
        in_specs=vmem(3),
        out_specs=vmem(3),
        compiler_params=params(16),
        name="gram",
    )(leaf_basis, rhs, local_transfer)

    records = []
    spans = []
    dev_transfer = dev_transfer[0]
    dev_coupling = dev_coupling[0]
    for start, bits in chunks(dev_count.bit_length() - 1, 1):
        blocks = exchange(top, "dev", start, bits)
        top, record = climb_call(blocks, dev_spot, start, bits, dev_count, dev_transfer)
        records.append(record)
        spans.append(bits)

    inv, packed = pl.pallas_call(
        local_kernel,
        out_shape=[f32(BATCH * RANK, RANK), f32(NRHS, POINT_SPAN + NODE_SPAN)],
        in_specs=vmem(3),
        out_specs=vmem(2),
        scratch_shapes=[
            pltpu.VMEM((BATCH * RANK, LANES), jnp.float32),
            pltpu.VMEM((RANK, RANK, LANES), jnp.float32),
            pltpu.VMEM((RANK, RANK, LANES), jnp.float32),
        ],
        compiler_params=params(24),
        name="local_factors",
    )(gram, z, rhs)

    both = ("grp", "dev")
    ends = grp_count * dev_count - 1
    lower = lax.ppermute(packed, both, [(i, i + 1) for i in range(ends)])
    upper = lax.ppermute(packed, both, [(i + 1, i) for i in range(ends)])

    window_tiles = 3 * (POINT_SPAN + NODE_SPAN) // PAIR
    base, lift = pl.pallas_call(
        couple_kernel,
        out_shape=[f32(NRHS, POINT_SPAN), f32(RANK, POINT_SPAN)],
        in_specs=smem(3) + vmem(8),
        out_specs=vmem(2),
        scratch_shapes=[pltpu.VMEM((2, window_tiles, NRHS, PAIR), jnp.float32)],
        compiler_params=params(24),
        name="couple",
    )(
        device_spot,
        near_partner,
        far_partner,
        packed,
        lower,
        upper,
        inv,
        local_coupling,
        local_transfer,
        leaf_basis,
        near_blocks,
    )

    grp_chunks = chunks(grp_count.bit_length() - 1, 2)
    for start, bits in grp_chunks[:-1]:
        blocks = exchange(top, "grp", start, bits)
        top, record = climb_call(blocks, grp_place[None], start, bits, grp_count, grp_transfer)
        records.append(record)
        spans.append(bits)
    start, bits = grp_chunks[-1]
    blocks = exchange(top, "grp", start, bits)
    levels = sum(spans) + bits
    batch = 8 * ((2 * levels + 1 + 7) // 8)
    return pl.pallas_call(
        functools.partial(top_kernel, grp_count, dev_count, start, bits, tuple(spans)),
        out_shape=[f32(NRHS, POINT_SPAN), f32(RANK, RANK)],
        in_specs=smem(1) + vmem(6 + len(blocks) + len(records)),
        out_specs=vmem(2),
        scratch_shapes=[
            pltpu.VMEM((2**bits, ROWS, RANK), jnp.float32),
            pltpu.VMEM((2 * levels, ROWS, RANK), jnp.float32),
            pltpu.VMEM((batch * RANK, LANES), jnp.float32),
            pltpu.VMEM((RANK, RANK, LANES), jnp.float32),
            pltpu.VMEM((RANK, RANK, LANES), jnp.float32),
            pltpu.VMEM((batch * RANK, RANK), jnp.float32),
        ],
        compiler_params=params(24),
        name="top",
    )(
        places,
        grp_transfer,
        grp_coupling,
        dev_transfer,
        dev_coupling,
        base,
        lift,
        *blocks,
        *records,
    )


def solution(mesh):
    return jax.shard_map(
        shards,
        mesh=mesh,
        in_specs=(
            P(None, ("grp", "dev")),
            P(None, ("grp", "dev")),
            P(None, ("grp", "dev")),
            P(("grp", "dev")),
            P(None, ("grp", "dev")),
            P(None, ("grp", "dev")),
            P(("grp", "dev"), None),
            P("grp", None, None),
            P("grp", None, None),
            P(),
            P(),
        ),
        out_specs=(P(None, ("grp", "dev")), P()),
        check_vma=False,
    )
```

profile of v0, /device:TPU:0, one launch (start us, length us, event | category | flops | bytes accessed | tf_op | source)
XLA Modules:
  0.0 67.9 jit_solution(887023898387426501)
XLA Ops:
  0.6 1.0 %copy-done.1 = f32[64,1920]{1,0:T(8,128)S(1)} copy-done((f32[64,1920]{1,0:T(8,128)S(1)}, f32[64,1920]{1,0:T(8,128)}, u32[]{:S(2)}) %copy-start.1) | copy-done | bytes 491544
  1.7 0.9 %copy-done.3 = f32[64,1024]{1,0:T(8,128)S(1)} copy-done((f32[64,1024]{1,0:T(8,128)S(1)}, f32[64,1024]{1,0:T(8,128)}, u32[]{:S(2)}) %copy-start.3) | copy-done | bytes 262168
  2.6 0.8 %copy-done.7 = f32[16,1024]{1,0:T(8,128)S(1)} copy-done((f32[16,1024]{1,0:T(8,128)S(1)}, f32[16,1024]{1,0:T(8,128)}, u32[]{:S(2)}) %copy-start.7) | copy-done | bytes 65560
  3.5 4.6 %gram.1 = (f32[15,128,128]{2,1,0:T(8,128)S(1)}, f32[16,1920]{1,0:T(8,128)S(1)}, f32[80,64]{1,0:T(8,128)S(1)}) custom-call(f32[64,1024]{1,0:T(8,128)S(1)} %copy-done.3, f32[16,1024]{1,0:T(8,128)S(1)} %copy-done.7, f32[64,1920]{1,0:T(8,128)S(1)} %copy-done.1), custom_call_target="tpu_custom_call" | custom-call | tf_op jit(solution)/shard_map/gram/pallas_call | solution.py:443
  8.0 0.0 copy-start.16
  8.1 0.0 copy-start.4
  8.1 0.0 copy-start.5
  8.1 7.8 %local_factors.1 = (f32[2048,64]{1,0:T(8,128)S(1)}, f32[16,2944]{1,0:T(8,128)S(1)}) custom-call(f32[15,128,128]{2,1,0:T(8,128)S(1)} %get-tuple-element.13.gram, f32[16,1920]{1,0:T(8,128)S(1)} %get-tuple-element.14.z, f32[16,1024]{1,0:T(8,128)S(1)} %copy-done.8), custom_call_target="tpu_custom_call" | custom-call | tf_op jit(solution)/shard_map/local_factors/pallas_call | solution.py:462
  16.0 2.5 %collective-permute-start = (f32[16,2944]{1,0:T(8,128)S(1)}, f32[16,2944]{1,0:T(8,128)S(1)}, u32[]{:S(2)}, u32[]{:S(2)}) collective-permute-start(f32[16,2944]{1,0:T(8,128)S(1)} %get-tuple-element.15.own), channel_id=1, source_target_pairs={{0,1},{1,2},{2,3},{3,4},{4,5},{5,6},{6,7},{7,8},{8,9},{9,10},{10,1... | collective-permute-start | bytes 565256 | tf_op jit(solution)/shard_map/ppermute | solution.py:478
  18.5 1.5 %collective-permute-start.1 = (f32[16,2944]{1,0:T(8,128)S(1)}, f32[16,2944]{1,0:T(8,128)}, u32[]{:S(2)}, u32[]{:S(2)}) collective-permute-start(f32[16,2944]{1,0:T(8,128)S(1)} %get-tuple-element.15.own), channel_id=1, source_target_pairs={{1,0},{2,1},{3,2},{4,3},{5,4},{6,5},{7,6},{8,7},{9,8},{10,9},{11,1... | collective-permute-start | bytes 565256 | tf_op jit(solution)/shard_map/ppermute | solution.py:479
  20.0 3.4 %collective-permute-start.2 = (f32[80,64]{1,0:T(8,128)S(1)}, f32[80,64]{1,0:T(8,128)S(1)}, u32[]{:S(2)}, u32[]{:S(2)}) collective-permute-start(f32[80,64]{1,0:T(8,128)S(1)} %get-tuple-element.19.refs_0_), channel_id=1, source_target_pairs={{0,1},{1,0},{2,3},{3,2},{4,5},{5,4},{6,7},{7,6},{8,9},{9,8},{10,11... | collective-permute-start | bytes 61448 | tf_op jit(solution)/shard_map/ppermute | solution.py:395
  23.4 0.9 %collective-permute-done.2.refs_1_ = f32[80,64]{1,0:T(8,128)S(1)} collective-permute-done((f32[80,64]{1,0:T(8,128)S(1)}, f32[80,64]{1,0:T(8,128)S(1)}, u32[]{:S(2)}, u32[]{:S(2)}) %collective-permute-start.2) | collective-permute-done | bytes 20512 | tf_op jit(solution)/shard_map/ppermute | solution.py:395
  24.2 0.6 copy-done.18
  24.9 0.8 %copy-done.17 = f32[80,64]{1,0:T(8,128)S(1)} copy-done((f32[80,64]{1,0:T(8,128)S(1)}, f32[80,64]{1,0:T(8,128)}, u32[]{:S(2)}) %copy-start.17) | copy-done | bytes 20504
  25.6 0.8 %copy-done.19 = f32[80,64]{1,0:T(8,128)S(1)} copy-done((f32[80,64]{1,0:T(8,128)S(1)}, f32[80,64]{1,0:T(8,128)}, u32[]{:S(2)}) %copy-start.19) | copy-done | bytes 20504
  26.4 0.5 climb.2
  26.9 2.0 %collective-permute-start.3 = (f32[80,64]{1,0:T(8,128)S(1)}, f32[80,64]{1,0:T(8,128)}, u32[]{:S(2)}, u32[]{:S(2)}) collective-permute-start(f32[80,64]{1,0:T(8,128)S(1)} %get-tuple-element.20.refs_0_), channel_id=1, source_target_pairs={{0,2},{1,3},{2,0},{3,1},{4,6},{5,7},{6,4},{7,5},{8,10},{9,11},{10,... | collective-permute-start | bytes 61448 | tf_op jit(solution)/shard_map/ppermute | solution.py:395
  28.9 2.6 %collective-permute-start.4 = (f32[80,64]{1,0:T(8,128)S(1)}, f32[80,64]{1,0:T(8,128)}, u32[]{:S(2)}, u32[]{:S(2)}) collective-permute-start(f32[80,64]{1,0:T(8,128)S(1)} %get-tuple-element.20.refs_0_), channel_id=1, source_target_pairs={{0,4},{1,5},{2,6},{3,7},{4,0},{5,1},{6,2},{7,3},{8,12},{9,13},{10,... | collective-permute-start | bytes 61448 | tf_op jit(solution)/shard_map/ppermute | solution.py:395
  31.5 0.6 copy-done.14
  32.1 2.6 %collective-permute-done.4.refs_2_ = f32[80,64]{1,0:T(8,128)} collective-permute-done((f32[80,64]{1,0:T(8,128)S(1)}, f32[80,64]{1,0:T(8,128)}, u32[]{:S(2)}, u32[]{:S(2)}) %collective-permute-start.4) | collective-permute-done | bytes 20512 | tf_op jit(solution)/shard_map/ppermute | solution.py:395
  34.7 2.7 %collective-permute-done.5.refs_3_ = f32[80,64]{1,0:T(8,128)} collective-permute-done((f32[80,64]{1,0:T(8,128)S(1)}, f32[80,64]{1,0:T(8,128)}, u32[]{:S(2)}, u32[]{:S(2)}) %collective-permute-start.5) | collective-permute-done | bytes 20512 | tf_op jit(solution)/shard_map/ppermute | solution.py:395
  37.4 0.8 %copy-done.15 = f32[80,64]{1,0:T(8,128)S(1)} copy-done((f32[80,64]{1,0:T(8,128)S(1)}, f32[80,64]{1,0:T(8,128)}, u32[]{:S(2)}) %copy-start.15) | copy-done | bytes 20504
  38.1 2.0 %climb.3 = (f32[80,64]{1,0:T(8,128)S(1)}, f32[4,80,64]{2,1,0:T(8,128)S(1)}) custom-call(s32[1]{0:T(128)} %bitcast.1.place, f32[64,896]{1,0:T(8,128)S(1)} %bitcast.6, f32[80,64]{1,0:T(8,128)S(1)} %copy-done.15, f32[80,64]{1,0:T(8,128)} %collective-permute-done.3.refs_1_, f32[80,64]{1,0:T(8,128)} %collective-permute-done.4.refs_2_, ...), custom_call_target="tpu_custom_call" | custom-call | tf_op jit(solution)/shard_map/climb/pallas_call | solution.py:411
  40.2 0.7 copy-done.10
  40.9 1.5 %collective-permute-start.6 = (f32[80,64]{1,0:T(8,128)S(1)}, f32[80,64]{1,0:T(8,128)}, u32[]{:S(2)}, u32[]{:S(2)}) collective-permute-start(f32[80,64]{1,0:T(8,128)S(1)} %get-tuple-element.21.refs_0_), channel_id=1, source_target_pairs={{0,8},{8,0},{16,24},{24,16},{1,9},{9,1},{17,25},{25,17},{2,10},{10... | collective-permute-start | bytes 61448 | tf_op jit(solution)/shard_map/ppermute | solution.py:395
  42.4 1.5 %collective-permute-start.7 = (f32[80,64]{1,0:T(8,128)S(1)}, f32[80,64]{1,0:T(8,128)}, u32[]{:S(2)}, u32[]{:S(2)}) collective-permute-start(f32[80,64]{1,0:T(8,128)S(1)} %get-tuple-element.21.refs_0_), channel_id=1, source_target_pairs={{0,16},{8,24},{16,0},{24,8},{1,17},{9,25},{17,1},{25,9},{2,18},{10... | collective-permute-start | bytes 61448 | tf_op jit(solution)/shard_map/ppermute | solution.py:395
  43.9 0.5 collective-permute-start.8
  44.4 0.1 pad_add_fusion.place
  44.5 0.6 copy-done.20
  45.1 0.0 copy-done.21
  45.1 12.9 %couple.1 = (f32[16,1024]{1,0:T(8,128)S(1)}, f32[64,1024]{1,0:T(8,128)S(1)}) custom-call(s32[1]{0:T(128)} %bitcast.4.place, s32[16]{0:T(128)S(1)} %copy-done.20, s32[1,30]{1,0:T(1,128)S(1)} %copy-done.21, f32[16,2944]{1,0:T(8,128)S(1)} %get-tuple-element.15.own, f32[16,2944]{1,0:T(8,128)S(1)} %collective-permute-done.lower, ...), custom_call_target="tpu_custom_call" | custom-call | tf_op jit(solution)/shard_map/couple/pallas_call | solution.py:482
  58.1 9.8 %top.1 = (f32[16,1024]{1,0:T(8,128)}, f32[64,64]{1,0:T(8,128)}) custom-call(s32[2]{0:T(128)S(1)} %pad_add_fusion.place, f32[64,384]{1,0:T(8,128)S(1)} %copy-done.12, f32[64,384]{1,0:T(8,128)S(1)} %copy-done.13, f32[64,896]{1,0:T(8,128)S(1)} %bitcast.7, f32[64,896]{1,0:T(8,128)S(1)} %bitcast.8, f32[16,1024]{1,0:T(8,128)S(1)} %get-tuple-element.17.base, ...), custom_call_target="tpu_custom_call" | custom-call | tf_op jit(solution)/shard_map/top/pallas_call | solution.py:514
  (37 shorter events, 0.1 us)
Async XLA Ops:
  0.6 1.0 %copy-start.1 = (f32[64,1920]{1,0:T(8,128)S(1)}, f32[64,1920]{1,0:T(8,128)}, u32[]{:S(2)}) copy-start(f32[64,1920]{1,0:T(8,128)} %transfer.3) | copy-start | bytes 1474564
  1.7 0.9 %copy-start.3 = (f32[64,1024]{1,0:T(8,128)S(1)}, f32[64,1024]{1,0:T(8,128)}, u32[]{:S(2)}) copy-start(f32[64,1024]{1,0:T(8,128)} %basis.3) | copy-start | bytes 786436
  2.6 0.8 %copy-start.7 = (f32[16,1024]{1,0:T(8,128)S(1)}, f32[16,1024]{1,0:T(8,128)}, u32[]{:S(2)}) copy-start(f32[16,1024]{1,0:T(8,128)} %rhs.3) | copy-start | bytes 196612
  3.5 4.6 %copy-start.8 = (f32[16,1024]{1,0:T(8,128)S(1)}, f32[16,1024]{1,0:T(8,128)}, u32[]{:S(2)}) copy-start(f32[16,1024]{1,0:T(8,128)} %rhs.3) | copy-start | bytes 196612
  3.5 41.0 %copy-start.6 = (f32[64,1920]{1,0:T(8,128)S(1)}, f32[64,1920]{1,0:T(8,128)}, u32[]{:S(2)}) copy-start(f32[64,1920]{1,0:T(8,128)} %coupling.1) | copy-start | bytes 1474564
  8.0 11.9 %copy-start.16 = (f32[80,64]{1,0:T(8,128)}, f32[80,64]{1,0:T(8,128)S(1)}, u32[]{:S(2)}) copy-start(f32[80,64]{1,0:T(8,128)S(1)} %get-tuple-element.19.refs_0_) | copy-start | bytes 61444
  8.1 16.8 %copy-start = (f32[1,64,896]{2,1,0:T(8,128)S(1)}, f32[1,64,896]{2,1,0:T(8,128)}, u32[]{:S(2)}) copy-start(f32[1,64,896]{2,1,0:T(8,128)} %param.18) | copy-start | bytes 688132
  8.1 36.4 %copy-start.4 = (f32[64,1024]{1,0:T(8,128)S(1)}, f32[64,1024]{1,0:T(8,128)}, u32[]{:S(2)}) copy-start(f32[64,1024]{1,0:T(8,128)} %basis.3) | copy-start | bytes 786436
  8.1 36.4 %copy-start.5 = (f32[64,2048]{1,0:T(8,128)S(1)}, f32[64,2048]{1,0:T(8,128)}, u32[]{:S(2)}) copy-start(f32[64,2048]{1,0:T(8,128)} %near.1) | copy-start | bytes 1572868
  15.9 28.5 %copy-start.2 = (f32[64,1920]{1,0:T(8,128)S(1)}, f32[64,1920]{1,0:T(8,128)}, u32[]{:S(2)}) copy-start(f32[64,1920]{1,0:T(8,128)} %transfer.3) | copy-start | bytes 1474564
  16.0 28.5 %collective-permute-start = (f32[16,2944]{1,0:T(8,128)S(1)}, f32[16,2944]{1,0:T(8,128)S(1)}, u32[]{:S(2)}, u32[]{:S(2)}) collective-permute-start(f32[16,2944]{1,0:T(8,128)S(1)} %get-tuple-element.15.own), channel_id=1, source_target_pairs={{0,1},{1,2},{2,3},{3,4},{4,5},{5,6},{6,7},{7,8},{8,9},{9,10},{10,1... | collective-permute-start | bytes 565256 | tf_op jit(solution)/shard_map/ppermute | solution.py:478
  18.5 25.9 %collective-permute-start.1 = (f32[16,2944]{1,0:T(8,128)S(1)}, f32[16,2944]{1,0:T(8,128)}, u32[]{:S(2)}, u32[]{:S(2)}) collective-permute-start(f32[16,2944]{1,0:T(8,128)S(1)} %get-tuple-element.15.own), channel_id=1, source_target_pairs={{1,0},{2,1},{3,2},{4,3},{5,4},{6,5},{7,6},{8,7},{9,8},{10,9},{11,1... | collective-permute-start | bytes 565256 | tf_op jit(solution)/shard_map/ppermute | solution.py:479
  20.0 4.2 %collective-permute-start.2 = (f32[80,64]{1,0:T(8,128)S(1)}, f32[80,64]{1,0:T(8,128)S(1)}, u32[]{:S(2)}, u32[]{:S(2)}) collective-permute-start(f32[80,64]{1,0:T(8,128)S(1)} %get-tuple-element.19.refs_0_), channel_id=1, source_target_pairs={{0,1},{1,0},{2,3},{3,2},{4,5},{5,4},{6,7},{7,6},{8,9},{9,8},{10,11... | collective-permute-start | bytes 61448 | tf_op jit(solution)/shard_map/ppermute | solution.py:395
  24.2 0.6 copy-start.18
  24.9 0.8 %copy-start.17 = (f32[80,64]{1,0:T(8,128)S(1)}, f32[80,64]{1,0:T(8,128)}, u32[]{:S(2)}) copy-start(f32[80,64]{1,0:T(8,128)} %copy-done.16) | copy-start | bytes 61444
  25.6 0.8 %copy-start.19 = (f32[80,64]{1,0:T(8,128)S(1)}, f32[80,64]{1,0:T(8,128)}, u32[]{:S(2)}) copy-start(f32[80,64]{1,0:T(8,128)} %copy-done.18) | copy-start | bytes 61444
  26.9 5.2 %collective-permute-start.3 = (f32[80,64]{1,0:T(8,128)S(1)}, f32[80,64]{1,0:T(8,128)}, u32[]{:S(2)}, u32[]{:S(2)}) collective-permute-start(f32[80,64]{1,0:T(8,128)S(1)} %get-tuple-element.20.refs_0_), channel_id=1, source_target_pairs={{0,2},{1,3},{2,0},{3,1},{4,6},{5,7},{6,4},{7,5},{8,10},{9,11},{10,... | collective-permute-start | bytes 61448 | tf_op jit(solution)/shard_map/ppermute | solution.py:395
  28.9 5.8 %collective-permute-start.4 = (f32[80,64]{1,0:T(8,128)S(1)}, f32[80,64]{1,0:T(8,128)}, u32[]{:S(2)}, u32[]{:S(2)}) collective-permute-start(f32[80,64]{1,0:T(8,128)S(1)} %get-tuple-element.20.refs_0_), channel_id=1, source_target_pairs={{0,4},{1,5},{2,6},{3,7},{4,0},{5,1},{6,2},{7,3},{8,12},{9,13},{10,... | collective-permute-start | bytes 61448 | tf_op jit(solution)/shard_map/ppermute | solution.py:395
  31.5 5.9 %collective-permute-start.5 = (f32[80,64]{1,0:T(8,128)S(1)}, f32[80,64]{1,0:T(8,128)}, u32[]{:S(2)}, u32[]{:S(2)}) collective-permute-start(f32[80,64]{1,0:T(8,128)S(1)} %get-tuple-element.20.refs_0_), channel_id=1, source_target_pairs={{0,6},{1,7},{2,4},{3,5},{4,2},{5,3},{6,0},{7,1},{8,14},{9,15},{10,... | collective-permute-start | bytes 61448 | tf_op jit(solution)/shard_map/ppermute | solution.py:395
  31.5 0.6 copy-start.14
  37.4 0.8 %copy-start.15 = (f32[80,64]{1,0:T(8,128)S(1)}, f32[80,64]{1,0:T(8,128)}, u32[]{:S(2)}) copy-start(f32[80,64]{1,0:T(8,128)} %copy-done.14) | copy-start | bytes 61444
  40.2 0.7 copy-start.10
  40.9 17.2 %collective-permute-start.6 = (f32[80,64]{1,0:T(8,128)S(1)}, f32[80,64]{1,0:T(8,128)}, u32[]{:S(2)}, u32[]{:S(2)}) collective-permute-start(f32[80,64]{1,0:T(8,128)S(1)} %get-tuple-element.21.refs_0_), channel_id=1, source_target_pairs={{0,8},{8,0},{16,24},{24,16},{1,9},{9,1},{17,25},{25,17},{2,10},{10... | collective-permute-start | bytes 61448 | tf_op jit(solution)/shard_map/ppermute | solution.py:395
  42.4 15.7 %collective-permute-start.7 = (f32[80,64]{1,0:T(8,128)S(1)}, f32[80,64]{1,0:T(8,128)}, u32[]{:S(2)}, u32[]{:S(2)}) collective-permute-start(f32[80,64]{1,0:T(8,128)S(1)} %get-tuple-element.21.refs_0_), channel_id=1, source_target_pairs={{0,16},{8,24},{16,0},{24,8},{1,17},{9,25},{17,1},{25,9},{2,18},{10... | collective-permute-start | bytes 61448 | tf_op jit(solution)/shard_map/ppermute | solution.py:395
  43.9 14.2 %collective-permute-start.8 = (f32[80,64]{1,0:T(8,128)S(1)}, f32[80,64]{1,0:T(8,128)}, u32[]{:S(2)}, u32[]{:S(2)}) collective-permute-start(f32[80,64]{1,0:T(8,128)S(1)} %get-tuple-element.21.refs_0_), channel_id=1, source_target_pairs={{0,24},{8,16},{16,8},{24,0},{1,25},{9,17},{17,9},{25,1},{2,26},{10... | collective-permute-start | bytes 61448 | tf_op jit(solution)/shard_map/ppermute | solution.py:395
  44.4 0.7 copy-start.20
  44.4 0.7 copy-start.21
  45.1 13.0 %copy-start.9 = (f32[1,64,896]{2,1,0:T(8,128)S(1)}, f32[1,64,896]{2,1,0:T(8,128)}, u32[]{:S(2)}) copy-start(f32[1,64,896]{2,1,0:T(8,128)} %param.19) | copy-start | bytes 688132
  45.1 13.0 %copy-start.11 = (f32[4,80,64]{2,1,0:T(8,128)S(1)}, f32[4,80,64]{2,1,0:T(8,128)}, u32[]{:S(2)}) copy-start(f32[4,80,64]{2,1,0:T(8,128)} %copy-done.10) | copy-start | bytes 245764
  45.1 13.0 %copy-start.12 = (f32[64,384]{1,0:T(8,128)S(1)}, f32[64,384]{1,0:T(8,128)}, u32[]{:S(2)}) copy-start(f32[64,384]{1,0:T(8,128)} %grp_transfer.1) | copy-start | bytes 294916
  45.1 13.0 %copy-start.13 = (f32[64,384]{1,0:T(8,128)S(1)}, f32[64,384]{1,0:T(8,128)}, u32[]{:S(2)}) copy-start(f32[64,384]{1,0:T(8,128)} %grp_coupling.1) | copy-start | bytes 294916
where the time goes:
time: 68.5 us; the launch traced here: 67.9 us
  Pallas kernels  37.7 us (55%)
  starting transfers between devices  15.4 us (22%)
  local copies, waits for them, and re-layouts  7.73 us (11%)
  waiting for transfers between devices  6.17 us (9%)
  between operations  0.84 us (1%)
    pallas_call x1, Pallas kernels, shards(): pl.pallas_call(couple_kernel, out_shape=[f32(NRHS, POINT_SPAN), f32(RANK,...  12.9 us
    ppermute x7, starting transfers between devices, exchange(): lax.ppermute(block, axis, [(i, i ^ k << start) for i in range(count)])  11.4 us
    pallas_call x1, Pallas kernels, shards(): pl.pallas_call(functools.partial(top_kernel, grp_count, dev_count, start,...  9.77 us
    pallas_call x1, Pallas kernels, shards(): pl.pallas_call(local_kernel, out_shape=[f32(BATCH * RANK, RANK), f32(NRHS...  7.85 us
    unnamed x44, local copies, waits for them, and re-layouts  7.73 us
    ppermute x7, waiting for transfers between devices, exchange(): lax.ppermute(block, axis, [(i, i ^ k << start) for i in range(count)])  6.16 us
    pallas_call x1, Pallas kernels, shards(): pl.pallas_call(gram_kernel, out_shape=[f32(PAIRS, PAIR, PAIR), f32(NRHS,...  4.58 us
    ppermute x1, starting transfers between devices, shards(): lower = lax.ppermute(packed, both, [(i, i + 1) for i in range(ends)])  2.54 us
  transfers between devices with their start and end apart: 9, of which 3 were waited for; matrix products, arithmetic and copies ran while one was open for 0% of the time, Pallas kernels for 23%

commit v1 on v0

--- a/solution.py
+++ b/solution.py
@@ -15,7 +15,7 @@
 LOCAL_NODES = 30
 PAIR = 2 * RANK
 LANES = 128
-BATCH = 32
+BATCH = 16
 ROWS = RANK + NRHS
 PAIRS = LOCAL_NODES // 2
 POINT_SPAN = LEAF_DEV * LEAF
@@ -26,16 +26,36 @@
 precise = lax.Precision.HIGHEST
 
 
+def halves(x):
+    high = x.astype(jnp.bfloat16)
+    return high, (x - high.astype(jnp.float32)).astype(jnp.bfloat16)
+
+
+def three_pass(a, b, side):
+    dims = (((1,), (side,)), ((), ()))
+    dot = functools.partial(
+        lax.dot_general, dimension_numbers=dims, preferred_element_type=jnp.float32
+    )
+    a_high, a_low = halves(a)
+    b_high, b_low = halves(b)
+    return dot(a_high, b_high) + (dot(a_high, b_low) + dot(a_low, b_high))
+
+
+def full(a, b, side):
+    dims = (((1,), (side,)), ((), ()))
+    return lax.dot_general(a, b, dims, precision=precise, preferred_element_type=jnp.float32)
+
+
 def mm(a, b):
-    return lax.dot_general(
-        a, b, (((1,), (0,)), ((), ())), precision=precise, preferred_element_type=jnp.float32
-    )
+    return three_pass(a, b, 0)
 
 
 def mm_t(a, b):
-    return lax.dot_general(
-        a, b, (((1,), (1,)), ((), ())), precision=precise, preferred_element_type=jnp.float32
-    )
+    return three_pass(a, b, 1)
+
+
+def mm_full(a, b):
+    return full(a, b, 0)
 
 
 def low_half(rows):
@@ -107,16 +127,28 @@
                 m[i, k0 : k0 + 8, :] = new
 
 
-def invert_nodes(d, a, m, inv, count):
+def invert_pairs(gram, a, m, inv, count):
     for i in range(RANK):
-        rows = d[pl.ds(i, count, stride=RANK), :]
-        a[i, :, 0:count] = rows.T[0:RANK]
+        rows = gram[pl.ds(i, count, stride=RANK), :]
+        both = jnp.concatenate([rows, swap_halves(rows)], axis=0)
+        a[i, :, 0 : 2 * count] = both[:, 0:RANK].T
     factor_batch(a, m)
     for i in range(RANK):
-        inv[pl.ds(i, count, stride=RANK), :] = m[i, :, 0:count].T
-
-
-def gram_kernel(basis, rhs, transfer, gram, z_out, top):
+        rows = m[i, :, 0 : 2 * count].T
+        inv[pl.ds(i, count, stride=RANK), :] = jnp.concatenate([rows[:count], rows[count:]], axis=1)
+
+
+def gram_kernel(basis_in, rhs_in, transfer_in, gram, z_out, top, basis, rhs, transfer, sems):
+    copies = [
+        pltpu.make_async_copy(source, target, sems.at[n])
+        for n, (source, target) in enumerate(
+            ((basis_in, basis), (rhs_in, rhs), (transfer_in, transfer))
+        )
+    ]
+    for copy in copies:
+        copy.start()
+    copies[0].wait()
+    copies[1].wait()
     blocks = []
     zs = []
     for p in range(LEAF_DEV // 2):
@@ -131,11 +163,14 @@
             )
         )
         zs.append(mm(rhs[:, lanes], spread))
+    copies[2].wait()
     tile = 0
     for level in range(LOC):
         pairs = len(blocks)
         for p in range(pairs):
-            gram[tile + p] = blocks[p]
+            gram[RANK * (tile + p) : RANK * (tile + p + 1), :] = jnp.where(
+                low_half(RANK), blocks[p][:RANK], blocks[p][RANK:]
+            )
             z_out[:, PAIR * (tile + p) : PAIR * (tile + p + 1)] = zs[p]
         next_blocks = []
         next_zs = []
@@ -160,18 +195,20 @@
     top[RANK:ROWS, :] = zs[0][:, 0:RANK]
 
 
-def local_kernel(gram, z, rhs, inv, packed, d, a, m):
-    for p in range(PAIRS):
-        d[PAIR * p : PAIR * p + RANK, :] = gram[p, 0:RANK, :]
-        d[PAIR * p + RANK : PAIR * (p + 1), :] = swap_halves(gram[p, RANK:PAIR, :])
-    invert_nodes(d, a, m, inv, BATCH)
+def pair_rows(p):
+    return slice(RANK * p, RANK * (p + 1))
+
+
+def pair_lanes(p):
+    return slice(PAIR * p, PAIR * (p + 1))
+
+
+def local_kernel(gram, z, rhs, after, inv, packed, a, m):
+    invert_pairs(gram, a, m, inv, BATCH)
     packed[:, 0:POINT_SPAN] = rhs[...]
     for p in range(PAIRS):
-        pair = z[:, PAIR * p : PAIR * (p + 1)]
-        even = mm_t(pair[:, 0:RANK], inv[PAIR * p : PAIR * p + RANK, :])
-        odd = mm_t(pair[:, RANK:PAIR], inv[PAIR * p + RANK : PAIR * (p + 1), :])
-        packed[:, POINT_SPAN + PAIR * p : POINT_SPAN + PAIR * (p + 1)] = jnp.concatenate(
-            [even, odd], axis=1
+        packed[:, POINT_SPAN + PAIR * p : POINT_SPAN + PAIR * (p + 1)] = mm_t(
+            z[:, pair_lanes(p)], spread_pair(inv[pair_rows(p), :])
         )
 
 
@@ -207,19 +244,19 @@
     return nodes[0]
 
 
-def climb_kernel(start, bits, count, place, transfer, *refs):
+def climb_kernel(axis, start, bits, count, transfer, *refs):
     blocks = refs[: 2**bits]
-    top, records, stack = refs[2**bits :]
-    top[...] = climb(blocks, place[0], start, bits, count, transfer, stack, records, 0)
+    top, records = refs[-3 - (len(refs) - 2**bits - 3) // 2 :][:2]
+    stack = refs[-1]
+    top[...] = climb(blocks, lax.axis_index(axis), start, bits, count, transfer, stack, records, 0)
 
 
 def couple_kernel(
-    place,
-    near_partner,
-    far_partner,
+    near_partner_in,
+    far_partner_in,
     own,
-    lower,
-    upper,
+    twin,
+    beside,
     inv,
     coupling,
     transfer,
@@ -228,21 +265,36 @@
     base,
     lift,
     window,
+    near_partner,
+    far_partner,
+    sems,
 ):
+    copies = [
+        pltpu.make_async_copy(near_partner_in, near_partner, sems.at[0]),
+        pltpu.make_async_copy(far_partner_in, far_partner, sems.at[1]),
+    ]
+    for copy in copies:
+        copy.start()
     packed_tiles = (POINT_SPAN + NODE_SPAN) // PAIR
     point_tiles = POINT_SPAN // PAIR
     starts = [point_tiles + OFFSETS[level] // 2 for level in range(LOC)]
     spans = [(0, point_tiles)] + [(starts[level], (LEAF_DEV >> level) // 2) for level in range(LOC)]
     firsts = []
     slot = 0
+    place = lax.axis_index("grp") * lax.axis_size("dev") + lax.axis_index("dev")
+    odd = place & 1
     for start, span in spans:
         firsts.append(slot)
-        for source in (lower, own, upper):
+        for source, shift in ((beside, odd), (own, None), (twin, 1 - odd)):
+            first = slot + span if shift is None else slot + 2 * span * shift
             for t in range(span):
                 tile = source[:, PAIR * (start + t) : PAIR * (start + t + 1)]
-                window[0, slot] = tile
-                window[1, slot] = swap_halves(tile)
-                slot += 1
+                window[0, first + t] = tile
+                window[1, first + t] = swap_halves(tile)
+        slot += 3 * span
+
+    for copy in copies:
+        copy.wait()
 
     def pick(first, index, parity):
         return window[(index & 1) ^ parity, first + lax.shift_right_logical(index, 1)]
@@ -254,15 +306,13 @@
         tiles = []
         for p in range(m // 2):
             node = OFFSETS[level] + 2 * p
-            sides = []
+            values = []
             for side in range(2):
-                index = far_partner[0, node + side] - (place[0] - 1) * m
-                value = pick(firsts[level + 1], index, 0)[:, 0:RANK]
-                s = coupling[:, PAIR * (node // 2) : PAIR * (node // 2 + 1)]
-                y = mm_t(value, s[:, RANK * side : RANK * (side + 1)])
-                rows = slice(RANK * (node + side), RANK * (node + side + 1))
-                sides.append(mm(y, inv[rows, :]))
-            tiles.append(jnp.concatenate(sides, axis=1))
+                index = far_partner[0, node + side] - (place - 1) * m
+                values.append(pick(firsts[level + 1], index, side))
+            xhat = jnp.where(low16, values[0], values[1])
+            y = mm_t(xhat, spread_pair(coupling[:, pair_lanes(node // 2)]))
+            tiles.append(mm(y, spread_pair(inv[pair_rows(node // 2), :])))
         lifted.append(tiles)
 
     state = None
@@ -291,7 +341,7 @@
         swapped = swap_halves(own_points)
         inputs = []
         for side in range(2):
-            index = near_partner[2 * p + side] - (place[0] - 1) * LEAF_DEV
+            index = near_partner[2 * p + side] - (place - 1) * LEAF_DEV
             value = pick(0, index, 1)
             inputs.append(jnp.where(low16, swapped if side else own_points, value))
         weights = jnp.concatenate(
@@ -306,9 +356,14 @@
         lift[:, lanes] = out[NRHS:]
 
 
-def half_of(array, index):
+def half_tile(array, index):
     pair = array[:, pl.ds(pl.multiple_of(PAIR * (index // 2), PAIR), PAIR)]
-    return jnp.where(index % 2 == 1, pair[:, RANK:], pair[:, 0:RANK])
+    lane = lax.broadcasted_iota(jnp.int32, (NRHS, PAIR), 1)
+    return pair, lax.shift_right_logical(lane, RANK.bit_length() - 1) == index % 2
+
+
+def twice(x):
+    return jnp.concatenate([x, x], axis=1)
 
 
 def top_kernel(
@@ -317,7 +372,6 @@
     start,
     bits,
     record_spans,
-    place,
     grp_transfer,
     grp_coupling,
     dev_transfer,
@@ -336,36 +390,40 @@
             records[2 * level + r] = ref[r]
         level += span
     top = climb(
-        blocks, place[0], start, bits, grp_count, grp_transfer, stack, records, level
+        blocks, lax.axis_index("grp"), start, bits, grp_count, grp_transfer, stack, records, level
     )
     levels = level + bits
-    batch = inv.shape[0] // RANK
-    for r in range(2 * levels):
-        d[RANK * r : RANK * (r + 1), 0:RANK] = records[r, 0:RANK]
-    d[RANK * 2 * levels : RANK * (2 * levels + 1), 0:RANK] = top[0:RANK]
-    invert_nodes(d, a, m, inv, batch)
-    root_inverse = inv[RANK * 2 * levels : RANK * (2 * levels + 1), :]
+    for n in range(levels):
+        d[pair_rows(n), :] = jnp.concatenate(
+            [records[2 * n, 0:RANK], records[2 * n + 1, 0:RANK]], axis=1
+        )
+    d[pair_rows(levels), :] = twice(top[0:RANK])
+    invert_pairs(d, a, m, inv, inv.shape[0] // RANK)
+    root_inverse = inv[pair_rows(levels), 0:RANK]
     keep = lax.broadcasted_iota(jnp.int32, (RANK, RANK), 0) >= lax.broadcasted_iota(
         jnp.int32, (RANK, RANK), 1
     )
     root[...] = jnp.where(keep, mm_t(top[0:RANK], root_inverse), 0.0)
     dev_levels = dev_count.bit_length() - 1
+    low = low_half(NRHS)
     terms = []
     for n in range(levels):
         if n < dev_levels:
-            count, shift, spot = dev_count, n, place[1]
+            count, shift, spot = dev_count, n, lax.axis_index("dev")
             transfer, coupling = dev_transfer, dev_coupling
         else:
-            count, shift, spot = grp_count, n - dev_levels, place[0]
+            count, shift, spot = grp_count, n - dev_levels, lax.axis_index("grp")
             transfer, coupling = grp_transfer, grp_coupling
         index = 2 * count - 2 * (count >> shift) + lax.shift_right_logical(spot, shift)
-        other = records[2 * n + 1, RANK:ROWS]
-        xhat = mm_t(other, inv[RANK * (2 * n + 1) : RANK * (2 * n + 2), :])
-        yhat = mm_t(xhat, half_of(coupling, index))
-        terms.append((mm(yhat, inv[RANK * 2 * n : RANK * (2 * n + 1), :]), half_of(transfer, index)))
+        factors = inv[pair_rows(n), :]
+        other = jnp.where(low, 0.0, twice(records[2 * n + 1, RANK:ROWS]))
+        pair, half = half_tile(coupling, index)
+        xhat = jnp.where(half, twice(mm_t(other, factors)), 0.0)
+        yhat = mm_t(xhat, pair)
+        terms.append((mm(yhat, factors)[:, 0:RANK], *half_tile(transfer, index)))
     value = None
-    for term, transfer in reversed(terms):
-        value = term if value is None else term + mm_t(value, transfer)
+    for term, pair, half in reversed(terms):
+        value = term if value is None else term + mm_t(jnp.where(half, twice(value), 0.0), pair)
     product[...] = base[...] + mm(value, lift[...])
 
 
@@ -373,8 +431,12 @@
     return [pl.BlockSpec(memory_space=pltpu.VMEM)] * count
 
 
-def smem(count):
-    return [pl.BlockSpec(memory_space=pltpu.SMEM)] * count
+def hbm(count):
+    return [pl.BlockSpec(memory_space=pltpu.HBM)] * count
+
+
+def in_hbm(x):
+    return pltpu.with_memory_space_constraint(x, pltpu.HBM)
 
 
 def f32(*shape):
@@ -385,8 +447,8 @@
     return pltpu.CompilerParams(vmem_limit_bytes=mib * MIB)
 
 
-def cost(flops, size):
-    return pl.CostEstimate(flops=flops, bytes_accessed=size, transcendentals=0)
+def micros(count):
+    return pl.CostEstimate(flops=count * 10**9, bytes_accessed=MIB, transcendentals=0)
 
 
 def exchange(block, axis, start, bits):
@@ -407,16 +469,35 @@
     return out
 
 
-def climb_call(blocks, place, start, bits, count, transfer):
+def climb_call(blocks, axis, start, bits, count, transfer, carried=()):
+    anywhere = [pl.BlockSpec(memory_space=pl.ANY)] * len(carried)
     return pl.pallas_call(
-        functools.partial(climb_kernel, start, bits, count),
-        out_shape=[f32(ROWS, RANK), f32(2 * bits, ROWS, RANK)],
-        in_specs=smem(1) + vmem(1 + 2**bits),
-        out_specs=vmem(2),
+        functools.partial(climb_kernel, axis, start, bits, count),
+        out_shape=[f32(ROWS, RANK), f32(2 * bits, ROWS, RANK)] + [f32(*c.shape) for c in carried],
+        in_specs=vmem(1 + 2**bits) + anywhere,
+        out_specs=vmem(2) + anywhere,
+        input_output_aliases={1 + 2**bits + n: 2 + n for n in range(len(carried))},
         scratch_shapes=[pltpu.VMEM((2**bits, ROWS, RANK), jnp.float32)],
         compiler_params=params(8),
+        cost_estimate=micros(1),
         name="climb",
-    )(place, transfer, *blocks)
+    )(transfer, *blocks, *carried)
+
+
+def local_call(gram, z, rhs, after):
+    return pl.pallas_call(
+        local_kernel,
+        out_shape=[f32(BATCH * RANK, PAIR), f32(NRHS, POINT_SPAN + NODE_SPAN)],
+        in_specs=vmem(3) + [pl.BlockSpec(memory_space=pl.ANY)],
+        out_specs=vmem(2),
+        scratch_shapes=[
+            pltpu.VMEM((RANK, RANK, LANES), jnp.float32),
+            pltpu.VMEM((RANK, RANK, LANES), jnp.float32),
+        ],
+        compiler_params=params(24),
+        cost_estimate=micros(8),
+        name="local_factors",
+    )(gram, z, rhs, after)
 
 
 def shards(
@@ -434,66 +515,68 @@
 ):
     dev_count = lax.axis_size("dev")
     grp_count = lax.axis_size("grp")
-    dev_place = lax.axis_index("dev").astype(jnp.int32)
-    grp_place = lax.axis_index("grp").astype(jnp.int32)
-    places = jnp.stack([grp_place, dev_place])
-    dev_spot = dev_place[None]
-    device_spot = (grp_place * dev_count + dev_place)[None]
-
     gram, z, top = pl.pallas_call(
         gram_kernel,
-        out_shape=[f32(PAIRS, PAIR, PAIR), f32(NRHS, NODE_SPAN), f32(ROWS, RANK)],
-        in_specs=vmem(3),
+        out_shape=[f32(BATCH * RANK, PAIR), f32(NRHS, NODE_SPAN), f32(ROWS, RANK)],
+        in_specs=hbm(3),
         out_specs=vmem(3),
+        scratch_shapes=[
+            pltpu.VMEM((LEAF, POINT_SPAN), jnp.float32),
+            pltpu.VMEM((NRHS, POINT_SPAN), jnp.float32),
+            pltpu.VMEM((RANK, NODE_SPAN), jnp.float32),
+            pltpu.SemaphoreType.DMA((3,)),
+        ],
         compiler_params=params(16),
+        cost_estimate=micros(4),
         name="gram",
-    )(leaf_basis, rhs, local_transfer)
+    )(in_hbm(leaf_basis), in_hbm(rhs), in_hbm(local_transfer))
 
     records = []
     spans = []
+    carried = ()
+    inv = None
     dev_transfer = dev_transfer[0]
     dev_coupling = dev_coupling[0]
     for start, bits in chunks(dev_count.bit_length() - 1, 1):
         blocks = exchange(top, "dev", start, bits)
-        top, record = climb_call(blocks, dev_spot, start, bits, dev_count, dev_transfer)
+        if records and inv is None:
+            inv, packed = local_call(gram, z, rhs, records[0])
+            carried = (packed,)
+        top, record, *carried = climb_call(
+            blocks, "dev", start, bits, dev_count, dev_transfer, carried
+        )
         records.append(record)
         spans.append(bits)
-
-    inv, packed = pl.pallas_call(
-        local_kernel,
-        out_shape=[f32(BATCH * RANK, RANK), f32(NRHS, POINT_SPAN + NODE_SPAN)],
-        in_specs=vmem(3),
-        out_specs=vmem(2),
-        scratch_shapes=[
-            pltpu.VMEM((BATCH * RANK, LANES), jnp.float32),
-            pltpu.VMEM((RANK, RANK, LANES), jnp.float32),
-            pltpu.VMEM((RANK, RANK, LANES), jnp.float32),
-        ],
-        compiler_params=params(24),
-        name="local_factors",
-    )(gram, z, rhs)
+    packed = carried[0]
 
     both = ("grp", "dev")
     ends = grp_count * dev_count - 1
-    lower = lax.ppermute(packed, both, [(i, i + 1) for i in range(ends)])
-    upper = lax.ppermute(packed, both, [(i + 1, i) for i in range(ends)])
+    twin = lax.ppermute(packed, both, [(i, i ^ 1) for i in range(ends + 1)])
+    beside = lax.ppermute(
+        packed, both, [(i, ((i + 1) ^ 1) - 1) for i in range(1, ends)]
+    )
 
     window_tiles = 3 * (POINT_SPAN + NODE_SPAN) // PAIR
     base, lift = pl.pallas_call(
         couple_kernel,
         out_shape=[f32(NRHS, POINT_SPAN), f32(RANK, POINT_SPAN)],
-        in_specs=smem(3) + vmem(8),
+        in_specs=hbm(2) + vmem(8),
         out_specs=vmem(2),
-        scratch_shapes=[pltpu.VMEM((2, window_tiles, NRHS, PAIR), jnp.float32)],
+        scratch_shapes=[
+            pltpu.VMEM((2, window_tiles, NRHS, PAIR), jnp.float32),
+            pltpu.SMEM(near_partner.shape, jnp.int32),
+            pltpu.SMEM(far_partner.shape, jnp.int32),
+            pltpu.SemaphoreType.DMA((2,)),
+        ],
         compiler_params=params(24),
+        cost_estimate=micros(10),
         name="couple",
     )(
-        device_spot,
-        near_partner,
-        far_partner,
+        in_hbm(near_partner),
+        in_hbm(far_partner),
         packed,
-        lower,
-        upper,
+        twin,
+        beside,
         inv,
         local_coupling,
         local_transfer,
@@ -504,17 +587,17 @@
     grp_chunks = chunks(grp_count.bit_length() - 1, 2)
     for start, bits in grp_chunks[:-1]:
         blocks = exchange(top, "grp", start, bits)
-        top, record = climb_call(blocks, grp_place[None], start, bits, grp_count, grp_transfer)
+        top, record = climb_call(blocks, "grp", start, bits, grp_count, grp_transfer)
         records.append(record)
         spans.append(bits)
     start, bits = grp_chunks[-1]
     blocks = exchange(top, "grp", start, bits)
     levels = sum(spans) + bits
-    batch = 8 * ((2 * levels + 1 + 7) // 8)
+    batch = 8 * ((levels + 1 + 7) // 8)
     return pl.pallas_call(
         functools.partial(top_kernel, grp_count, dev_count, start, bits, tuple(spans)),
         out_shape=[f32(NRHS, POINT_SPAN), f32(RANK, RANK)],
-        in_specs=smem(1) + vmem(6 + len(blocks) + len(records)),
+        in_specs=vmem(6 + len(blocks) + len(records)),
         out_specs=vmem(2),
         scratch_shapes=[
             pltpu.VMEM((2**bits, ROWS, RANK), jnp.float32),
@@ -522,12 +605,12 @@
             pltpu.VMEM((batch * RANK, LANES), jnp.float32),
             pltpu.VMEM((RANK, RANK, LANES), jnp.float32),
             pltpu.VMEM((RANK, RANK, LANES), jnp.float32),
-            pltpu.VMEM((batch * RANK, RANK), jnp.float32),
+            pltpu.VMEM((batch * RANK, PAIR), jnp.float32),
         ],
         compiler_params=params(24),
+        cost_estimate=micros(9),
         name="top",
     )(
-        places,
         grp_transfer,
         grp_coupling,
         dev_transfer,

time: 68.5 us -> 47.3 us (0.69)
  the two profiles are of different devices: /device:TPU:0 before, /device:TPU:4 now
where the time goes in v1:
time: 47.3 us; the launch traced here: 47.1 us
  Pallas kernels  28.5 us (60%)
  starting transfers between devices  14.7 us (31%)
  waiting for transfers between devices  3.07 us (6%)
  between operations  0.8 us (2%)
    pallas_call x1, Pallas kernels, shards(): pl.pallas_call(functools.partial(top_kernel, grp_count, dev_count, start,...  9.77 us
    ppermute x7, starting transfers between devices, exchange(): lax.ppermute(block, axis, [(i, i ^ k << start) for i in range(count)])  8.03 us
    pallas_call x1, Pallas kernels, shards(): pl.pallas_call(couple_kernel, out_shape=[f32(NRHS, POINT_SPAN), f32(RANK,...  6.8 us
    ppermute x1, starting transfers between devices, shards(): lax.ppermute(packed, both, [(i, (i + 1 ^ 1) - 1) for i in range(1, ends)])  6.68 us
    pallas_call x1, Pallas kernels, local_call(): pl.pallas_call(local_kernel, out_shape=[f32(BATCH * RANK, PAIR), f32(NRHS...  6.38 us
    pallas_call x1, Pallas kernels, shards(): pl.pallas_call(gram_kernel, out_shape=[f32(BATCH * RANK, PAIR), f32(NRHS,...  4.16 us
    ppermute x1, waiting for transfers between devices, shards(): lax.ppermute(packed, both, [(i, (i + 1 ^ 1) - 1) for i in range(1, ends)])  1.82 us
    pallas_call x2, Pallas kernels, climb_call(): pl.pallas_call(functools.partial(climb_kernel, axis, start, bits, count),...  1.38 us
  transfers between devices with their start and end apart: 9, of which 2 were waited for; matrix products, arithmetic and copies ran while one was open for 0% of the time, Pallas kernels for 28%

profile of v1, /device:TPU:4, one launch (start us, length us, event | category | flops | bytes accessed | tf_op | source)
XLA Modules:
  0.0 47.1 jit_solution(13879883554325450851)
XLA Ops:
  0.6 4.2 %gram.1 = (f32[1024,128]{1,0:T(8,128)S(1)}, f32[16,1920]{1,0:T(8,128)S(1)}, f32[80,64]{1,0:T(8,128)S(1)}) custom-call(f32[64,1024]{1,0:T(8,128)} %basis.1, f32[16,1024]{1,0:T(8,128)} %rhs.1, f32[64,1920]{1,0:T(8,128)} %transfer.1), custom_call_target="tpu_custom_call" | custom-call | flops 4000000000 | bytes 1048576 | tf_op jit(solution)/shard_map/gram/pallas_call | solution.py:518
  4.8 0.1 collective-permute-start
  4.9 1.2 %collective-permute-done.refs_1_ = f32[80,64]{1,0:T(8,128)S(1)} collective-permute-done((f32[80,64]{1,0:T(8,128)S(1)}, f32[80,64]{1,0:T(8,128)S(1)}, u32[]{:S(2)}, u32[]{:S(2)}) %collective-permute-start) | collective-permute-done | bytes 20512 | tf_op jit(solution)/shard_map/ppermute | solution.py:457
  6.1 0.4 climb.2
  6.5 1.6 %collective-permute-start.1 = (f32[80,64]{1,0:T(8,128)S(1)}, f32[80,64]{1,0:T(8,128)S(1)}, u32[]{:S(2)}, u32[]{:S(2)}) collective-permute-start(f32[80,64]{1,0:T(8,128)S(1)} %get-tuple-element.15.refs_0_), channel_id=1, source_target_pairs={{0,2},{1,3},{2,0},{3,1},{4,6},{5,7},{6,4},{7,5},{8,10},{9,11},{10,... | collective-permute-start | bytes 61448 | tf_op jit(solution)/shard_map/ppermute | solution.py:457
  8.1 2.6 %collective-permute-start.2 = (f32[80,64]{1,0:T(8,128)S(1)}, f32[80,64]{1,0:T(8,128)S(1)}, u32[]{:S(2)}, u32[]{:S(2)}) collective-permute-start(f32[80,64]{1,0:T(8,128)S(1)} %get-tuple-element.15.refs_0_), channel_id=1, source_target_pairs={{0,4},{1,5},{2,6},{3,7},{4,0},{5,1},{6,2},{7,3},{8,12},{9,13},{10,... | collective-permute-start | bytes 61448 | tf_op jit(solution)/shard_map/ppermute | solution.py:457
  10.7 0.2 collective-permute-start.3
  10.9 0.0 copy-done.8
  10.9 6.4 %local_factors.1 = (f32[1024,128]{1,0:T(8,128)S(1)}, f32[16,2944]{1,0:T(8,128)S(1)}) custom-call(f32[1024,128]{1,0:T(8,128)S(1)} %get-tuple-element.16.gram, f32[16,1920]{1,0:T(8,128)S(1)} %get-tuple-element.17.z, f32[16,1024]{1,0:T(8,128)S(1)} %copy-done.8, f32[2,80,64]{2,1,0:T(8,128)S(1)} %get-tuple-element.18.after.refs_4_), custom_call_target="tpu_custom_call" | custom-call | flops 8000000000 | bytes 1048576 | tf_op jit(solution)/shard_map/local_factors/pallas_call | solution.py:488
  17.3 0.0 collective-permute-done.1.refs_1_
  17.3 0.0 collective-permute-done.2.refs_2_
  17.3 0.0 collective-permute-done.3.refs_3_
  17.3 0.0 copy-start
  17.3 0.0 copy-start.1
  17.3 0.0 copy-start.2
  17.4 0.0 copy-start.3
  17.4 1.0 %climb.3 = (f32[80,64]{1,0:T(8,128)S(1)}, f32[4,80,64]{2,1,0:T(8,128)S(1)}, f32[16,2944]{1,0:T(8,128)S(1)}) custom-call(f32[64,896]{1,0:T(8,128)S(1)} %bitcast.3, f32[80,64]{1,0:T(8,128)S(1)} %get-tuple-element.15.refs_0_, f32[80,64]{1,0:T(8,128)S(1)} %collective-permute-done.1.refs_1_, ...), custom_call_target="tpu_custom_call", output_to_operand_aliasing={{2}: (5, {})} | custom-call | flops 1000000000 | bytes 1048576 | tf_op jit(solution)/shard_map/climb/pallas_call | solution.py:474
  18.4 0.0 collective-permute-start.4
  18.4 6.7 %collective-permute-start.5 = (f32[16,2944]{1,0:T(8,128)S(1)}, f32[16,2944]{1,0:T(8,128)S(1)}, u32[]{:S(2)}, u32[]{:S(2)}) collective-permute-start(f32[16,2944]{1,0:T(8,128)S(1)} %get-tuple-element.20.own), channel_id=1, source_target_pairs={{1,2},{2,1},{3,4},{4,3},{5,6},{6,5},{7,8},{8,7},{9,10},{10,9},{11,... | collective-permute-start | bytes 565256 | tf_op jit(solution)/shard_map/ppermute | solution.py:555
  25.0 0.7 %collective-permute-start.6 = (f32[80,64]{1,0:T(8,128)S(1)}, f32[80,64]{1,0:T(8,128)S(1)}, u32[]{:S(2)}, u32[]{:S(2)}) collective-permute-start(f32[80,64]{1,0:T(8,128)S(1)} %get-tuple-element.24.refs_0_), channel_id=1, source_target_pairs={{0,8},{8,0},{16,24},{24,16},{1,9},{9,1},{17,25},{25,17},{2,10},{10... | collective-permute-start | bytes 61448 | tf_op jit(solution)/shard_map/ppermute | solution.py:457
  25.7 0.5 %collective-permute-start.7 = (f32[80,64]{1,0:T(8,128)S(1)}, f32[80,64]{1,0:T(8,128)S(1)}, u32[]{:S(2)}, u32[]{:S(2)}) collective-permute-start(f32[80,64]{1,0:T(8,128)S(1)} %get-tuple-element.24.refs_0_), channel_id=1, source_target_pairs={{0,16},{8,24},{16,0},{24,8},{1,17},{9,25},{17,1},{25,9},{2,18},{10... | collective-permute-start | bytes 61448 | tf_op jit(solution)/shard_map/ppermute | solution.py:457
  26.2 2.4 %collective-permute-start.8 = (f32[80,64]{1,0:T(8,128)S(1)}, f32[80,64]{1,0:T(8,128)S(1)}, u32[]{:S(2)}, u32[]{:S(2)}) collective-permute-start(f32[80,64]{1,0:T(8,128)S(1)} %get-tuple-element.24.refs_0_), channel_id=1, source_target_pairs={{0,24},{8,16},{16,8},{24,0},{1,25},{9,17},{17,9},{25,1},{2,26},{10... | collective-permute-start | bytes 61448 | tf_op jit(solution)/shard_map/ppermute | solution.py:457
  28.6 0.0 collective-permute-done.4.twin
  28.6 1.8 %collective-permute-done.5.beside = f32[16,2944]{1,0:T(8,128)S(1)} collective-permute-done((f32[16,2944]{1,0:T(8,128)S(1)}, f32[16,2944]{1,0:T(8,128)S(1)}, u32[]{:S(2)}, u32[]{:S(2)}) %collective-permute-start.5) | collective-permute-done | bytes 188448 | tf_op jit(solution)/shard_map/ppermute | solution.py:555
  30.4 0.0 copy-start.5
  30.5 0.0 copy-start.6
  30.5 0.0 copy-start.7
  30.5 6.8 %couple.1 = (f32[16,1024]{1,0:T(8,128)S(1)}, f32[64,1024]{1,0:T(8,128)S(1)}) custom-call(s32[16]{0:T(128)} %near_partner_in.1, s32[1,30]{1,0:T(1,128)} %far_partner_in.1, f32[16,2944]{1,0:T(8,128)S(1)} %get-tuple-element.20.own, f32[16,2944]{1,0:T(8,128)S(1)} %collective-permute-done.4.twin, f32[16,2944]{1,0:T(8,128)S(1)} %collective-permute-done.5.beside, ...), custom_call_target="tpu_custom_call" | custom-call | flops 10000000000 | bytes 1048576 | tf_op jit(solution)/shard_map/couple/pallas_call | solution.py:560
  37.3 0.0 collective-permute-done.6.refs_1_
  37.3 0.0 collective-permute-done.7.refs_2_
  37.3 0.0 collective-permute-done.8.refs_3_
  37.3 9.8 %top.1 = (f32[16,1024]{1,0:T(8,128)}, f32[64,64]{1,0:T(8,128)}) custom-call(f32[64,384]{1,0:T(8,128)S(1)} %copy-done.6, f32[64,384]{1,0:T(8,128)S(1)} %copy-done.7, f32[64,896]{1,0:T(8,128)S(1)} %bitcast.4, f32[64,896]{1,0:T(8,128)S(1)} %bitcast.5, f32[16,1024]{1,0:T(8,128)S(1)} %get-tuple-element.22.base, f32[64,1024]{1,0:T(8,128)S(1)} %get-tuple-element.23.lift, ...), custom_call_target="tpu_custom_call" | custom-call | flops 8999999488 | bytes 1048576 | tf_op jit(solution)/shard_map/top/pallas_call | solution.py:597
  (10 shorter events, 0.0 us)
Async XLA Ops:
  0.6 5.5 %copy-start.4 = (f32[1,64,896]{2,1,0:T(8,128)S(1)}, f32[1,64,896]{2,1,0:T(8,128)}, u32[]{:S(2)}) copy-start(f32[1,64,896]{2,1,0:T(8,128)} %param.18) | copy-start | bytes 688132
  4.8 1.3 %collective-permute-start = (f32[80,64]{1,0:T(8,128)S(1)}, f32[80,64]{1,0:T(8,128)S(1)}, u32[]{:S(2)}, u32[]{:S(2)}) collective-permute-start(f32[80,64]{1,0:T(8,128)S(1)} %get-tuple-element.14.refs_0_), channel_id=1, source_target_pairs={{0,1},{1,0},{2,3},{3,2},{4,5},{5,4},{6,7},{7,6},{8,9},{9,8},{10,11... | collective-permute-start | bytes 61448 | tf_op jit(solution)/shard_map/ppermute | solution.py:457
  6.1 4.8 %copy-start.8 = (f32[16,1024]{1,0:T(8,128)S(1)}, f32[16,1024]{1,0:T(8,128)}, u32[]{:S(2)}) copy-start(f32[16,1024]{1,0:T(8,128)} %rhs.1) | copy-start | bytes 196612
  6.5 10.8 %collective-permute-start.1 = (f32[80,64]{1,0:T(8,128)S(1)}, f32[80,64]{1,0:T(8,128)S(1)}, u32[]{:S(2)}, u32[]{:S(2)}) collective-permute-start(f32[80,64]{1,0:T(8,128)S(1)} %get-tuple-element.15.refs_0_), channel_id=1, source_target_pairs={{0,2},{1,3},{2,0},{3,1},{4,6},{5,7},{6,4},{7,5},{8,10},{9,11},{10,... | collective-permute-start | bytes 61448 | tf_op jit(solution)/shard_map/ppermute | solution.py:457
  8.1 9.2 %collective-permute-start.2 = (f32[80,64]{1,0:T(8,128)S(1)}, f32[80,64]{1,0:T(8,128)S(1)}, u32[]{:S(2)}, u32[]{:S(2)}) collective-permute-start(f32[80,64]{1,0:T(8,128)S(1)} %get-tuple-element.15.refs_0_), channel_id=1, source_target_pairs={{0,4},{1,5},{2,6},{3,7},{4,0},{5,1},{6,2},{7,3},{8,12},{9,13},{10,... | collective-permute-start | bytes 61448 | tf_op jit(solution)/shard_map/ppermute | solution.py:457
  10.7 6.6 %collective-permute-start.3 = (f32[80,64]{1,0:T(8,128)S(1)}, f32[80,64]{1,0:T(8,128)S(1)}, u32[]{:S(2)}, u32[]{:S(2)}) collective-permute-start(f32[80,64]{1,0:T(8,128)S(1)} %get-tuple-element.15.refs_0_), channel_id=1, source_target_pairs={{0,6},{1,7},{2,4},{3,5},{4,2},{5,3},{6,0},{7,1},{8,14},{9,15},{10,... | collective-permute-start | bytes 61448 | tf_op jit(solution)/shard_map/ppermute | solution.py:457
  17.3 13.1 %copy-start = (f32[64,2048]{1,0:T(8,128)S(1)}, f32[64,2048]{1,0:T(8,128)}, u32[]{:S(2)}) copy-start(f32[64,2048]{1,0:T(8,128)} %near.1) | copy-start | bytes 1572868
  17.3 13.1 %copy-start.1 = (f32[64,1920]{1,0:T(8,128)S(1)}, f32[64,1920]{1,0:T(8,128)}, u32[]{:S(2)}) copy-start(f32[64,1920]{1,0:T(8,128)} %transfer.1) | copy-start | bytes 1474564
  17.3 13.1 %copy-start.2 = (f32[64,1920]{1,0:T(8,128)S(1)}, f32[64,1920]{1,0:T(8,128)}, u32[]{:S(2)}) copy-start(f32[64,1920]{1,0:T(8,128)} %coupling.1) | copy-start | bytes 1474564
  17.4 13.1 %copy-start.3 = (f32[64,1024]{1,0:T(8,128)S(1)}, f32[64,1024]{1,0:T(8,128)}, u32[]{:S(2)}) copy-start(f32[64,1024]{1,0:T(8,128)} %basis.1) | copy-start | bytes 786436
  18.4 10.2 %collective-permute-start.4 = (f32[16,2944]{1,0:T(8,128)S(1)}, f32[16,2944]{1,0:T(8,128)S(1)}, u32[]{:S(2)}, u32[]{:S(2)}) collective-permute-start(f32[16,2944]{1,0:T(8,128)S(1)} %get-tuple-element.20.own), channel_id=1, source_target_pairs={{0,1},{1,0},{2,3},{3,2},{4,5},{5,4},{6,7},{7,6},{8,9},{9,8},{10,11... | collective-permute-start | bytes 565256 | tf_op jit(solution)/shard_map/ppermute | solution.py:554
  18.4 12.1 %collective-permute-start.5 = (f32[16,2944]{1,0:T(8,128)S(1)}, f32[16,2944]{1,0:T(8,128)S(1)}, u32[]{:S(2)}, u32[]{:S(2)}) collective-permute-start(f32[16,2944]{1,0:T(8,128)S(1)} %get-tuple-element.20.own), channel_id=1, source_target_pairs={{1,2},{2,1},{3,4},{4,3},{5,6},{6,5},{7,8},{8,7},{9,10},{10,9},{11,... | collective-permute-start | bytes 565256 | tf_op jit(solution)/shard_map/ppermute | solution.py:555
  25.0 12.2 %collective-permute-start.6 = (f32[80,64]{1,0:T(8,128)S(1)}, f32[80,64]{1,0:T(8,128)S(1)}, u32[]{:S(2)}, u32[]{:S(2)}) collective-permute-start(f32[80,64]{1,0:T(8,128)S(1)} %get-tuple-element.24.refs_0_), channel_id=1, source_target_pairs={{0,8},{8,0},{16,24},{24,16},{1,9},{9,1},{17,25},{25,17},{2,10},{10... | collective-permute-start | bytes 61448 | tf_op jit(solution)/shard_map/ppermute | solution.py:457
  25.7 11.6 %collective-permute-start.7 = (f32[80,64]{1,0:T(8,128)S(1)}, f32[80,64]{1,0:T(8,128)S(1)}, u32[]{:S(2)}, u32[]{:S(2)}) collective-permute-start(f32[80,64]{1,0:T(8,128)S(1)} %get-tuple-element.24.refs_0_), channel_id=1, source_target_pairs={{0,16},{8,24},{16,0},{24,8},{1,17},{9,25},{17,1},{25,9},{2,18},{10... | collective-permute-start | bytes 61448 | tf_op jit(solution)/shard_map/ppermute | solution.py:457
  26.2 11.1 %collective-permute-start.8 = (f32[80,64]{1,0:T(8,128)S(1)}, f32[80,64]{1,0:T(8,128)S(1)}, u32[]{:S(2)}, u32[]{:S(2)}) collective-permute-start(f32[80,64]{1,0:T(8,128)S(1)} %get-tuple-element.24.refs_0_), channel_id=1, source_target_pairs={{0,24},{8,16},{16,8},{24,0},{1,25},{9,17},{17,9},{25,1},{2,26},{10... | collective-permute-start | bytes 61448 | tf_op jit(solution)/shard_map/ppermute | solution.py:457
  30.4 6.9 %copy-start.5 = (f32[1,64,896]{2,1,0:T(8,128)S(1)}, f32[1,64,896]{2,1,0:T(8,128)}, u32[]{:S(2)}) copy-start(f32[1,64,896]{2,1,0:T(8,128)} %param.19) | copy-start | bytes 688132
  30.5 6.9 %copy-start.6 = (f32[64,384]{1,0:T(8,128)S(1)}, f32[64,384]{1,0:T(8,128)}, u32[]{:S(2)}) copy-start(f32[64,384]{1,0:T(8,128)} %grp_transfer.1) | copy-start | bytes 294916
  30.5 6.9 %copy-start.7 = (f32[64,384]{1,0:T(8,128)S(1)}, f32[64,384]{1,0:T(8,128)}, u32[]{:S(2)}) copy-start(f32[64,384]{1,0:T(8,128)} %grp_coupling.1) | copy-start | bytes 294916

commit v2 on v1

--- a/solution.py
+++ b/solution.py
@@ -23,8 +23,6 @@
 OFFSETS = [2 * LEAF_DEV - 2 * (LEAF_DEV >> level) for level in range(LOC)]
 MIB = 1 << 20
 
-precise = lax.Precision.HIGHEST
-
 
 def halves(x):
     high = x.astype(jnp.bfloat16)
@@ -32,18 +30,19 @@
 
 
 def three_pass(a, b, side):
-    dims = (((1,), (side,)), ((), ()))
     dot = functools.partial(
-        lax.dot_general, dimension_numbers=dims, preferred_element_type=jnp.float32
+        lax.dot_general,
+        dimension_numbers=(((1,), (side,)), ((), ())),
+        preferred_element_type=jnp.float32,
     )
     a_high, a_low = halves(a)
     b_high, b_low = halves(b)
-    return dot(a_high, b_high) + (dot(a_high, b_low) + dot(a_low, b_high))
-
-
-def full(a, b, side):
-    dims = (((1,), (side,)), ((), ()))
-    return lax.dot_general(a, b, dims, precision=precise, preferred_element_type=jnp.float32)
+    if a.shape[1] % LANES:
+        return dot(a_high, b_high) + (dot(a_high, b_low) + dot(a_low, b_high))
+    return dot(
+        jnp.concatenate([a_high, a_low, a_high], axis=1),
+        jnp.concatenate([b_high, b_high, b_low], axis=side),
+    )
 
 
 def mm(a, b):
@@ -54,8 +53,14 @@
     return three_pass(a, b, 1)
 
 
-def mm_full(a, b):
-    return full(a, b, 0)
+def gram_pair(u):
+    u_high, u_low = halves(u)
+    t_high, t_low = halves(u.T)
+    dot = functools.partial(jnp.dot, preferred_element_type=jnp.float32)
+    wide = dot(t_high, jnp.concatenate([u_high, u_low], axis=1))
+    full = wide[:, 0:PAIR] + (wide[:, PAIR:] + dot(t_low, u_high))
+    row = lax.broadcasted_iota(jnp.int32, (PAIR, PAIR), 0) < RANK
+    return jnp.where(row == low_half(PAIR), full, 0.0)
 
 
 def low_half(rows):
@@ -106,8 +111,6 @@
         for k in range(8):
             a[k0 + k, k0:RANK, :] = rows[k]
             m[k0 + k, 0 : k0 + 8, :] = mrows[k]
-            if kb + 1 < blocks:
-                m[k0 + k, k0 + 8 : RANK, :] = jnp.zeros((RANK - k0 - 8, LANES), jnp.float32)
         for ib in range(kb + 1, blocks):
             for i in range(8 * ib, 8 * ib + 8):
                 acc = a[i, 8 * ib : RANK, :]
@@ -131,10 +134,15 @@
     for i in range(RANK):
         rows = gram[pl.ds(i, count, stride=RANK), :]
         both = jnp.concatenate([rows, swap_halves(rows)], axis=0)
-        a[i, :, 0 : 2 * count] = both[:, 0:RANK].T
+        first = i - i % 8
+        a[i, first:RANK, 0 : 2 * count] = both[:, 0:RANK].T[first:]
     factor_batch(a, m)
     for i in range(RANK):
-        rows = m[i, :, 0 : 2 * count].T
+        width = i - i % 8 + 8
+        rows = m[i, 0:width, 0 : 2 * count].T
+        if width < RANK:
+            rest = jnp.zeros((2 * count, RANK - width), jnp.float32)
+            rows = jnp.concatenate([rows, rest], axis=1)
         inv[pl.ds(i, count, stride=RANK), :] = jnp.concatenate([rows[:count], rows[count:]], axis=1)
 
 
@@ -150,49 +158,38 @@
     copies[0].wait()
     copies[1].wait()
     blocks = []
-    zs = []
     for p in range(LEAF_DEV // 2):
-        lanes = slice(PAIR * p, PAIR * (p + 1))
-        u = basis[:, lanes]
-        spread = spread_pair(u)
-        full = mm(u.T, u)
-        low = low_half(RANK)
+        u = basis[:, pair_lanes(p)]
         blocks.append(
-            jnp.concatenate(
-                [jnp.where(low, full[:RANK], 0.0), jnp.where(low, 0.0, full[RANK:])], axis=0
-            )
-        )
-        zs.append(mm(rhs[:, lanes], spread))
+            jnp.concatenate([gram_pair(u), mm(rhs[:, pair_lanes(p)], spread_pair(u))], axis=0)
+        )
     copies[2].wait()
     tile = 0
+    low = low_half(RANK)
     for level in range(LOC):
         pairs = len(blocks)
         for p in range(pairs):
-            gram[RANK * (tile + p) : RANK * (tile + p + 1), :] = jnp.where(
-                low_half(RANK), blocks[p][:RANK], blocks[p][RANK:]
+            gram[pair_rows(tile + p), :] = jnp.where(
+                low, blocks[p][0:RANK], blocks[p][RANK:PAIR]
             )
-            z_out[:, PAIR * (tile + p) : PAIR * (tile + p + 1)] = zs[p]
-        next_blocks = []
-        next_zs = []
+            z_out[:, pair_lanes(tile + p)] = blocks[p][PAIR:]
+        fs = [
+            (stack_high if p % 2 else stack_low)(transfer[:, pair_lanes(tile + p)])
+            for p in range(pairs)
+        ]
+        hs = [mm(block, f) for block, f in zip(blocks, fs)]
+        parents = []
         for q in range((pairs + 1) // 2):
-            first = transfer[:, PAIR * (tile + 2 * q) : PAIR * (tile + 2 * q + 1)]
-            f = stack_low(first)
-            h = mm(blocks[2 * q], f)
-            z = mm(zs[2 * q], f)
-            parent = mm(f.T, h)
-            if pairs > 1:
-                second = transfer[:, PAIR * (tile + 2 * q + 1) : PAIR * (tile + 2 * q + 2)]
-                f = stack_high(second)
-                h = mm(blocks[2 * q + 1], f)
-                z = z + mm(zs[2 * q + 1], f)
-                parent = parent + mm(f.T, h)
-            next_blocks.append(parent)
-            next_zs.append(z)
+            both = slice(2 * q, 2 * q + 2)
+            g = mm(
+                jnp.concatenate([f.T for f in fs[both]], axis=1),
+                jnp.concatenate([h[0:PAIR] for h in hs[both]], axis=0),
+            )
+            parents.append(jnp.concatenate([g, sum(h[PAIR:] for h in hs[both])], axis=0))
         tile += pairs
-        blocks = next_blocks
-        zs = next_zs
+        blocks = parents
     top[0:RANK, :] = blocks[0][0:RANK, 0:RANK]
-    top[RANK:ROWS, :] = zs[0][:, 0:RANK]
+    top[RANK:ROWS, :] = blocks[0][PAIR:, 0:RANK]
 
 
 def pair_rows(p):
@@ -213,19 +210,27 @@
 
 
 def merge(nodes, tile, transfer):
-    parents = []
-    for p in range(len(nodes) // 2):
-        pair = transfer[:, pl.ds(pl.multiple_of(PAIR * (tile + p), PAIR), PAIR)]
-        even, odd = pair[:, 0:RANK], pair[:, RANK:PAIR]
-        he, ho = mm(nodes[2 * p], even), mm(nodes[2 * p + 1], odd)
-        g = mm(even.T, he[0:RANK]) + mm(odd.T, ho[0:RANK])
-        parents.append(jnp.concatenate([g, he[RANK:] + ho[RANK:]], axis=0))
-    return parents
+    pairs = range(len(nodes) // 2)
+    fs = [
+        stack_low(transfer[:, pl.ds(pl.multiple_of(PAIR * (tile + p), PAIR), PAIR)]) for p in pairs
+    ]
+    hs = [
+        mm(jnp.concatenate([nodes[2 * p], swap_halves(nodes[2 * p + 1])], axis=0), fs[p])
+        for p in pairs
+    ]
+    gs = [
+        mm(f[:, 0:RANK].T, jnp.concatenate([h[0:RANK], h[ROWS : ROWS + RANK]], axis=0))
+        for f, h in zip(fs, hs)
+    ]
+    return [
+        jnp.concatenate([g, h[RANK:ROWS] + h[ROWS + RANK :]], axis=0) for g, h in zip(gs, hs)
+    ]
 
 
 def climb(blocks, place, start, bits, count, transfer, stack, records, first_record):
+    empty = jnp.zeros((ROWS, RANK), jnp.float32)
     for k, block in enumerate(blocks):
-        stack[k] = block[...]
+        stack[k] = jnp.concatenate([block[...], empty], axis=1)
     here = lax.shift_right_logical(place, start)
     low = here & (2**bits - 1)
     base = here - low
@@ -248,10 +253,28 @@
     blocks = refs[: 2**bits]
     top, records = refs[-3 - (len(refs) - 2**bits - 3) // 2 :][:2]
     stack = refs[-1]
-    top[...] = climb(blocks, lax.axis_index(axis), start, bits, count, transfer, stack, records, 0)
+    top[...] = climb(blocks, lax.axis_index(axis), start, bits, count, transfer, stack, records, 0)[
+        :, 0:RANK
+    ]
+
+
+def own_tile(n, grp_count, dev_count, grp_blocks, dev_blocks):
+    dev_levels = dev_count.bit_length() - 1
+    if n < dev_levels:
+        count, shift, place, blocks = dev_count, n, lax.axis_index("dev"), dev_blocks
+    else:
+        count, shift, place, blocks = grp_count, n - dev_levels, lax.axis_index("grp"), grp_blocks
+    index = 2 * count - 2 * (count >> shift) + lax.shift_right_logical(place, shift)
+    pair = blocks[:, pl.ds(pl.multiple_of(PAIR * (index // 2), PAIR), PAIR)]
+    lane = lax.broadcasted_iota(jnp.int32, (NRHS, PAIR), 1)
+    odd = index % 2
+    return pair, lax.shift_right_logical(lane, RANK.bit_length() - 1) == odd, odd == 1
 
 
 def couple_kernel(
+    grp_count,
+    dev_count,
+    levels,
     near_partner_in,
     far_partner_in,
     own,
@@ -259,11 +282,12 @@
     beside,
     inv,
     coupling,
-    transfer,
-    basis,
     near,
+    grp_transfer,
+    dev_transfer,
     base,
-    lift,
+    terms,
+    paths,
     window,
     near_partner,
     far_partner,
@@ -293,17 +317,25 @@
                 window[1, first + t] = swap_halves(tile)
         slot += 3 * span
 
+    def pick(first, index, parity):
+        return window[(index & 1) ^ parity, first + lax.shift_right_logical(index, 1)]
+
+    low16 = low_half(NRHS)
+    edges = []
+    for n in range(levels - 1):
+        pair, _, odd_node = own_tile(n, grp_count, dev_count, grp_transfer, dev_transfer)
+        edge = jnp.where(odd_node, swap_halves(pair), pair)
+        edges.append(jnp.where(low_half(RANK), edge, 0.0))
+    path = None
+    for n, edge in enumerate(edges):
+        path = edge if path is None else mm(path, jnp.concatenate([edge, edge], axis=0))
+        paths[:, RANK * n : RANK * (n + 1)] = path[:, 0:RANK]
+
     for copy in copies:
         copy.wait()
-
-    def pick(first, index, parity):
-        return window[(index & 1) ^ parity, first + lax.shift_right_logical(index, 1)]
-
-    low16 = low_half(NRHS)
-    lifted = []
+    coupled = []
     for level in range(LOC):
         m = LEAF_DEV >> level
-        tiles = []
         for p in range(m // 2):
             node = OFFSETS[level] + 2 * p
             values = []
@@ -311,32 +343,12 @@
                 index = far_partner[0, node + side] - (place - 1) * m
                 values.append(pick(firsts[level + 1], index, side))
             xhat = jnp.where(low16, values[0], values[1])
-            y = mm_t(xhat, spread_pair(coupling[:, pair_lanes(node // 2)]))
-            tiles.append(mm(y, spread_pair(inv[pair_rows(node // 2), :])))
-        lifted.append(tiles)
-
-    state = None
-    for level in reversed(range(LOC)):
-        m = LEAF_DEV >> level
-        tile = OFFSETS[level] // 2
-        next_state = []
-        for p in range(m // 2):
-            pair = transfer[:, PAIR * (tile + p) : PAIR * (tile + p + 1)]
-            if state is None:
-                f = stack_low(pair)
-                rows = f[:, 0:RANK].T
-                next_state.append(jnp.concatenate([lifted[level][p], rows], axis=0))
-                continue
-            f = stack_high(pair) if p % 2 else stack_low(pair)
-            rows = mm_t(state[p // 2], f)
-            next_state.append(
-                jnp.concatenate([rows[0:NRHS] + lifted[level][p], rows[NRHS:]], axis=0)
-            )
-        state = next_state
+            coupled.append(mm_t(xhat, spread_pair(coupling[:, pair_lanes(node // 2)])))
+    for p, y in enumerate(coupled):
+        terms[:, pair_lanes(p)] = mm(y, spread_pair(inv[pair_rows(p), :]))
 
     for p in range(LEAF_DEV // 2):
         lanes = slice(PAIR * p, PAIR * (p + 1))
-        out = mm_t(state[p], spread_pair(basis[:, lanes]))
         own_points = own[:, lanes]
         swapped = swap_halves(own_points)
         inputs = []
@@ -352,14 +364,7 @@
             axis=0,
         )
         near_out = mm_t(jnp.concatenate(inputs, axis=0), weights)
-        base[:, lanes] = out[0:NRHS] + jnp.where(low16, near_out[0:NRHS], near_out[NRHS:])
-        lift[:, lanes] = out[NRHS:]
-
-
-def half_tile(array, index):
-    pair = array[:, pl.ds(pl.multiple_of(PAIR * (index // 2), PAIR), PAIR)]
-    lane = lax.broadcasted_iota(jnp.int32, (NRHS, PAIR), 1)
-    return pair, lax.shift_right_logical(lane, RANK.bit_length() - 1) == index % 2
+        base[:, lanes] = jnp.where(low16, near_out[0:NRHS], near_out[NRHS:])
 
 
 def twice(x):
@@ -374,10 +379,12 @@
     record_spans,
     grp_transfer,
     grp_coupling,
-    dev_transfer,
     dev_coupling,
     base,
-    lift,
+    terms,
+    paths,
+    transfer,
+    basis,
     *refs,
 ):
     blocks = refs[: 2**bits]
@@ -395,36 +402,51 @@
     levels = level + bits
     for n in range(levels):
         d[pair_rows(n), :] = jnp.concatenate(
-            [records[2 * n, 0:RANK], records[2 * n + 1, 0:RANK]], axis=1
-        )
-    d[pair_rows(levels), :] = twice(top[0:RANK])
+            [records[2 * n, 0:RANK, 0:RANK], records[2 * n + 1, 0:RANK, 0:RANK]], axis=1
+        )
+    d[pair_rows(levels), :] = top[0:RANK]
     invert_pairs(d, a, m, inv, inv.shape[0] // RANK)
     root_inverse = inv[pair_rows(levels), 0:RANK]
     keep = lax.broadcasted_iota(jnp.int32, (RANK, RANK), 0) >= lax.broadcasted_iota(
         jnp.int32, (RANK, RANK), 1
     )
-    root[...] = jnp.where(keep, mm_t(top[0:RANK], root_inverse), 0.0)
-    dev_levels = dev_count.bit_length() - 1
+    root[...] = jnp.where(keep, mm_t(top[0:RANK, 0:RANK], root_inverse), 0.0)
     low = low_half(NRHS)
-    terms = []
+    xhats = [
+        mm_t(
+            jnp.where(low, 0.0, swap_halves(records[2 * n + 1, RANK:ROWS])), inv[pair_rows(n), :]
+        )
+        for n in range(levels)
+    ]
+    yhats = []
     for n in range(levels):
-        if n < dev_levels:
-            count, shift, spot = dev_count, n, lax.axis_index("dev")
-            transfer, coupling = dev_transfer, dev_coupling
-        else:
-            count, shift, spot = grp_count, n - dev_levels, lax.axis_index("grp")
-            transfer, coupling = grp_transfer, grp_coupling
-        index = 2 * count - 2 * (count >> shift) + lax.shift_right_logical(spot, shift)
-        factors = inv[pair_rows(n), :]
-        other = jnp.where(low, 0.0, twice(records[2 * n + 1, RANK:ROWS]))
-        pair, half = half_tile(coupling, index)
-        xhat = jnp.where(half, twice(mm_t(other, factors)), 0.0)
-        yhat = mm_t(xhat, pair)
-        terms.append((mm(yhat, factors)[:, 0:RANK], *half_tile(transfer, index)))
-    value = None
-    for term, pair, half in reversed(terms):
-        value = term if value is None else term + mm_t(jnp.where(half, twice(value), 0.0), pair)
-    product[...] = base[...] + mm(value, lift[...])
+        pair, half, _ = own_tile(n, grp_count, dev_count, grp_coupling, dev_coupling)
+        yhats.append(mm_t(jnp.where(half, twice(xhats[n]), 0.0), pair))
+    values = [mm(yhats[n], inv[pair_rows(n), :])[:, 0:RANK] for n in range(levels)]
+    value = values[0]
+    if levels > 1:
+        upper = values[1:]
+        edges = paths[...]
+        if len(upper) % 2:
+            upper.append(jnp.zeros_like(value))
+            edges = jnp.concatenate([edges, jnp.zeros_like(edges[:, 0:RANK])], axis=1)
+        value = value + mm_t(jnp.concatenate(upper, axis=1), edges)
+    state = [twice(value)]
+    for level in reversed(range(LOC)):
+        m = LEAF_DEV >> level
+        tile = OFFSETS[level] // 2
+        state = [
+            terms[:, pair_lanes(tile + p)]
+            + mm_t(
+                state[p // 2],
+                (stack_high if p % 2 else stack_low)(transfer[:, pair_lanes(tile + p)]),
+            )
+            for p in range(m // 2)
+        ]
+    for p in range(LEAF_DEV // 2):
+        product[:, pair_lanes(p)] = base[:, pair_lanes(p)] + mm_t(
+            state[p], spread_pair(basis[:, pair_lanes(p)])
+        )
 
 
 def vmem(count):
@@ -473,11 +495,11 @@
     anywhere = [pl.BlockSpec(memory_space=pl.ANY)] * len(carried)
     return pl.pallas_call(
         functools.partial(climb_kernel, axis, start, bits, count),
-        out_shape=[f32(ROWS, RANK), f32(2 * bits, ROWS, RANK)] + [f32(*c.shape) for c in carried],
+        out_shape=[f32(ROWS, RANK), f32(2 * bits, ROWS, PAIR)] + [f32(*c.shape) for c in carried],
         in_specs=vmem(1 + 2**bits) + anywhere,
         out_specs=vmem(2) + anywhere,
         input_output_aliases={1 + 2**bits + n: 2 + n for n in range(len(carried))},
-        scratch_shapes=[pltpu.VMEM((2**bits, ROWS, RANK), jnp.float32)],
+        scratch_shapes=[pltpu.VMEM((2**bits, ROWS, PAIR), jnp.float32)],
         compiler_params=params(8),
         cost_estimate=micros(1),
         name="climb",
@@ -556,12 +578,18 @@
         packed, both, [(i, ((i + 1) ^ 1) - 1) for i in range(1, ends)]
     )
 
+    grp_chunks = chunks(grp_count.bit_length() - 1, 2)
+    levels = sum(spans) + grp_count.bit_length() - 1
     window_tiles = 3 * (POINT_SPAN + NODE_SPAN) // PAIR
-    base, lift = pl.pallas_call(
-        couple_kernel,
-        out_shape=[f32(NRHS, POINT_SPAN), f32(RANK, POINT_SPAN)],
+    base, terms, paths = pl.pallas_call(
+        functools.partial(couple_kernel, grp_count, dev_count, levels),
+        out_shape=[
+            f32(NRHS, POINT_SPAN),
+            f32(NRHS, NODE_SPAN),
+            f32(RANK, RANK * (levels - 1)),
+        ],
         in_specs=hbm(2) + vmem(8),
-        out_specs=vmem(2),
+        out_specs=vmem(3),
         scratch_shapes=[
             pltpu.VMEM((2, window_tiles, NRHS, PAIR), jnp.float32),
             pltpu.SMEM(near_partner.shape, jnp.int32),
@@ -569,7 +597,7 @@
             pltpu.SemaphoreType.DMA((2,)),
         ],
         compiler_params=params(24),
-        cost_estimate=micros(10),
+        cost_estimate=micros(4),
         name="couple",
     )(
         in_hbm(near_partner),
@@ -579,12 +607,11 @@
         beside,
         inv,
         local_coupling,
-        local_transfer,
-        leaf_basis,
         near_blocks,
-    )
-
-    grp_chunks = chunks(grp_count.bit_length() - 1, 2)
+        grp_transfer,
+        dev_transfer,
+    )
+
     for start, bits in grp_chunks[:-1]:
         blocks = exchange(top, "grp", start, bits)
         top, record = climb_call(blocks, "grp", start, bits, grp_count, grp_transfer)
@@ -592,16 +619,15 @@
         spans.append(bits)
     start, bits = grp_chunks[-1]
     blocks = exchange(top, "grp", start, bits)
-    levels = sum(spans) + bits
     batch = 8 * ((levels + 1 + 7) // 8)
     return pl.pallas_call(
         functools.partial(top_kernel, grp_count, dev_count, start, bits, tuple(spans)),
         out_shape=[f32(NRHS, POINT_SPAN), f32(RANK, RANK)],
-        in_specs=vmem(6 + len(blocks) + len(records)),
+        in_specs=vmem(8 + len(blocks) + len(records)),
         out_specs=vmem(2),
         scratch_shapes=[
-            pltpu.VMEM((2**bits, ROWS, RANK), jnp.float32),
-            pltpu.VMEM((2 * levels, ROWS, RANK), jnp.float32),
+            pltpu.VMEM((2**bits, ROWS, PAIR), jnp.float32),
+            pltpu.VMEM((2 * levels, ROWS, PAIR), jnp.float32),
             pltpu.VMEM((batch * RANK, LANES), jnp.float32),
             pltpu.VMEM((RANK, RANK, LANES), jnp.float32),
             pltpu.VMEM((RANK, RANK, LANES), jnp.float32),
@@ -613,10 +639,12 @@
     )(
         grp_transfer,
         grp_coupling,
-        dev_transfer,
         dev_coupling,
         base,
-        lift,
+        terms,
+        paths,
+        local_transfer,
+        leaf_basis,
         *blocks,
         *records,
     )

time: 47.3 us -> 40.7 us (0.86)
  the two profiles are of different devices: /device:TPU:4 before, /device:TPU:0 now
where the time goes in v2:
time: 40.7 us; the launch traced here: 40.6 us
  Pallas kernels  20.9 us (51%)
  starting transfers between devices  16.1 us (40%)
  waiting for transfers between devices  2.73 us (7%)
  between operations  0.81 us (2%)
    ppermute x7, starting transfers between devices, exchange(): lax.ppermute(block, axis, [(i, i ^ k << start) for i in range(count)])  15.2 us
    pallas_call x1, Pallas kernels, shards(): pl.pallas_call(functools.partial(top_kernel, grp_count, dev_count, start,...  8.35 us
    pallas_call x1, Pallas kernels, local_call(): pl.pallas_call(local_kernel, out_shape=[f32(BATCH * RANK, PAIR), f32(NRHS...  6 us
    pallas_call x1, Pallas kernels, shards(): pl.pallas_call(gram_kernel, out_shape=[f32(BATCH * RANK, PAIR), f32(NRHS,...  3.27 us
    ppermute x7, waiting for transfers between devices, exchange(): lax.ppermute(block, axis, [(i, i ^ k << start) for i in range(count)])  2.72 us
    pallas_call x1, Pallas kernels, shards(): pl.pallas_call(functools.partial(couple_kernel, grp_count, dev_count, lev...  2.09 us
    pallas_call x2, Pallas kernels, climb_call(): pl.pallas_call(functools.partial(climb_kernel, axis, start, bits, count),...  1.17 us
    ppermute x1, starting transfers between devices, shards(): lax.ppermute(packed, both, [(i, (i + 1 ^ 1) - 1) for i in range(1, ends)])  0.85 us
  transfers between devices with their start and end apart: 9, of which 2 were waited for; matrix products, arithmetic and copies ran while one was open for 0% of the time, Pallas kernels for 20%

profile of v2, /device:TPU:0, one launch (start us, length us, event | category | flops | bytes accessed | tf_op | source)
XLA Modules:
  0.0 40.6 jit_solution(3265075527242358731)
XLA Ops:
  0.6 0.0 copy-start.4
  0.6 3.3 %gram.1 = (f32[1024,128]{1,0:T(8,128)S(1)}, f32[16,1920]{1,0:T(8,128)S(1)}, f32[80,64]{1,0:T(8,128)S(1)}) custom-call(f32[64,1024]{1,0:T(8,128)} %basis.1, f32[16,1024]{1,0:T(8,128)} %rhs.1, f32[64,1920]{1,0:T(8,128)} %transfer.1), custom_call_target="tpu_custom_call" | custom-call | flops 4000000000 | bytes 1048576 | tf_op jit(solution)/shard_map/gram/pallas_call | solution.py:540
  3.9 0.5 %collective-permute-start = (f32[80,64]{1,0:T(8,128)S(1)}, f32[80,64]{1,0:T(8,128)S(1)}, u32[]{:S(2)}, u32[]{:S(2)}) collective-permute-start(f32[80,64]{1,0:T(8,128)S(1)} %get-tuple-element.15.refs_0_), channel_id=1, source_target_pairs={{0,1},{1,0},{2,3},{3,2},{4,5},{5,4},{6,7},{7,6},{8,9},{9,8},{10,11... | collective-permute-start | bytes 61448 | tf_op jit(solution)/shard_map/ppermute | solution.py:479
  4.4 0.9 %collective-permute-done.refs_1_ = f32[80,64]{1,0:T(8,128)S(1)} collective-permute-done((f32[80,64]{1,0:T(8,128)S(1)}, f32[80,64]{1,0:T(8,128)S(1)}, u32[]{:S(2)}, u32[]{:S(2)}) %collective-permute-start) | collective-permute-done | bytes 20512 | tf_op jit(solution)/shard_map/ppermute | solution.py:479
  5.3 0.4 climb.2
  5.7 3.0 %collective-permute-start.1 = (f32[80,64]{1,0:T(8,128)S(1)}, f32[80,64]{1,0:T(8,128)S(1)}, u32[]{:S(2)}, u32[]{:S(2)}) collective-permute-start(f32[80,64]{1,0:T(8,128)S(1)} %get-tuple-element.16.refs_0_), channel_id=1, source_target_pairs={{0,2},{1,3},{2,0},{3,1},{4,6},{5,7},{6,4},{7,5},{8,10},{9,11},{10,... | collective-permute-start | bytes 61448 | tf_op jit(solution)/shard_map/ppermute | solution.py:479
  8.7 2.6 %collective-permute-start.2 = (f32[80,64]{1,0:T(8,128)S(1)}, f32[80,64]{1,0:T(8,128)S(1)}, u32[]{:S(2)}, u32[]{:S(2)}) collective-permute-start(f32[80,64]{1,0:T(8,128)S(1)} %get-tuple-element.16.refs_0_), channel_id=1, source_target_pairs={{0,4},{1,5},{2,6},{3,7},{4,0},{5,1},{6,2},{7,3},{8,12},{9,13},{10,... | collective-permute-start | bytes 61448 | tf_op jit(solution)/shard_map/ppermute | solution.py:479
  11.3 0.0 collective-permute-start.3
  11.3 6.0 %local_factors.1 = (f32[1024,128]{1,0:T(8,128)S(1)}, f32[16,2944]{1,0:T(8,128)S(1)}) custom-call(f32[1024,128]{1,0:T(8,128)S(1)} %get-tuple-element.17.gram, f32[16,1920]{1,0:T(8,128)S(1)} %get-tuple-element.18.z, f32[16,1024]{1,0:T(8,128)S(1)} %copy-done.8, f32[2,80,128]{2,1,0:T(8,128)S(1)} %get-tuple-element.19.after.refs_4_), custom_call_target="tpu_custom_call" | custom-call | flops 8000000000 | bytes 1048576 | tf_op jit(solution)/shard_map/local_factors/pallas_call | solution.py:510
  17.3 0.0 collective-permute-done.1.refs_1_
  17.3 0.0 collective-permute-done.2.refs_2_
  17.3 0.0 collective-permute-done.3.refs_3_
  17.3 0.0 copy-start
  17.3 0.0 copy-start.1
  17.3 0.0 copy-start.6
  17.4 0.8 %climb.3 = (f32[80,64]{1,0:T(8,128)S(1)}, f32[4,80,128]{2,1,0:T(8,128)S(1)}, f32[16,2944]{1,0:T(8,128)S(1)}) custom-call(f32[64,896]{1,0:T(8,128)S(1)} %bitcast.3, f32[80,64]{1,0:T(8,128)S(1)} %get-tuple-element.16.refs_0_, f32[80,64]{1,0:T(8,128)S(1)} %collective-permute-done.1.refs_1_, ...), custom_call_target="tpu_custom_call", output_to_operand_aliasing={{2}: (5, {})} | custom-call | flops 1000000000 | bytes 1048576 | tf_op jit(solution)/shard_map/climb/pallas_call | solution.py:496
  18.1 0.1 collective-permute-start.4
  18.2 0.9 %collective-permute-start.5 = (f32[16,2944]{1,0:T(8,128)S(1)}, f32[16,2944]{1,0:T(8,128)S(1)}, u32[]{:S(2)}, u32[]{:S(2)}) collective-permute-start(f32[16,2944]{1,0:T(8,128)S(1)} %get-tuple-element.21.own), channel_id=1, source_target_pairs={{1,2},{2,1},{3,4},{4,3},{5,6},{6,5},{7,8},{8,7},{9,10},{10,9},{11,... | collective-permute-start | bytes 565256 | tf_op jit(solution)/shard_map/ppermute | solution.py:577
  19.1 6.7 %collective-permute-start.6 = (f32[80,64]{1,0:T(8,128)S(1)}, f32[80,64]{1,0:T(8,128)S(1)}, u32[]{:S(2)}, u32[]{:S(2)}) collective-permute-start(f32[80,64]{1,0:T(8,128)S(1)} %get-tuple-element.26.refs_0_), channel_id=1, source_target_pairs={{0,8},{8,0},{16,24},{24,16},{1,9},{9,1},{17,25},{25,17},{2,10},{10... | collective-permute-start | bytes 61448 | tf_op jit(solution)/shard_map/ppermute | solution.py:479
  25.8 1.5 %collective-permute-start.7 = (f32[80,64]{1,0:T(8,128)S(1)}, f32[80,64]{1,0:T(8,128)S(1)}, u32[]{:S(2)}, u32[]{:S(2)}) collective-permute-start(f32[80,64]{1,0:T(8,128)S(1)} %get-tuple-element.26.refs_0_), channel_id=1, source_target_pairs={{0,16},{8,24},{16,0},{24,8},{1,17},{9,25},{17,1},{25,9},{2,18},{10... | collective-permute-start | bytes 61448 | tf_op jit(solution)/shard_map/ppermute | solution.py:479
  27.3 0.9 %collective-permute-start.8 = (f32[80,64]{1,0:T(8,128)S(1)}, f32[80,64]{1,0:T(8,128)S(1)}, u32[]{:S(2)}, u32[]{:S(2)}) collective-permute-start(f32[80,64]{1,0:T(8,128)S(1)} %get-tuple-element.26.refs_0_), channel_id=1, source_target_pairs={{0,24},{8,16},{16,8},{24,0},{1,25},{9,17},{17,9},{25,1},{2,26},{10... | collective-permute-start | bytes 61448 | tf_op jit(solution)/shard_map/ppermute | solution.py:479
  28.2 0.0 collective-permute-done.4.twin
  28.2 0.0 collective-permute-done.5.beside
  28.2 0.0 copy-start.2
  28.2 0.0 copy-start.3
  28.2 0.0 copy-start.5
  28.2 0.0 copy-start.7
  28.2 2.1 %couple.1 = (f32[16,1024]{1,0:T(8,128)S(1)}, f32[16,1920]{1,0:T(8,128)S(1)}, f32[64,256]{1,0:T(8,128)S(1)}) custom-call(s32[16]{0:T(128)} %near_partner_in.1, s32[1,30]{1,0:T(1,128)} %far_partner_in.1, f32[16,2944]{1,0:T(8,128)S(1)} %get-tuple-element.21.own, f32[16,2944]{1,0:T(8,128)S(1)} %collective-permute-done.4.twin, ...), custom_call_target="tpu_custom_call" | custom-call | flops 4000000000 | bytes 1048576 | tf_op jit(solution)/shard_map/couple/pallas_call | solution.py:584
  30.3 0.0 collective-permute-done.6.refs_1_
  30.3 0.0 collective-permute-done.7.refs_2_
  30.4 1.8 %collective-permute-done.8.refs_3_ = f32[80,64]{1,0:T(8,128)S(1)} collective-permute-done((f32[80,64]{1,0:T(8,128)S(1)}, f32[80,64]{1,0:T(8,128)S(1)}, u32[]{:S(2)}, u32[]{:S(2)}) %collective-permute-start.8) | collective-permute-done | bytes 20512 | tf_op jit(solution)/shard_map/ppermute | solution.py:479
  32.2 8.4 %top.1 = (f32[16,1024]{1,0:T(8,128)}, f32[64,64]{1,0:T(8,128)}) custom-call(f32[64,384]{1,0:T(8,128)S(1)} %copy-done.6, f32[64,384]{1,0:T(8,128)S(1)} %copy-done.7, f32[64,896]{1,0:T(8,128)S(1)} %bitcast.5, f32[16,1024]{1,0:T(8,128)S(1)} %get-tuple-element.23.base, f32[16,1920]{1,0:T(8,128)S(1)} %get-tuple-element.24.terms, ...), custom_call_target="tpu_custom_call" | custom-call | flops 8999999488 | bytes 1048576 | tf_op jit(solution)/shard_map/top/pallas_call | solution.py:623
  (10 shorter events, 0.0 us)
Async XLA Ops:
  0.6 4.7 %copy-start.4 = (f32[1,64,896]{2,1,0:T(8,128)S(1)}, f32[1,64,896]{2,1,0:T(8,128)}, u32[]{:S(2)}) copy-start(f32[1,64,896]{2,1,0:T(8,128)} %param.18) | copy-start | bytes 688132
  3.9 1.4 %collective-permute-start = (f32[80,64]{1,0:T(8,128)S(1)}, f32[80,64]{1,0:T(8,128)S(1)}, u32[]{:S(2)}, u32[]{:S(2)}) collective-permute-start(f32[80,64]{1,0:T(8,128)S(1)} %get-tuple-element.15.refs_0_), channel_id=1, source_target_pairs={{0,1},{1,0},{2,3},{3,2},{4,5},{5,4},{6,7},{7,6},{8,9},{9,8},{10,11... | collective-permute-start | bytes 61448 | tf_op jit(solution)/shard_map/ppermute | solution.py:479
  5.3 6.0 %copy-start.8 = (f32[16,1024]{1,0:T(8,128)S(1)}, f32[16,1024]{1,0:T(8,128)}, u32[]{:S(2)}) copy-start(f32[16,1024]{1,0:T(8,128)} %rhs.1) | copy-start | bytes 196612
  5.7 11.6 %collective-permute-start.1 = (f32[80,64]{1,0:T(8,128)S(1)}, f32[80,64]{1,0:T(8,128)S(1)}, u32[]{:S(2)}, u32[]{:S(2)}) collective-permute-start(f32[80,64]{1,0:T(8,128)S(1)} %get-tuple-element.16.refs_0_), channel_id=1, source_target_pairs={{0,2},{1,3},{2,0},{3,1},{4,6},{5,7},{6,4},{7,5},{8,10},{9,11},{10,... | collective-permute-start | bytes 61448 | tf_op jit(solution)/shard_map/ppermute | solution.py:479
  8.7 8.6 %collective-permute-start.2 = (f32[80,64]{1,0:T(8,128)S(1)}, f32[80,64]{1,0:T(8,128)S(1)}, u32[]{:S(2)}, u32[]{:S(2)}) collective-permute-start(f32[80,64]{1,0:T(8,128)S(1)} %get-tuple-element.16.refs_0_), channel_id=1, source_target_pairs={{0,4},{1,5},{2,6},{3,7},{4,0},{5,1},{6,2},{7,3},{8,12},{9,13},{10,... | collective-permute-start | bytes 61448 | tf_op jit(solution)/shard_map/ppermute | solution.py:479
  11.3 6.0 %collective-permute-start.3 = (f32[80,64]{1,0:T(8,128)S(1)}, f32[80,64]{1,0:T(8,128)S(1)}, u32[]{:S(2)}, u32[]{:S(2)}) collective-permute-start(f32[80,64]{1,0:T(8,128)S(1)} %get-tuple-element.16.refs_0_), channel_id=1, source_target_pairs={{0,6},{1,7},{2,4},{3,5},{4,2},{5,3},{6,0},{7,1},{8,14},{9,15},{10,... | collective-permute-start | bytes 61448 | tf_op jit(solution)/shard_map/ppermute | solution.py:479
  17.3 10.8 %copy-start = (f32[64,2048]{1,0:T(8,128)S(1)}, f32[64,2048]{1,0:T(8,128)}, u32[]{:S(2)}) copy-start(f32[64,2048]{1,0:T(8,128)} %near.1) | copy-start | bytes 1572868
  17.3 10.8 %copy-start.1 = (f32[64,1920]{1,0:T(8,128)S(1)}, f32[64,1920]{1,0:T(8,128)}, u32[]{:S(2)}) copy-start(f32[64,1920]{1,0:T(8,128)} %coupling.1) | copy-start | bytes 1474564
  17.3 10.8 %copy-start.6 = (f32[64,384]{1,0:T(8,128)S(1)}, f32[64,384]{1,0:T(8,128)}, u32[]{:S(2)}) copy-start(f32[64,384]{1,0:T(8,128)} %grp_transfer.3) | copy-start | bytes 294916
  18.1 10.0 %collective-permute-start.4 = (f32[16,2944]{1,0:T(8,128)S(1)}, f32[16,2944]{1,0:T(8,128)S(1)}, u32[]{:S(2)}, u32[]{:S(2)}) collective-permute-start(f32[16,2944]{1,0:T(8,128)S(1)} %get-tuple-element.21.own), channel_id=1, source_target_pairs={{0,1},{1,0},{2,3},{3,2},{4,5},{5,4},{6,7},{7,6},{8,9},{9,8},{10,11... | collective-permute-start | bytes 565256 | tf_op jit(solution)/shard_map/ppermute | solution.py:576
  18.2 9.9 %collective-permute-start.5 = (f32[16,2944]{1,0:T(8,128)S(1)}, f32[16,2944]{1,0:T(8,128)S(1)}, u32[]{:S(2)}, u32[]{:S(2)}) collective-permute-start(f32[16,2944]{1,0:T(8,128)S(1)} %get-tuple-element.21.own), channel_id=1, source_target_pairs={{1,2},{2,1},{3,4},{4,3},{5,6},{6,5},{7,8},{8,7},{9,10},{10,9},{11,... | collective-permute-start | bytes 565256 | tf_op jit(solution)/shard_map/ppermute | solution.py:577
  19.1 11.3 %collective-permute-start.6 = (f32[80,64]{1,0:T(8,128)S(1)}, f32[80,64]{1,0:T(8,128)S(1)}, u32[]{:S(2)}, u32[]{:S(2)}) collective-permute-start(f32[80,64]{1,0:T(8,128)S(1)} %get-tuple-element.26.refs_0_), channel_id=1, source_target_pairs={{0,8},{8,0},{16,24},{24,16},{1,9},{9,1},{17,25},{25,17},{2,10},{10... | collective-permute-start | bytes 61448 | tf_op jit(solution)/shard_map/ppermute | solution.py:479
  25.8 4.6 %collective-permute-start.7 = (f32[80,64]{1,0:T(8,128)S(1)}, f32[80,64]{1,0:T(8,128)S(1)}, u32[]{:S(2)}, u32[]{:S(2)}) collective-permute-start(f32[80,64]{1,0:T(8,128)S(1)} %get-tuple-element.26.refs_0_), channel_id=1, source_target_pairs={{0,16},{8,24},{16,0},{24,8},{1,17},{9,25},{17,1},{25,9},{2,18},{10... | collective-permute-start | bytes 61448 | tf_op jit(solution)/shard_map/ppermute | solution.py:479
  27.3 4.9 %collective-permute-start.8 = (f32[80,64]{1,0:T(8,128)S(1)}, f32[80,64]{1,0:T(8,128)S(1)}, u32[]{:S(2)}, u32[]{:S(2)}) collective-permute-start(f32[80,64]{1,0:T(8,128)S(1)} %get-tuple-element.26.refs_0_), channel_id=1, source_target_pairs={{0,24},{8,16},{16,8},{24,0},{1,25},{9,17},{17,9},{25,1},{2,26},{10... | collective-permute-start | bytes 61448 | tf_op jit(solution)/shard_map/ppermute | solution.py:479
  28.2 4.0 %copy-start.2 = (f32[64,1920]{1,0:T(8,128)S(1)}, f32[64,1920]{1,0:T(8,128)}, u32[]{:S(2)}) copy-start(f32[64,1920]{1,0:T(8,128)} %transfer.1) | copy-start | bytes 1474564
  28.2 4.0 %copy-start.3 = (f32[64,1024]{1,0:T(8,128)S(1)}, f32[64,1024]{1,0:T(8,128)}, u32[]{:S(2)}) copy-start(f32[64,1024]{1,0:T(8,128)} %basis.1) | copy-start | bytes 786436
  28.2 4.0 %copy-start.5 = (f32[1,64,896]{2,1,0:T(8,128)S(1)}, f32[1,64,896]{2,1,0:T(8,128)}, u32[]{:S(2)}) copy-start(f32[1,64,896]{2,1,0:T(8,128)} %param.19) | copy-start | bytes 688132
  28.2 4.0 %copy-start.7 = (f32[64,384]{1,0:T(8,128)S(1)}, f32[64,384]{1,0:T(8,128)}, u32[]{:S(2)}) copy-start(f32[64,384]{1,0:T(8,128)} %grp_coupling.1) | copy-start | bytes 294916

commit v3 on v2

--- a/solution.py
+++ b/solution.py
@@ -272,22 +272,18 @@
 
 
 def couple_kernel(
-    grp_count,
-    dev_count,
-    levels,
     near_partner_in,
     far_partner_in,
     own,
     twin,
     beside,
     inv,
+    root_value,
     coupling,
+    transfer,
+    basis,
     near,
-    grp_transfer,
-    dev_transfer,
-    base,
-    terms,
-    paths,
+    product,
     window,
     near_partner,
     far_partner,
@@ -321,16 +317,6 @@
         return window[(index & 1) ^ parity, first + lax.shift_right_logical(index, 1)]
 
     low16 = low_half(NRHS)
-    edges = []
-    for n in range(levels - 1):
-        pair, _, odd_node = own_tile(n, grp_count, dev_count, grp_transfer, dev_transfer)
-        edge = jnp.where(odd_node, swap_halves(pair), pair)
-        edges.append(jnp.where(low_half(RANK), edge, 0.0))
-    path = None
-    for n, edge in enumerate(edges):
-        path = edge if path is None else mm(path, jnp.concatenate([edge, edge], axis=0))
-        paths[:, RANK * n : RANK * (n + 1)] = path[:, 0:RANK]
-
     for copy in copies:
         copy.wait()
     coupled = []
@@ -344,9 +330,8 @@
                 values.append(pick(firsts[level + 1], index, side))
             xhat = jnp.where(low16, values[0], values[1])
             coupled.append(mm_t(xhat, spread_pair(coupling[:, pair_lanes(node // 2)])))
-    for p, y in enumerate(coupled):
-        terms[:, pair_lanes(p)] = mm(y, spread_pair(inv[pair_rows(p), :]))
-
+    terms = [mm(y, spread_pair(inv[pair_rows(p), :])) for p, y in enumerate(coupled)]
+    nears = []
     for p in range(LEAF_DEV // 2):
         lanes = slice(PAIR * p, PAIR * (p + 1))
         own_points = own[:, lanes]
@@ -364,7 +349,23 @@
             axis=0,
         )
         near_out = mm_t(jnp.concatenate(inputs, axis=0), weights)
-        base[:, lanes] = jnp.where(low16, near_out[0:NRHS], near_out[NRHS:])
+        nears.append(jnp.where(low16, near_out[0:NRHS], near_out[NRHS:]))
+    state = [twice(root_value[...])]
+    for level in reversed(range(LOC)):
+        m = LEAF_DEV >> level
+        tile = OFFSETS[level] // 2
+        state = [
+            terms[tile + p]
+            + mm_t(
+                state[p // 2],
+                (stack_high if p % 2 else stack_low)(transfer[:, pair_lanes(tile + p)]),
+            )
+            for p in range(m // 2)
+        ]
+    for p in range(LEAF_DEV // 2):
+        product[:, pair_lanes(p)] = nears[p] + mm_t(
+            state[p], spread_pair(basis[:, pair_lanes(p)])
+        )
 
 
 def twice(x):
@@ -379,18 +380,14 @@
     record_spans,
     grp_transfer,
     grp_coupling,
+    dev_transfer,
     dev_coupling,
-    base,
-    terms,
-    paths,
-    transfer,
-    basis,
     *refs,
 ):
     blocks = refs[: 2**bits]
     refs = refs[2**bits :]
     earlier = refs[: len(record_spans)]
-    product, root, stack, records, d, a, m, inv = refs[len(record_spans) :]
+    value_out, root, stack, records, d, a, m, inv = refs[len(record_spans) :]
     level = 0
     for ref, span in zip(earlier, record_spans):
         for r in range(2 * span):
@@ -400,6 +397,16 @@
         blocks, lax.axis_index("grp"), start, bits, grp_count, grp_transfer, stack, records, level
     )
     levels = level + bits
+    edges = []
+    for n in range(levels - 1):
+        pair, _, odd_node = own_tile(n, grp_count, dev_count, grp_transfer, dev_transfer)
+        edge = jnp.where(odd_node, swap_halves(pair), pair)
+        edges.append(jnp.where(low_half(RANK), edge, 0.0))
+    path = None
+    paths = []
+    for n, edge in enumerate(edges):
+        path = edge if path is None else mm(path, jnp.concatenate([edge, edge], axis=0))
+        paths.append(path[:, 0:RANK])
     for n in range(levels):
         d[pair_rows(n), :] = jnp.concatenate(
             [records[2 * n, 0:RANK, 0:RANK], records[2 * n + 1, 0:RANK, 0:RANK]], axis=1
@@ -426,27 +433,11 @@
     value = values[0]
     if levels > 1:
         upper = values[1:]
-        edges = paths[...]
         if len(upper) % 2:
             upper.append(jnp.zeros_like(value))
-            edges = jnp.concatenate([edges, jnp.zeros_like(edges[:, 0:RANK])], axis=1)
-        value = value + mm_t(jnp.concatenate(upper, axis=1), edges)
-    state = [twice(value)]
-    for level in reversed(range(LOC)):
-        m = LEAF_DEV >> level
-        tile = OFFSETS[level] // 2
-        state = [
-            terms[:, pair_lanes(tile + p)]
-            + mm_t(
-                state[p // 2],
-                (stack_high if p % 2 else stack_low)(transfer[:, pair_lanes(tile + p)]),
-            )
-            for p in range(m // 2)
-        ]
-    for p in range(LEAF_DEV // 2):
-        product[:, pair_lanes(p)] = base[:, pair_lanes(p)] + mm_t(
-            state[p], spread_pair(basis[:, pair_lanes(p)])
-        )
+            paths.append(jnp.zeros_like(paths[0]))
+        value = value + mm_t(jnp.concatenate(upper, axis=1), jnp.concatenate(paths, axis=1))
+    value_out[...] = value
 
 
 def vmem(count):
@@ -574,44 +565,11 @@
     both = ("grp", "dev")
     ends = grp_count * dev_count - 1
     twin = lax.ppermute(packed, both, [(i, i ^ 1) for i in range(ends + 1)])
-    beside = lax.ppermute(
-        packed, both, [(i, ((i + 1) ^ 1) - 1) for i in range(1, ends)]
-    )
+    pairs = [(i, i + 1) for i in range(1, ends, 2)]
+    beside = lax.ppermute(packed, both, pairs + [(j, i) for i, j in pairs])
 
     grp_chunks = chunks(grp_count.bit_length() - 1, 2)
     levels = sum(spans) + grp_count.bit_length() - 1
-    window_tiles = 3 * (POINT_SPAN + NODE_SPAN) // PAIR
-    base, terms, paths = pl.pallas_call(
-        functools.partial(couple_kernel, grp_count, dev_count, levels),
-        out_shape=[
-            f32(NRHS, POINT_SPAN),
-            f32(NRHS, NODE_SPAN),
-            f32(RANK, RANK * (levels - 1)),
-        ],
-        in_specs=hbm(2) + vmem(8),
-        out_specs=vmem(3),
-        scratch_shapes=[
-            pltpu.VMEM((2, window_tiles, NRHS, PAIR), jnp.float32),
-            pltpu.SMEM(near_partner.shape, jnp.int32),
-            pltpu.SMEM(far_partner.shape, jnp.int32),
-            pltpu.SemaphoreType.DMA((2,)),
-        ],
-        compiler_params=params(24),
-        cost_estimate=micros(4),
-        name="couple",
-    )(
-        in_hbm(near_partner),
-        in_hbm(far_partner),
-        packed,
-        twin,
-        beside,
-        inv,
-        local_coupling,
-        near_blocks,
-        grp_transfer,
-        dev_transfer,
-    )
-
     for start, bits in grp_chunks[:-1]:
         blocks = exchange(top, "grp", start, bits)
         top, record = climb_call(blocks, "grp", start, bits, grp_count, grp_transfer)
@@ -620,10 +578,10 @@
     start, bits = grp_chunks[-1]
     blocks = exchange(top, "grp", start, bits)
     batch = 8 * ((levels + 1 + 7) // 8)
-    return pl.pallas_call(
+    value, root = pl.pallas_call(
         functools.partial(top_kernel, grp_count, dev_count, start, bits, tuple(spans)),
-        out_shape=[f32(NRHS, POINT_SPAN), f32(RANK, RANK)],
-        in_specs=vmem(8 + len(blocks) + len(records)),
+        out_shape=[f32(NRHS, RANK), f32(RANK, RANK)],
+        in_specs=vmem(4 + len(blocks) + len(records)),
         out_specs=vmem(2),
         scratch_shapes=[
             pltpu.VMEM((2**bits, ROWS, PAIR), jnp.float32),
@@ -634,20 +592,39 @@
             pltpu.VMEM((batch * RANK, PAIR), jnp.float32),
         ],
         compiler_params=params(24),
-        cost_estimate=micros(9),
+        cost_estimate=micros(7),
         name="top",
+    )(grp_transfer, grp_coupling, dev_transfer, dev_coupling, *blocks, *records)
+
+    window_tiles = 3 * (POINT_SPAN + NODE_SPAN) // PAIR
+    product = pl.pallas_call(
+        couple_kernel,
+        out_shape=f32(NRHS, POINT_SPAN),
+        in_specs=hbm(2) + vmem(9),
+        out_specs=vmem(1)[0],
+        scratch_shapes=[
+            pltpu.VMEM((2, window_tiles, NRHS, PAIR), jnp.float32),
+            pltpu.SMEM(near_partner.shape, jnp.int32),
+            pltpu.SMEM(far_partner.shape, jnp.int32),
+            pltpu.SemaphoreType.DMA((2,)),
+        ],
+        compiler_params=params(24),
+        cost_estimate=micros(3),
+        name="couple",
     )(
-        grp_transfer,
-        grp_coupling,
-        dev_coupling,
-        base,
-        terms,
-        paths,
+        in_hbm(near_partner),
+        in_hbm(far_partner),
+        packed,
+        twin,
+        beside,
+        inv,
+        value,
+        local_coupling,
         local_transfer,
         leaf_basis,
-        *blocks,
-        *records,
-    )
+        near_blocks,
+    )
+    return product, root
 
 
 def solution(mesh):

time: 40.7 us -> 38.2 us (0.939)
  the two profiles are of different devices: /device:TPU:0 before, /device:TPU:4 now
where the time goes in v3:
time: 38.2 us; the launch traced here: 38.1 us
  Pallas kernels  21 us (55%)
  starting transfers between devices  14.7 us (38%)
  waiting for transfers between devices  1.24 us (3%)
  between operations  0.99 us (3%)
    ppermute x7, starting transfers between devices, exchange(): lax.ppermute(block, axis, [(i, i ^ k << start) for i in range(count)])  8.08 us
    pallas_call x1, Pallas kernels, shards(): pl.pallas_call(functools.partial(top_kernel, grp_count, dev_count, start,...  7.01 us
    ppermute x1, starting transfers between devices, shards(): beside = lax.ppermute(packed, both, pairs + [(j, i) for i, j in pairs])  6.66 us
    pallas_call x1, Pallas kernels, local_call(): pl.pallas_call(local_kernel, out_shape=[f32(BATCH * RANK, PAIR), f32(NRHS...  6 us
    pallas_call x1, Pallas kernels, shards(): pl.pallas_call(couple_kernel, out_shape=f32(NRHS, POINT_SPAN), in_specs=h...  3.59 us
    pallas_call x1, Pallas kernels, shards(): pl.pallas_call(gram_kernel, out_shape=[f32(BATCH * RANK, PAIR), f32(NRHS,...  3.28 us
    ppermute x7, waiting for transfers between devices, exchange(): lax.ppermute(block, axis, [(i, i ^ k << start) for i in range(count)])  1.23 us
    pallas_call x2, Pallas kernels, climb_call(): pl.pallas_call(functools.partial(climb_kernel, axis, start, bits, count),...  1.16 us
  transfers between devices with their start and end apart: 9, of which 1 were waited for; matrix products, arithmetic and copies ran while one was open for 0% of the time, Pallas kernels for 34%

profile of v3, /device:TPU:4, one launch (start us, length us, event | category | flops | bytes accessed | tf_op | source)
XLA Modules:
  0.0 38.1 jit_solution(5482406325954701854)
XLA Ops:
  0.6 0.0 copy-start.4
  0.6 3.3 %gram.1 = (f32[1024,128]{1,0:T(8,128)S(1)}, f32[16,1920]{1,0:T(8,128)S(1)}, f32[80,64]{1,0:T(8,128)S(1)}) custom-call(f32[64,1024]{1,0:T(8,128)} %basis.1, f32[16,1024]{1,0:T(8,128)} %rhs.1, f32[64,1920]{1,0:T(8,128)} %transfer.1), custom_call_target="tpu_custom_call" | custom-call | flops 4000000000 | bytes 1048576 | tf_op jit(solution)/shard_map/gram/pallas_call | solution.py:531
  3.9 0.1 collective-permute-start
  4.0 1.2 %collective-permute-done.refs_1_ = f32[80,64]{1,0:T(8,128)S(1)} collective-permute-done((f32[80,64]{1,0:T(8,128)S(1)}, f32[80,64]{1,0:T(8,128)S(1)}, u32[]{:S(2)}, u32[]{:S(2)}) %collective-permute-start) | collective-permute-done | bytes 20512 | tf_op jit(solution)/shard_map/ppermute | solution.py:470
  5.2 0.4 %climb.2 = (f32[80,64]{1,0:T(8,128)S(1)}, f32[2,80,128]{2,1,0:T(8,128)S(1)}) custom-call(f32[64,896]{1,0:T(8,128)S(1)} %bitcast.2, f32[80,64]{1,0:T(8,128)S(1)} %get-tuple-element.14.refs_0_, f32[80,64]{1,0:T(8,128)S(1)} %collective-permute-done.refs_1_), custom_call_target="tpu_custom_call" | custom-call | flops 1000000000 | bytes 1048576 | tf_op jit(solution)/shard_map/climb/pallas_call | solution.py:487
  5.6 1.6 %collective-permute-start.1 = (f32[80,64]{1,0:T(8,128)S(1)}, f32[80,64]{1,0:T(8,128)S(1)}, u32[]{:S(2)}, u32[]{:S(2)}) collective-permute-start(f32[80,64]{1,0:T(8,128)S(1)} %get-tuple-element.15.refs_0_), channel_id=1, source_target_pairs={{0,2},{1,3},{2,0},{3,1},{4,6},{5,7},{6,4},{7,5},{8,10},{9,11},{10,... | collective-permute-start | bytes 61448 | tf_op jit(solution)/shard_map/ppermute | solution.py:470
  7.2 2.6 %collective-permute-start.2 = (f32[80,64]{1,0:T(8,128)S(1)}, f32[80,64]{1,0:T(8,128)S(1)}, u32[]{:S(2)}, u32[]{:S(2)}) collective-permute-start(f32[80,64]{1,0:T(8,128)S(1)} %get-tuple-element.15.refs_0_), channel_id=1, source_target_pairs={{0,4},{1,5},{2,6},{3,7},{4,0},{5,1},{6,2},{7,3},{8,12},{9,13},{10,... | collective-permute-start | bytes 61448 | tf_op jit(solution)/shard_map/ppermute | solution.py:470
  9.8 0.2 collective-permute-start.3
  10.1 6.0 %local_factors.1 = (f32[1024,128]{1,0:T(8,128)S(1)}, f32[16,2944]{1,0:T(8,128)S(1)}) custom-call(f32[1024,128]{1,0:T(8,128)S(1)} %get-tuple-element.16.gram, f32[16,1920]{1,0:T(8,128)S(1)} %get-tuple-element.17.z, f32[16,1024]{1,0:T(8,128)S(1)} %copy-done.8, f32[2,80,128]{2,1,0:T(8,128)S(1)} %get-tuple-element.18.after.refs_4_), custom_call_target="tpu_custom_call" | custom-call | flops 8000000000 | bytes 1048576 | tf_op jit(solution)/shard_map/local_factors/pallas_call | solution.py:501
  16.1 0.0 collective-permute-done.1.refs_1_
  16.1 0.0 collective-permute-done.2.refs_2_
  16.1 0.0 collective-permute-done.3.refs_3_
  16.1 0.0 copy-start.5
  16.1 0.0 copy-start.6
  16.1 0.0 copy-start.7
  16.1 0.8 %climb.3 = (f32[80,64]{1,0:T(8,128)S(1)}, f32[4,80,128]{2,1,0:T(8,128)S(1)}, f32[16,2944]{1,0:T(8,128)S(1)}) custom-call(f32[64,896]{1,0:T(8,128)S(1)} %bitcast.3, f32[80,64]{1,0:T(8,128)S(1)} %get-tuple-element.15.refs_0_, f32[80,64]{1,0:T(8,128)S(1)} %collective-permute-done.1.refs_1_, ...), custom_call_target="tpu_custom_call", output_to_operand_aliasing={{2}: (5, {})} | custom-call | flops 1000000000 | bytes 1048576 | tf_op jit(solution)/shard_map/climb/pallas_call | solution.py:487
  16.9 1.5 %collective-permute-start.6 = (f32[80,64]{1,0:T(8,128)S(1)}, f32[80,64]{1,0:T(8,128)S(1)}, u32[]{:S(2)}, u32[]{:S(2)}) collective-permute-start(f32[80,64]{1,0:T(8,128)S(1)} %get-tuple-element.22.refs_0_), channel_id=1, source_target_pairs={{0,8},{8,0},{16,24},{24,16},{1,9},{9,1},{17,25},{25,17},{2,10},{10... | collective-permute-start | bytes 61448 | tf_op jit(solution)/shard_map/ppermute | solution.py:470
  18.5 0.5 %collective-permute-start.7 = (f32[80,64]{1,0:T(8,128)S(1)}, f32[80,64]{1,0:T(8,128)S(1)}, u32[]{:S(2)}, u32[]{:S(2)}) collective-permute-start(f32[80,64]{1,0:T(8,128)S(1)} %get-tuple-element.22.refs_0_), channel_id=1, source_target_pairs={{0,16},{8,24},{16,0},{24,8},{1,17},{9,25},{17,1},{25,9},{2,18},{10... | collective-permute-start | bytes 61448 | tf_op jit(solution)/shard_map/ppermute | solution.py:470
  19.0 1.5 %collective-permute-start.8 = (f32[80,64]{1,0:T(8,128)S(1)}, f32[80,64]{1,0:T(8,128)S(1)}, u32[]{:S(2)}, u32[]{:S(2)}) collective-permute-start(f32[80,64]{1,0:T(8,128)S(1)} %get-tuple-element.22.refs_0_), channel_id=1, source_target_pairs={{0,24},{8,16},{16,8},{24,0},{1,25},{9,17},{17,9},{25,1},{2,26},{10... | collective-permute-start | bytes 61448 | tf_op jit(solution)/shard_map/ppermute | solution.py:470
  20.5 0.0 collective-permute-start.4
  20.5 6.7 %collective-permute-start.5 = (f32[16,2944]{1,0:T(8,128)S(1)}, f32[16,2944]{1,0:T(8,128)S(1)}, u32[]{:S(2)}, u32[]{:S(2)}) collective-permute-start(f32[16,2944]{1,0:T(8,128)S(1)} %get-tuple-element.20.own), channel_id=1, source_target_pairs={{1,2},{3,4},{5,6},{7,8},{9,10},{11,12},{13,14},{15,16},{17,18},{19... | collective-permute-start | bytes 565256 | tf_op jit(solution)/shard_map/ppermute | solution.py:569
  27.2 0.0 collective-permute-done.6.refs_1_
  27.2 0.0 collective-permute-done.7.refs_2_
  27.2 0.0 collective-permute-done.8.refs_3_
  27.2 0.0 copy-start
  27.2 0.0 copy-start.1
  27.2 0.0 copy-start.2
  27.2 0.0 copy-start.3
  27.3 7.0 %top.1 = (f32[16,64]{1,0:T(8,128)S(1)}, f32[64,64]{1,0:T(8,128)}) custom-call(f32[64,384]{1,0:T(8,128)S(1)} %copy-done.6, f32[64,384]{1,0:T(8,128)S(1)} %copy-done.7, f32[64,896]{1,0:T(8,128)S(1)} %bitcast.4, f32[64,896]{1,0:T(8,128)S(1)} %bitcast.5, f32[80,64]{1,0:T(8,128)S(1)} %get-tuple-element.22.refs_0_, f32[80,64]{1,0:T(8,128)S(1)} %collective-permute-done.6.refs_1_, ...), custom_call_target="tpu_custom_call" | custom-call | flops 7000000000 | bytes 1048576 | tf_op jit(solution)/shard_map/top/pallas_call | solution.py:581
  34.3 0.0 collective-permute-done.4.twin
  34.3 0.0 collective-permute-done.5.beside
  34.3 3.6 %couple.1 = f32[16,1024]{1,0:T(8,128)} custom-call(s32[16]{0:T(128)} %near_partner_in.1, s32[1,30]{1,0:T(1,128)} %far_partner_in.1, f32[16,2944]{1,0:T(8,128)S(1)} %get-tuple-element.20.own, f32[16,2944]{1,0:T(8,128)S(1)} %collective-permute-done.4.twin, f32[16,2944]{1,0:T(8,128)S(1)} %collective-permute-done.5.beside, ...), custom_call_target="tpu_custom_call" | custom-call | flops 3000000000 | bytes 1048576 | tf_op jit(solution)/shard_map/couple/pallas_call | solution.py:600
  (10 shorter events, 0.0 us)
Async XLA Ops:
  0.6 4.6 %copy-start.4 = (f32[1,64,896]{2,1,0:T(8,128)S(1)}, f32[1,64,896]{2,1,0:T(8,128)}, u32[]{:S(2)}) copy-start(f32[1,64,896]{2,1,0:T(8,128)} %param.18) | copy-start | bytes 688132
  3.9 1.3 %collective-permute-start = (f32[80,64]{1,0:T(8,128)S(1)}, f32[80,64]{1,0:T(8,128)S(1)}, u32[]{:S(2)}, u32[]{:S(2)}) collective-permute-start(f32[80,64]{1,0:T(8,128)S(1)} %get-tuple-element.14.refs_0_), channel_id=1, source_target_pairs={{0,1},{1,0},{2,3},{3,2},{4,5},{5,4},{6,7},{7,6},{8,9},{9,8},{10,11... | collective-permute-start | bytes 61448 | tf_op jit(solution)/shard_map/ppermute | solution.py:470
  5.2 4.9 %copy-start.8 = (f32[16,1024]{1,0:T(8,128)S(1)}, f32[16,1024]{1,0:T(8,128)}, u32[]{:S(2)}) copy-start(f32[16,1024]{1,0:T(8,128)} %rhs.1) | copy-start | bytes 196612
  5.6 10.5 %collective-permute-start.1 = (f32[80,64]{1,0:T(8,128)S(1)}, f32[80,64]{1,0:T(8,128)S(1)}, u32[]{:S(2)}, u32[]{:S(2)}) collective-permute-start(f32[80,64]{1,0:T(8,128)S(1)} %get-tuple-element.15.refs_0_), channel_id=1, source_target_pairs={{0,2},{1,3},{2,0},{3,1},{4,6},{5,7},{6,4},{7,5},{8,10},{9,11},{10,... | collective-permute-start | bytes 61448 | tf_op jit(solution)/shard_map/ppermute | solution.py:470
  7.2 8.8 %collective-permute-start.2 = (f32[80,64]{1,0:T(8,128)S(1)}, f32[80,64]{1,0:T(8,128)S(1)}, u32[]{:S(2)}, u32[]{:S(2)}) collective-permute-start(f32[80,64]{1,0:T(8,128)S(1)} %get-tuple-element.15.refs_0_), channel_id=1, source_target_pairs={{0,4},{1,5},{2,6},{3,7},{4,0},{5,1},{6,2},{7,3},{8,12},{9,13},{10,... | collective-permute-start | bytes 61448 | tf_op jit(solution)/shard_map/ppermute | solution.py:470
  9.8 6.3 %collective-permute-start.3 = (f32[80,64]{1,0:T(8,128)S(1)}, f32[80,64]{1,0:T(8,128)S(1)}, u32[]{:S(2)}, u32[]{:S(2)}) collective-permute-start(f32[80,64]{1,0:T(8,128)S(1)} %get-tuple-element.15.refs_0_), channel_id=1, source_target_pairs={{0,6},{1,7},{2,4},{3,5},{4,2},{5,3},{6,0},{7,1},{8,14},{9,15},{10,... | collective-permute-start | bytes 61448 | tf_op jit(solution)/shard_map/ppermute | solution.py:470
  16.1 11.1 %copy-start.5 = (f32[1,64,896]{2,1,0:T(8,128)S(1)}, f32[1,64,896]{2,1,0:T(8,128)}, u32[]{:S(2)}) copy-start(f32[1,64,896]{2,1,0:T(8,128)} %param.19) | copy-start | bytes 688132
  16.1 11.1 %copy-start.6 = (f32[64,384]{1,0:T(8,128)S(1)}, f32[64,384]{1,0:T(8,128)}, u32[]{:S(2)}) copy-start(f32[64,384]{1,0:T(8,128)} %grp_transfer.1) | copy-start | bytes 294916
  16.1 11.1 %copy-start.7 = (f32[64,384]{1,0:T(8,128)S(1)}, f32[64,384]{1,0:T(8,128)}, u32[]{:S(2)}) copy-start(f32[64,384]{1,0:T(8,128)} %grp_coupling.1) | copy-start | bytes 294916
  16.9 10.2 %collective-permute-start.6 = (f32[80,64]{1,0:T(8,128)S(1)}, f32[80,64]{1,0:T(8,128)S(1)}, u32[]{:S(2)}, u32[]{:S(2)}) collective-permute-start(f32[80,64]{1,0:T(8,128)S(1)} %get-tuple-element.22.refs_0_), channel_id=1, source_target_pairs={{0,8},{8,0},{16,24},{24,16},{1,9},{9,1},{17,25},{25,17},{2,10},{10... | collective-permute-start | bytes 61448 | tf_op jit(solution)/shard_map/ppermute | solution.py:470
  18.5 8.7 %collective-permute-start.7 = (f32[80,64]{1,0:T(8,128)S(1)}, f32[80,64]{1,0:T(8,128)S(1)}, u32[]{:S(2)}, u32[]{:S(2)}) collective-permute-start(f32[80,64]{1,0:T(8,128)S(1)} %get-tuple-element.22.refs_0_), channel_id=1, source_target_pairs={{0,16},{8,24},{16,0},{24,8},{1,17},{9,25},{17,1},{25,9},{2,18},{10... | collective-permute-start | bytes 61448 | tf_op jit(solution)/shard_map/ppermute | solution.py:470
  19.0 8.2 %collective-permute-start.8 = (f32[80,64]{1,0:T(8,128)S(1)}, f32[80,64]{1,0:T(8,128)S(1)}, u32[]{:S(2)}, u32[]{:S(2)}) collective-permute-start(f32[80,64]{1,0:T(8,128)S(1)} %get-tuple-element.22.refs_0_), channel_id=1, source_target_pairs={{0,24},{8,16},{16,8},{24,0},{1,25},{9,17},{17,9},{25,1},{2,26},{10... | collective-permute-start | bytes 61448 | tf_op jit(solution)/shard_map/ppermute | solution.py:470
  20.5 13.8 %collective-permute-start.4 = (f32[16,2944]{1,0:T(8,128)S(1)}, f32[16,2944]{1,0:T(8,128)S(1)}, u32[]{:S(2)}, u32[]{:S(2)}) collective-permute-start(f32[16,2944]{1,0:T(8,128)S(1)} %get-tuple-element.20.own), channel_id=1, source_target_pairs={{0,1},{1,0},{2,3},{3,2},{4,5},{5,4},{6,7},{7,6},{8,9},{9,8},{10,11... | collective-permute-start | bytes 565256 | tf_op jit(solution)/shard_map/ppermute | solution.py:567
  20.5 13.8 %collective-permute-start.5 = (f32[16,2944]{1,0:T(8,128)S(1)}, f32[16,2944]{1,0:T(8,128)S(1)}, u32[]{:S(2)}, u32[]{:S(2)}) collective-permute-start(f32[16,2944]{1,0:T(8,128)S(1)} %get-tuple-element.20.own), channel_id=1, source_target_pairs={{1,2},{3,4},{5,6},{7,8},{9,10},{11,12},{13,14},{15,16},{17,18},{19... | collective-permute-start | bytes 565256 | tf_op jit(solution)/shard_map/ppermute | solution.py:569
  27.2 7.1 %copy-start = (f32[64,2048]{1,0:T(8,128)S(1)}, f32[64,2048]{1,0:T(8,128)}, u32[]{:S(2)}) copy-start(f32[64,2048]{1,0:T(8,128)} %near.1) | copy-start | bytes 1572868
  27.2 7.1 %copy-start.1 = (f32[64,1920]{1,0:T(8,128)S(1)}, f32[64,1920]{1,0:T(8,128)}, u32[]{:S(2)}) copy-start(f32[64,1920]{1,0:T(8,128)} %transfer.1) | copy-start | bytes 1474564
  27.2 7.1 %copy-start.2 = (f32[64,1920]{1,0:T(8,128)S(1)}, f32[64,1920]{1,0:T(8,128)}, u32[]{:S(2)}) copy-start(f32[64,1920]{1,0:T(8,128)} %coupling.1) | copy-start | bytes 1474564
  27.2 7.1 %copy-start.3 = (f32[64,1024]{1,0:T(8,128)S(1)}, f32[64,1024]{1,0:T(8,128)}, u32[]{:S(2)}) copy-start(f32[64,1024]{1,0:T(8,128)} %basis.1) | copy-start | bytes 786436

commit v4 on v3

--- a/solution.py
+++ b/solution.py
@@ -200,13 +200,23 @@
     return slice(PAIR * p, PAIR * (p + 1))
 
 
-def local_kernel(gram, z, rhs, after, inv, packed, a, m):
+def local_kernel(
+    gram, z, rhs, after, near_in, far_in, inv, packed, near_partner, far_partner, a, m, sems
+):
+    copies = [
+        pltpu.make_async_copy(near_in, near_partner, sems.at[0]),
+        pltpu.make_async_copy(far_in, far_partner, sems.at[1]),
+    ]
+    for copy in copies:
+        copy.start()
     invert_pairs(gram, a, m, inv, BATCH)
     packed[:, 0:POINT_SPAN] = rhs[...]
     for p in range(PAIRS):
         packed[:, POINT_SPAN + PAIR * p : POINT_SPAN + PAIR * (p + 1)] = mm_t(
             z[:, pair_lanes(p)], spread_pair(inv[pair_rows(p), :])
         )
+    for copy in copies:
+        copy.wait()
 
 
 def merge(nodes, tile, transfer):
@@ -309,12 +319,12 @@
             first = slot + span if shift is None else slot + 2 * span * shift
             for t in range(span):
                 tile = source[:, PAIR * (start + t) : PAIR * (start + t + 1)]
-                window[0, first + t] = tile
-                window[1, first + t] = swap_halves(tile)
+                window[first + t] = tile
         slot += 3 * span
 
     def pick(first, index, parity):
-        return window[(index & 1) ^ parity, first + lax.shift_right_logical(index, 1)]
+        tile = window[first + lax.shift_right_logical(index, 1)]
+        return jnp.where((index & 1) == parity, tile, swap_halves(tile))
 
     low16 = low_half(NRHS)
     for copy in copies:
@@ -330,17 +340,22 @@
                 values.append(pick(firsts[level + 1], index, side))
             xhat = jnp.where(low16, values[0], values[1])
             coupled.append(mm_t(xhat, spread_pair(coupling[:, pair_lanes(node // 2)])))
-    terms = [mm(y, spread_pair(inv[pair_rows(p), :])) for p, y in enumerate(coupled)]
-    nears = []
-    for p in range(LEAF_DEV // 2):
-        lanes = slice(PAIR * p, PAIR * (p + 1))
-        own_points = own[:, lanes]
+
+    def terms(level):
+        tile = OFFSETS[level] // 2
+        return [
+            mm(coupled[p], spread_pair(inv[pair_rows(p), :]))
+            for p in range(tile, tile + (LEAF_DEV >> level + 1))
+        ]
+
+    def near_field(p):
+        own_points = own[:, pair_lanes(p)]
         swapped = swap_halves(own_points)
         inputs = []
         for side in range(2):
             index = near_partner[2 * p + side] - (place - 1) * LEAF_DEV
-            value = pick(0, index, 1)
-            inputs.append(jnp.where(low16, swapped if side else own_points, value))
+            partner = pick(0, index, 1)
+            inputs.append(jnp.where(low16, swapped if side else own_points, partner))
         weights = jnp.concatenate(
             [
                 near[:, 2 * PAIR * p : 2 * PAIR * p + PAIR],
@@ -348,20 +363,26 @@
             ],
             axis=0,
         )
-        near_out = mm_t(jnp.concatenate(inputs, axis=0), weights)
-        nears.append(jnp.where(low16, near_out[0:NRHS], near_out[NRHS:]))
+        out = mm_t(jnp.concatenate(inputs, axis=0), weights)
+        return jnp.where(low16, out[0:NRHS], out[NRHS:])
+
+    nears = []
     state = [twice(root_value[...])]
+    ready = terms(LOC - 1)
     for level in reversed(range(LOC)):
-        m = LEAF_DEV >> level
         tile = OFFSETS[level] // 2
-        state = [
-            terms[tile + p]
-            + mm_t(
+        pairs = LEAF_DEV >> level + 1
+        swept = [
+            mm_t(
                 state[p // 2],
                 (stack_high if p % 2 else stack_low)(transfer[:, pair_lanes(tile + p)]),
             )
-            for p in range(m // 2)
+            for p in range(pairs)
         ]
+        state = [term + value for term, value in zip(ready, swept)]
+        if level:
+            ready = terms(level - 1)
+        nears += [near_field(p) for p in range(2 * len(nears) // 2, 2 * (LOC - level))]
     for p in range(LEAF_DEV // 2):
         product[:, pair_lanes(p)] = nears[p] + mm_t(
             state[p], spread_pair(basis[:, pair_lanes(p)])
@@ -497,20 +518,26 @@
     )(transfer, *blocks, *carried)
 
 
-def local_call(gram, z, rhs, after):
+def local_call(gram, z, rhs, after, near_partner, far_partner):
     return pl.pallas_call(
         local_kernel,
-        out_shape=[f32(BATCH * RANK, PAIR), f32(NRHS, POINT_SPAN + NODE_SPAN)],
-        in_specs=vmem(3) + [pl.BlockSpec(memory_space=pl.ANY)],
-        out_specs=vmem(2),
+        out_shape=[
+            f32(BATCH * RANK, PAIR),
+            f32(NRHS, POINT_SPAN + NODE_SPAN),
+            jax.ShapeDtypeStruct(near_partner.shape, jnp.int32),
+            jax.ShapeDtypeStruct(far_partner.shape, jnp.int32),
+        ],
+        in_specs=vmem(3) + [pl.BlockSpec(memory_space=pl.ANY)] + hbm(2),
+        out_specs=vmem(4),
         scratch_shapes=[
             pltpu.VMEM((RANK, RANK, LANES), jnp.float32),
             pltpu.VMEM((RANK, RANK, LANES), jnp.float32),
+            pltpu.SemaphoreType.DMA((2,)),
         ],
         compiler_params=params(24),
         cost_estimate=micros(8),
         name="local_factors",
-    )(gram, z, rhs, after)
+    )(gram, z, rhs, after, in_hbm(near_partner), in_hbm(far_partner))
 
 
 def shards(
@@ -553,7 +580,9 @@
     for start, bits in chunks(dev_count.bit_length() - 1, 1):
         blocks = exchange(top, "dev", start, bits)
         if records and inv is None:
-            inv, packed = local_call(gram, z, rhs, records[0])
+            inv, packed, near_partner, far_partner = local_call(
+                gram, z, rhs, records[0], near_partner, far_partner
+            )
             carried = (packed,)
         top, record, *carried = climb_call(
             blocks, "dev", start, bits, dev_count, dev_transfer, carried
@@ -600,10 +629,10 @@
     product = pl.pallas_call(
         couple_kernel,
         out_shape=f32(NRHS, POINT_SPAN),
-        in_specs=hbm(2) + vmem(9),
+        in_specs=[pl.BlockSpec(memory_space=pl.ANY)] * 2 + vmem(9),
         out_specs=vmem(1)[0],
         scratch_shapes=[
-            pltpu.VMEM((2, window_tiles, NRHS, PAIR), jnp.float32),
+            pltpu.VMEM((window_tiles, NRHS, PAIR), jnp.float32),
             pltpu.SMEM(near_partner.shape, jnp.int32),
             pltpu.SMEM(far_partner.shape, jnp.int32),
             pltpu.SemaphoreType.DMA((2,)),
@@ -612,8 +641,8 @@
         cost_estimate=micros(3),
         name="couple",
     )(
-        in_hbm(near_partner),
-        in_hbm(far_partner),
+        near_partner,
+        far_partner,
         packed,
         twin,
         beside,

time: 38.2 us -> 38 us (level)
  no operation moved by 1% of the time
where the time goes in v4:
time: 38 us; the launch traced here: 37.9 us
  Pallas kernels  20.8 us (55%)
  starting transfers between devices  14.7 us (39%)
  waiting for transfers between devices  1.23 us (3%)
  between operations  1 us (3%)
    ppermute x7, starting transfers between devices, exchange(): lax.ppermute(block, axis, [(i, i ^ k << start) for i in range(count)])  8.08 us
    pallas_call x1, Pallas kernels, shards(): pl.pallas_call(functools.partial(top_kernel, grp_count, dev_count, start,...  7.01 us
    ppermute x1, starting transfers between devices, shards(): beside = lax.ppermute(packed, both, pairs + [(j, i) for i, j in pairs])  6.66 us
    pallas_call x1, Pallas kernels, local_call(): pl.pallas_call(local_kernel, out_shape=[f32(BATCH * RANK, PAIR), f32(NRHS...  6.04 us
    pallas_call x1, Pallas kernels, shards(): pl.pallas_call(couple_kernel, out_shape=f32(NRHS, POINT_SPAN), in_specs=[...  3.33 us
    pallas_call x1, Pallas kernels, shards(): pl.pallas_call(gram_kernel, out_shape=[f32(BATCH * RANK, PAIR), f32(NRHS,...  3.28 us
    ppermute x7, waiting for transfers between devices, exchange(): lax.ppermute(block, axis, [(i, i ^ k << start) for i in range(count)])  1.22 us
    pallas_call x2, Pallas kernels, climb_call(): pl.pallas_call(functools.partial(climb_kernel, axis, start, bits, count),...  1.17 us
  transfers between devices with their start and end apart: 9, of which 1 were waited for; matrix products, arithmetic and copies ran while one was open for 0% of the time, Pallas kernels for 34%

profile of v4, /device:TPU:4, one launch (start us, length us, event | category | flops | bytes accessed | tf_op | source)
XLA Modules:
  0.0 37.9 jit_solution(18010273022230358165)
XLA Ops:
  0.6 0.0 copy-start.4
  0.6 3.3 %gram.1 = (f32[1024,128]{1,0:T(8,128)S(1)}, f32[16,1920]{1,0:T(8,128)S(1)}, f32[80,64]{1,0:T(8,128)S(1)}) custom-call(f32[64,1024]{1,0:T(8,128)} %basis.1, f32[16,1024]{1,0:T(8,128)} %rhs.1, f32[64,1920]{1,0:T(8,128)} %transfer.1), custom_call_target="tpu_custom_call" | custom-call | flops 4000000000 | bytes 1048576 | tf_op jit(solution)/shard_map/gram/pallas_call | solution.py:558
  3.9 0.1 collective-permute-start
  4.0 1.2 %collective-permute-done.refs_1_ = f32[80,64]{1,0:T(8,128)S(1)} collective-permute-done((f32[80,64]{1,0:T(8,128)S(1)}, f32[80,64]{1,0:T(8,128)S(1)}, u32[]{:S(2)}, u32[]{:S(2)}) %collective-permute-start) | collective-permute-done | bytes 20512 | tf_op jit(solution)/shard_map/ppermute | solution.py:491
  5.2 0.4 %climb.2 = (f32[80,64]{1,0:T(8,128)S(1)}, f32[2,80,128]{2,1,0:T(8,128)S(1)}) custom-call(f32[64,896]{1,0:T(8,128)S(1)} %bitcast.2, f32[80,64]{1,0:T(8,128)S(1)} %get-tuple-element.18.refs_0_, f32[80,64]{1,0:T(8,128)S(1)} %collective-permute-done.refs_1_), custom_call_target="tpu_custom_call" | custom-call | flops 1000000000 | bytes 1048576 | tf_op jit(solution)/shard_map/climb/pallas_call | solution.py:508
  5.6 1.6 %collective-permute-start.1 = (f32[80,64]{1,0:T(8,128)S(1)}, f32[80,64]{1,0:T(8,128)S(1)}, u32[]{:S(2)}, u32[]{:S(2)}) collective-permute-start(f32[80,64]{1,0:T(8,128)S(1)} %get-tuple-element.22.refs_0_), channel_id=1, source_target_pairs={{0,2},{1,3},{2,0},{3,1},{4,6},{5,7},{6,4},{7,5},{8,10},{9,11},{10,... | collective-permute-start | bytes 61448 | tf_op jit(solution)/shard_map/ppermute | solution.py:491
  7.2 2.6 %collective-permute-start.2 = (f32[80,64]{1,0:T(8,128)S(1)}, f32[80,64]{1,0:T(8,128)S(1)}, u32[]{:S(2)}, u32[]{:S(2)}) collective-permute-start(f32[80,64]{1,0:T(8,128)S(1)} %get-tuple-element.22.refs_0_), channel_id=1, source_target_pairs={{0,4},{1,5},{2,6},{3,7},{4,0},{5,1},{6,2},{7,3},{8,12},{9,13},{10,... | collective-permute-start | bytes 61448 | tf_op jit(solution)/shard_map/ppermute | solution.py:491
  9.8 0.2 collective-permute-start.3
  10.1 6.0 %local_factors.1 = (f32[1024,128]{1,0:T(8,128)S(1)}, f32[16,2944]{1,0:T(8,128)S(1)}, s32[16]{0:T(128)S(1)}, s32[1,30]{1,0:T(1,128)S(1)}) custom-call(f32[1024,128]{1,0:T(8,128)S(1)} %get-tuple-element.16.gram, f32[16,1920]{1,0:T(8,128)S(1)} %get-tuple-element.17.z, f32[16,1024]{1,0:T(8,128)S(1)} %copy-done.8, ...), custom_call_target="tpu_custom_call" | custom-call | flops 8000000000 | bytes 1048576 | tf_op jit(solution)/shard_map/local_factors/pallas_call | solution.py:522
  16.1 0.0 collective-permute-done.1.refs_1_
  16.1 0.0 collective-permute-done.2.refs_2_
  16.1 0.0 collective-permute-done.3.refs_3_
  16.1 0.0 copy-start.5
  16.2 0.0 copy-start.6
  16.2 0.0 copy-start.7
  16.2 0.8 %climb.3 = (f32[80,64]{1,0:T(8,128)S(1)}, f32[4,80,128]{2,1,0:T(8,128)S(1)}, f32[16,2944]{1,0:T(8,128)S(1)}) custom-call(f32[64,896]{1,0:T(8,128)S(1)} %bitcast.3, f32[80,64]{1,0:T(8,128)S(1)} %get-tuple-element.22.refs_0_, f32[80,64]{1,0:T(8,128)S(1)} %collective-permute-done.1.refs_1_, ...), custom_call_target="tpu_custom_call", output_to_operand_aliasing={{2}: (5, {})} | custom-call | flops 1000000000 | bytes 1048576 | tf_op jit(solution)/shard_map/climb/pallas_call | solution.py:508
  17.0 1.5 %collective-permute-start.6 = (f32[80,64]{1,0:T(8,128)S(1)}, f32[80,64]{1,0:T(8,128)S(1)}, u32[]{:S(2)}, u32[]{:S(2)}) collective-permute-start(f32[80,64]{1,0:T(8,128)S(1)} %get-tuple-element.26.refs_0_), channel_id=1, source_target_pairs={{0,8},{8,0},{16,24},{24,16},{1,9},{9,1},{17,25},{25,17},{2,10},{10... | collective-permute-start | bytes 61448 | tf_op jit(solution)/shard_map/ppermute | solution.py:491
  18.5 0.5 %collective-permute-start.7 = (f32[80,64]{1,0:T(8,128)S(1)}, f32[80,64]{1,0:T(8,128)S(1)}, u32[]{:S(2)}, u32[]{:S(2)}) collective-permute-start(f32[80,64]{1,0:T(8,128)S(1)} %get-tuple-element.26.refs_0_), channel_id=1, source_target_pairs={{0,16},{8,24},{16,0},{24,8},{1,17},{9,25},{17,1},{25,9},{2,18},{10... | collective-permute-start | bytes 61448 | tf_op jit(solution)/shard_map/ppermute | solution.py:491
  19.0 1.5 %collective-permute-start.8 = (f32[80,64]{1,0:T(8,128)S(1)}, f32[80,64]{1,0:T(8,128)S(1)}, u32[]{:S(2)}, u32[]{:S(2)}) collective-permute-start(f32[80,64]{1,0:T(8,128)S(1)} %get-tuple-element.26.refs_0_), channel_id=1, source_target_pairs={{0,24},{8,16},{16,8},{24,0},{1,25},{9,17},{17,9},{25,1},{2,26},{10... | collective-permute-start | bytes 61448 | tf_op jit(solution)/shard_map/ppermute | solution.py:491
  20.5 0.0 collective-permute-start.4
  20.5 6.7 %collective-permute-start.5 = (f32[16,2944]{1,0:T(8,128)S(1)}, f32[16,2944]{1,0:T(8,128)S(1)}, u32[]{:S(2)}, u32[]{:S(2)}) collective-permute-start(f32[16,2944]{1,0:T(8,128)S(1)} %get-tuple-element.24.own), channel_id=1, source_target_pairs={{1,2},{3,4},{5,6},{7,8},{9,10},{11,12},{13,14},{15,16},{17,18},{19... | collective-permute-start | bytes 565256 | tf_op jit(solution)/shard_map/ppermute | solution.py:598
  27.2 0.0 collective-permute-done.6.refs_1_
  27.2 0.0 collective-permute-done.7.refs_2_
  27.2 0.0 collective-permute-done.8.refs_3_
  27.3 0.0 copy-start
  27.3 0.0 copy-start.1
  27.3 0.0 copy-start.2
  27.3 0.0 copy-start.3
  27.3 7.0 %top.1 = (f32[16,64]{1,0:T(8,128)S(1)}, f32[64,64]{1,0:T(8,128)}) custom-call(f32[64,384]{1,0:T(8,128)S(1)} %copy-done.6, f32[64,384]{1,0:T(8,128)S(1)} %copy-done.7, f32[64,896]{1,0:T(8,128)S(1)} %bitcast.4, f32[64,896]{1,0:T(8,128)S(1)} %bitcast.5, f32[80,64]{1,0:T(8,128)S(1)} %get-tuple-element.26.refs_0_, f32[80,64]{1,0:T(8,128)S(1)} %collective-permute-done.6.refs_1_, ...), custom_call_target="tpu_custom_call" | custom-call | flops 7000000000 | bytes 1048576 | tf_op jit(solution)/shard_map/top/pallas_call | solution.py:610
  34.3 0.0 collective-permute-done.4.twin
  34.3 0.0 collective-permute-done.5.beside
  34.4 3.3 %couple.1 = f32[16,1024]{1,0:T(8,128)} custom-call(s32[16]{0:T(128)S(1)} %get-tuple-element.20.near_partner_in, s32[1,30]{1,0:T(1,128)S(1)} %get-tuple-element.21.far_partner_in, f32[16,2944]{1,0:T(8,128)S(1)} %get-tuple-element.24.own, f32[16,2944]{1,0:T(8,128)S(1)} %collective-permute-done.4.twin, f32[16,2944]{1,0:T(8,128)S(1)} %collective-permute-done.5.beside, ...), custom_call_target="tpu_custom_call" | custom-call | flops 3000000000 | bytes 1048576 | tf_op jit(solution)/shard_map/couple/pallas_call | solution.py:629
  (10 shorter events, 0.0 us)
Async XLA Ops:
  0.6 4.6 %copy-start.4 = (f32[1,64,896]{2,1,0:T(8,128)S(1)}, f32[1,64,896]{2,1,0:T(8,128)}, u32[]{:S(2)}) copy-start(f32[1,64,896]{2,1,0:T(8,128)} %param.18) | copy-start | bytes 688132
  3.9 1.3 %collective-permute-start = (f32[80,64]{1,0:T(8,128)S(1)}, f32[80,64]{1,0:T(8,128)S(1)}, u32[]{:S(2)}, u32[]{:S(2)}) collective-permute-start(f32[80,64]{1,0:T(8,128)S(1)} %get-tuple-element.18.refs_0_), channel_id=1, source_target_pairs={{0,1},{1,0},{2,3},{3,2},{4,5},{5,4},{6,7},{7,6},{8,9},{9,8},{10,11... | collective-permute-start | bytes 61448 | tf_op jit(solution)/shard_map/ppermute | solution.py:491
  5.2 4.9 %copy-start.8 = (f32[16,1024]{1,0:T(8,128)S(1)}, f32[16,1024]{1,0:T(8,128)}, u32[]{:S(2)}) copy-start(f32[16,1024]{1,0:T(8,128)} %rhs.1) | copy-start | bytes 196612
  5.6 10.5 %collective-permute-start.1 = (f32[80,64]{1,0:T(8,128)S(1)}, f32[80,64]{1,0:T(8,128)S(1)}, u32[]{:S(2)}, u32[]{:S(2)}) collective-permute-start(f32[80,64]{1,0:T(8,128)S(1)} %get-tuple-element.22.refs_0_), channel_id=1, source_target_pairs={{0,2},{1,3},{2,0},{3,1},{4,6},{5,7},{6,4},{7,5},{8,10},{9,11},{10,... | collective-permute-start | bytes 61448 | tf_op jit(solution)/shard_map/ppermute | solution.py:491
  7.2 8.9 %collective-permute-start.2 = (f32[80,64]{1,0:T(8,128)S(1)}, f32[80,64]{1,0:T(8,128)S(1)}, u32[]{:S(2)}, u32[]{:S(2)}) collective-permute-start(f32[80,64]{1,0:T(8,128)S(1)} %get-tuple-element.22.refs_0_), channel_id=1, source_target_pairs={{0,4},{1,5},{2,6},{3,7},{4,0},{5,1},{6,2},{7,3},{8,12},{9,13},{10,... | collective-permute-start | bytes 61448 | tf_op jit(solution)/shard_map/ppermute | solution.py:491
  9.8 6.3 %collective-permute-start.3 = (f32[80,64]{1,0:T(8,128)S(1)}, f32[80,64]{1,0:T(8,128)S(1)}, u32[]{:S(2)}, u32[]{:S(2)}) collective-permute-start(f32[80,64]{1,0:T(8,128)S(1)} %get-tuple-element.22.refs_0_), channel_id=1, source_target_pairs={{0,6},{1,7},{2,4},{3,5},{4,2},{5,3},{6,0},{7,1},{8,14},{9,15},{10,... | collective-permute-start | bytes 61448 | tf_op jit(solution)/shard_map/ppermute | solution.py:491
  16.1 11.1 %copy-start.5 = (f32[1,64,896]{2,1,0:T(8,128)S(1)}, f32[1,64,896]{2,1,0:T(8,128)}, u32[]{:S(2)}) copy-start(f32[1,64,896]{2,1,0:T(8,128)} %param.19) | copy-start | bytes 688132
  16.2 11.1 %copy-start.6 = (f32[64,384]{1,0:T(8,128)S(1)}, f32[64,384]{1,0:T(8,128)}, u32[]{:S(2)}) copy-start(f32[64,384]{1,0:T(8,128)} %grp_transfer.1) | copy-start | bytes 294916
  16.2 11.1 %copy-start.7 = (f32[64,384]{1,0:T(8,128)S(1)}, f32[64,384]{1,0:T(8,128)}, u32[]{:S(2)}) copy-start(f32[64,384]{1,0:T(8,128)} %grp_coupling.1) | copy-start | bytes 294916
  17.0 10.2 %collective-permute-start.6 = (f32[80,64]{1,0:T(8,128)S(1)}, f32[80,64]{1,0:T(8,128)S(1)}, u32[]{:S(2)}, u32[]{:S(2)}) collective-permute-start(f32[80,64]{1,0:T(8,128)S(1)} %get-tuple-element.26.refs_0_), channel_id=1, source_target_pairs={{0,8},{8,0},{16,24},{24,16},{1,9},{9,1},{17,25},{25,17},{2,10},{10... | collective-permute-start | bytes 61448 | tf_op jit(solution)/shard_map/ppermute | solution.py:491
  18.5 8.7 %collective-permute-start.7 = (f32[80,64]{1,0:T(8,128)S(1)}, f32[80,64]{1,0:T(8,128)S(1)}, u32[]{:S(2)}, u32[]{:S(2)}) collective-permute-start(f32[80,64]{1,0:T(8,128)S(1)} %get-tuple-element.26.refs_0_), channel_id=1, source_target_pairs={{0,16},{8,24},{16,0},{24,8},{1,17},{9,25},{17,1},{25,9},{2,18},{10... | collective-permute-start | bytes 61448 | tf_op jit(solution)/shard_map/ppermute | solution.py:491
  19.0 8.2 %collective-permute-start.8 = (f32[80,64]{1,0:T(8,128)S(1)}, f32[80,64]{1,0:T(8,128)S(1)}, u32[]{:S(2)}, u32[]{:S(2)}) collective-permute-start(f32[80,64]{1,0:T(8,128)S(1)} %get-tuple-element.26.refs_0_), channel_id=1, source_target_pairs={{0,24},{8,16},{16,8},{24,0},{1,25},{9,17},{17,9},{25,1},{2,26},{10... | collective-permute-start | bytes 61448 | tf_op jit(solution)/shard_map/ppermute | solution.py:491
  20.5 13.8 %collective-permute-start.4 = (f32[16,2944]{1,0:T(8,128)S(1)}, f32[16,2944]{1,0:T(8,128)S(1)}, u32[]{:S(2)}, u32[]{:S(2)}) collective-permute-start(f32[16,2944]{1,0:T(8,128)S(1)} %get-tuple-element.24.own), channel_id=1, source_target_pairs={{0,1},{1,0},{2,3},{3,2},{4,5},{5,4},{6,7},{7,6},{8,9},{9,8},{10,11... | collective-permute-start | bytes 565256 | tf_op jit(solution)/shard_map/ppermute | solution.py:596
  20.5 13.8 %collective-permute-start.5 = (f32[16,2944]{1,0:T(8,128)S(1)}, f32[16,2944]{1,0:T(8,128)S(1)}, u32[]{:S(2)}, u32[]{:S(2)}) collective-permute-start(f32[16,2944]{1,0:T(8,128)S(1)} %get-tuple-element.24.own), channel_id=1, source_target_pairs={{1,2},{3,4},{5,6},{7,8},{9,10},{11,12},{13,14},{15,16},{17,18},{19... | collective-permute-start | bytes 565256 | tf_op jit(solution)/shard_map/ppermute | solution.py:598
  27.3 7.1 %copy-start = (f32[64,2048]{1,0:T(8,128)S(1)}, f32[64,2048]{1,0:T(8,128)}, u32[]{:S(2)}) copy-start(f32[64,2048]{1,0:T(8,128)} %near.1) | copy-start | bytes 1572868
  27.3 7.1 %copy-start.1 = (f32[64,1920]{1,0:T(8,128)S(1)}, f32[64,1920]{1,0:T(8,128)}, u32[]{:S(2)}) copy-start(f32[64,1920]{1,0:T(8,128)} %transfer.1) | copy-start | bytes 1474564
  27.3 7.1 %copy-start.2 = (f32[64,1920]{1,0:T(8,128)S(1)}, f32[64,1920]{1,0:T(8,128)}, u32[]{:S(2)}) copy-start(f32[64,1920]{1,0:T(8,128)} %coupling.1) | copy-start | bytes 1474564
  27.3 7.1 %copy-start.3 = (f32[64,1024]{1,0:T(8,128)S(1)}, f32[64,1024]{1,0:T(8,128)}, u32[]{:S(2)}) copy-start(f32[64,1024]{1,0:T(8,128)} %basis.1) | copy-start | bytes 786436

commit v5 on v4

--- a/solution.py
+++ b/solution.py
@@ -90,9 +90,49 @@
     )
 
 
-def factor_batch(a, m):
+def spaced(tasks, step, steps):
+    return tasks[len(tasks) * step // steps : len(tasks) * (step + 1) // steps]
+
+
+def invert_pairs(gram, a, m, inv, count):
     blocks = RANK // 8
     sub = lax.broadcasted_iota(jnp.int32, (8, LANES), 0)
+
+    def load(i):
+        rows = gram[pl.ds(i, count, stride=RANK), :]
+        both = jnp.concatenate([rows, swap_halves(rows)], axis=0)
+        first = i - i % 8
+        a[i, first:RANK, 0 : 2 * count] = both[:, 0:RANK].T[first:]
+
+    def store(i):
+        width = i - i % 8 + 8
+        rows = m[i, 0:width, 0 : 2 * count].T
+        if width < RANK:
+            rest = jnp.zeros((2 * count, RANK - width), jnp.float32)
+            rows = jnp.concatenate([rows, rest], axis=1)
+        inv[pl.ds(i, count, stride=RANK), :] = jnp.concatenate([rows[:count], rows[count:]], axis=1)
+
+    def trail(kb, i):
+        k0, first = 8 * kb, i - i % 8
+        acc = a[i, first:RANK, :]
+        old = m[i, 0:k0, :] if kb else None
+        new = None
+        for k in range(k0, k0 + 8):
+            f = a[k, i : i + 1, :]
+            acc = acc - f * a[k, first:RANK, :]
+            part = f * m[k, 0 : k0 + 8, :]
+            if kb:
+                old = old - part[0:k0]
+            tail = part[k0 : k0 + 8]
+            new = -tail if new is None else new - tail
+        a[i, first:RANK, :] = acc
+        if kb:
+            m[i, 0:k0, :] = old
+        m[i, k0 : k0 + 8, :] = new
+
+    for i in range(8):
+        load(i)
+    tasks = [functools.partial(load, i) for i in range(8, RANK)]
     for kb in range(blocks):
         k0 = 8 * kb
         rows = [a[k0 + k, k0:RANK, :] for k in range(8)]
@@ -108,42 +148,20 @@
                 f = rows[k][k2 : k2 + 1, :]
                 rows[k2] = rows[k2] - f * rows[k]
                 mrows[k2] = mrows[k2] - f * mrows[k]
+            for task in spaced(tasks, k, 8):
+                task()
         for k in range(8):
             a[k0 + k, k0:RANK, :] = rows[k]
             m[k0 + k, 0 : k0 + 8, :] = mrows[k]
-        for ib in range(kb + 1, blocks):
-            for i in range(8 * ib, 8 * ib + 8):
-                acc = a[i, 8 * ib : RANK, :]
-                old = m[i, 0:k0, :] if kb else None
-                new = None
-                for k in range(8):
-                    f = a[k0 + k, i : i + 1, :]
-                    acc = acc - f * a[k0 + k, 8 * ib : RANK, :]
-                    part = f * m[k0 + k, 0 : k0 + 8, :]
-                    if kb:
-                        old = old - part[0:k0]
-                    tail = part[k0 : k0 + 8]
-                    new = -tail if new is None else new - tail
-                a[i, 8 * ib : RANK, :] = acc
-                if kb:
-                    m[i, 0:k0, :] = old
-                m[i, k0 : k0 + 8, :] = new
-
-
-def invert_pairs(gram, a, m, inv, count):
-    for i in range(RANK):
-        rows = gram[pl.ds(i, count, stride=RANK), :]
-        both = jnp.concatenate([rows, swap_halves(rows)], axis=0)
-        first = i - i % 8
-        a[i, first:RANK, 0 : 2 * count] = both[:, 0:RANK].T[first:]
-    factor_batch(a, m)
-    for i in range(RANK):
-        width = i - i % 8 + 8
-        rows = m[i, 0:width, 0 : 2 * count].T
-        if width < RANK:
-            rest = jnp.zeros((2 * count, RANK - width), jnp.float32)
-            rows = jnp.concatenate([rows, rest], axis=1)
-        inv[pl.ds(i, count, stride=RANK), :] = jnp.concatenate([rows[:count], rows[count:]], axis=1)
+        stores = [functools.partial(store, i) for i in range(k0, k0 + 8)]
+        for i in range(k0 + 8, min(k0 + 16, RANK)):
+            trail(kb, i)
+        trails = [functools.partial(trail, kb, i) for i in range(k0 + 16, RANK)]
+        tasks = []
+        for step in range(8):
+            tasks += spaced(trails, step, 8) + spaced(stores, step, 8)
+    for task in tasks:
+        task()
 
 
 def gram_kernel(basis_in, rhs_in, transfer_in, gram, z_out, top, basis, rhs, transfer, sems):

time: 38 us -> 38 us (level)
  transfers between devices with their start and end apart: 9 -> 9, of which waited for: 1 -> 1; matrix products, arithmetic and copies ran while one was open for 0% -> 0% of each run, Pallas kernels for 34% -> 35%
where the time goes in v5:
time: 38 us; the launch traced here: 37.8 us
  Pallas kernels  20.8 us (55%)
  starting transfers between devices  14.7 us (39%)
  waiting for transfers between devices  1.23 us (3%)
  between operations  1 us (3%)
    ppermute x7, starting transfers between devices, exchange(): lax.ppermute(block, axis, [(i, i ^ k << start) for i in range(count)])  8.08 us
    pallas_call x1, Pallas kernels, shards(): pl.pallas_call(functools.partial(top_kernel, grp_count, dev_count, start,...  7.01 us
    ppermute x1, starting transfers between devices, shards(): beside = lax.ppermute(packed, both, pairs + [(j, i) for i, j in pairs])  6.66 us
    pallas_call x1, Pallas kernels, local_call(): pl.pallas_call(local_kernel, out_shape=[f32(BATCH * RANK, PAIR), f32(NRHS...  6.04 us
    pallas_call x1, Pallas kernels, shards(): pl.pallas_call(couple_kernel, out_shape=f32(NRHS, POINT_SPAN), in_specs=[...  3.33 us
    pallas_call x1, Pallas kernels, shards(): pl.pallas_call(gram_kernel, out_shape=[f32(BATCH * RANK, PAIR), f32(NRHS,...  3.28 us
    ppermute x7, waiting for transfers between devices, exchange(): lax.ppermute(block, axis, [(i, i ^ k << start) for i in range(count)])  1.22 us
    pallas_call x2, Pallas kernels, climb_call(): pl.pallas_call(functools.partial(climb_kernel, axis, start, bits, count),...  1.17 us
  transfers between devices with their start and end apart: 9, of which 1 were waited for; matrix products, arithmetic and copies ran while one was open for 0% of the time, Pallas kernels for 35%

profile of v5, /device:TPU:4, one launch (start us, length us, event | category | flops | bytes accessed | tf_op | source)
XLA Modules:
  0.0 37.8 jit_solution(14661947436966522968)
XLA Ops:
  0.6 0.0 copy-start.4
  0.6 3.3 %gram.1 = (f32[1024,128]{1,0:T(8,128)S(1)}, f32[16,1920]{1,0:T(8,128)S(1)}, f32[80,64]{1,0:T(8,128)S(1)}) custom-call(f32[64,1024]{1,0:T(8,128)} %basis.1, f32[16,1024]{1,0:T(8,128)} %rhs.1, f32[64,1920]{1,0:T(8,128)} %transfer.1), custom_call_target="tpu_custom_call" | custom-call | flops 4000000000 | bytes 1048576 | tf_op jit(solution)/shard_map/gram/pallas_call | solution.py:576
  3.9 0.1 collective-permute-start
  4.0 1.2 %collective-permute-done.refs_1_ = f32[80,64]{1,0:T(8,128)S(1)} collective-permute-done((f32[80,64]{1,0:T(8,128)S(1)}, f32[80,64]{1,0:T(8,128)S(1)}, u32[]{:S(2)}, u32[]{:S(2)}) %collective-permute-start) | collective-permute-done | bytes 20512 | tf_op jit(solution)/shard_map/ppermute | solution.py:509
  5.2 0.4 %climb.2 = (f32[80,64]{1,0:T(8,128)S(1)}, f32[2,80,128]{2,1,0:T(8,128)S(1)}) custom-call(f32[64,896]{1,0:T(8,128)S(1)} %bitcast.2, f32[80,64]{1,0:T(8,128)S(1)} %get-tuple-element.18.refs_0_, f32[80,64]{1,0:T(8,128)S(1)} %collective-permute-done.refs_1_), custom_call_target="tpu_custom_call" | custom-call | flops 1000000000 | bytes 1048576 | tf_op jit(solution)/shard_map/climb/pallas_call | solution.py:526
  5.6 1.6 %collective-permute-start.1 = (f32[80,64]{1,0:T(8,128)S(1)}, f32[80,64]{1,0:T(8,128)S(1)}, u32[]{:S(2)}, u32[]{:S(2)}) collective-permute-start(f32[80,64]{1,0:T(8,128)S(1)} %get-tuple-element.22.refs_0_), channel_id=1, source_target_pairs={{0,2},{1,3},{2,0},{3,1},{4,6},{5,7},{6,4},{7,5},{8,10},{9,11},{10,... | collective-permute-start | bytes 61448 | tf_op jit(solution)/shard_map/ppermute | solution.py:509
  7.2 2.6 %collective-permute-start.2 = (f32[80,64]{1,0:T(8,128)S(1)}, f32[80,64]{1,0:T(8,128)S(1)}, u32[]{:S(2)}, u32[]{:S(2)}) collective-permute-start(f32[80,64]{1,0:T(8,128)S(1)} %get-tuple-element.22.refs_0_), channel_id=1, source_target_pairs={{0,4},{1,5},{2,6},{3,7},{4,0},{5,1},{6,2},{7,3},{8,12},{9,13},{10,... | collective-permute-start | bytes 61448 | tf_op jit(solution)/shard_map/ppermute | solution.py:509
  9.8 0.2 collective-permute-start.3
  10.1 6.0 %local_factors.1 = (f32[1024,128]{1,0:T(8,128)S(1)}, f32[16,2944]{1,0:T(8,128)S(1)}, s32[16]{0:T(128)S(1)}, s32[1,30]{1,0:T(1,128)S(1)}) custom-call(f32[1024,128]{1,0:T(8,128)S(1)} %get-tuple-element.16.gram, f32[16,1920]{1,0:T(8,128)S(1)} %get-tuple-element.17.z, f32[16,1024]{1,0:T(8,128)S(1)} %copy-done.8, ...), custom_call_target="tpu_custom_call" | custom-call | flops 8000000000 | bytes 1048576 | tf_op jit(solution)/shard_map/local_factors/pallas_call | solution.py:540
  16.1 0.0 collective-permute-done.1.refs_1_
  16.1 0.0 collective-permute-done.2.refs_2_
  16.1 0.0 collective-permute-done.3.refs_3_
  16.1 0.0 copy-start.5
  16.2 0.0 copy-start.6
  16.2 0.0 copy-start.7
  16.2 0.8 %climb.3 = (f32[80,64]{1,0:T(8,128)S(1)}, f32[4,80,128]{2,1,0:T(8,128)S(1)}, f32[16,2944]{1,0:T(8,128)S(1)}) custom-call(f32[64,896]{1,0:T(8,128)S(1)} %bitcast.3, f32[80,64]{1,0:T(8,128)S(1)} %get-tuple-element.22.refs_0_, f32[80,64]{1,0:T(8,128)S(1)} %collective-permute-done.1.refs_1_, ...), custom_call_target="tpu_custom_call", output_to_operand_aliasing={{2}: (5, {})} | custom-call | flops 1000000000 | bytes 1048576 | tf_op jit(solution)/shard_map/climb/pallas_call | solution.py:526
  17.0 1.5 %collective-permute-start.6 = (f32[80,64]{1,0:T(8,128)S(1)}, f32[80,64]{1,0:T(8,128)S(1)}, u32[]{:S(2)}, u32[]{:S(2)}) collective-permute-start(f32[80,64]{1,0:T(8,128)S(1)} %get-tuple-element.26.refs_0_), channel_id=1, source_target_pairs={{0,8},{8,0},{16,24},{24,16},{1,9},{9,1},{17,25},{25,17},{2,10},{10... | collective-permute-start | bytes 61448 | tf_op jit(solution)/shard_map/ppermute | solution.py:509
  18.5 0.5 %collective-permute-start.7 = (f32[80,64]{1,0:T(8,128)S(1)}, f32[80,64]{1,0:T(8,128)S(1)}, u32[]{:S(2)}, u32[]{:S(2)}) collective-permute-start(f32[80,64]{1,0:T(8,128)S(1)} %get-tuple-element.26.refs_0_), channel_id=1, source_target_pairs={{0,16},{8,24},{16,0},{24,8},{1,17},{9,25},{17,1},{25,9},{2,18},{10... | collective-permute-start | bytes 61448 | tf_op jit(solution)/shard_map/ppermute | solution.py:509
  19.0 1.5 %collective-permute-start.8 = (f32[80,64]{1,0:T(8,128)S(1)}, f32[80,64]{1,0:T(8,128)S(1)}, u32[]{:S(2)}, u32[]{:S(2)}) collective-permute-start(f32[80,64]{1,0:T(8,128)S(1)} %get-tuple-element.26.refs_0_), channel_id=1, source_target_pairs={{0,24},{8,16},{16,8},{24,0},{1,25},{9,17},{17,9},{25,1},{2,26},{10... | collective-permute-start | bytes 61448 | tf_op jit(solution)/shard_map/ppermute | solution.py:509
  20.5 0.0 collective-permute-start.4
  20.5 6.7 %collective-permute-start.5 = (f32[16,2944]{1,0:T(8,128)S(1)}, f32[16,2944]{1,0:T(8,128)S(1)}, u32[]{:S(2)}, u32[]{:S(2)}) collective-permute-start(f32[16,2944]{1,0:T(8,128)S(1)} %get-tuple-element.24.own), channel_id=1, source_target_pairs={{1,2},{3,4},{5,6},{7,8},{9,10},{11,12},{13,14},{15,16},{17,18},{19... | collective-permute-start | bytes 565256 | tf_op jit(solution)/shard_map/ppermute | solution.py:616
  27.2 0.0 collective-permute-done.6.refs_1_
  27.2 0.0 collective-permute-done.7.refs_2_
  27.2 0.0 collective-permute-done.8.refs_3_
  27.2 0.0 copy-start
  27.3 0.0 copy-start.1
  27.3 0.0 copy-start.2
  27.3 0.0 copy-start.3
  27.3 7.0 %top.1 = (f32[16,64]{1,0:T(8,128)S(1)}, f32[64,64]{1,0:T(8,128)}) custom-call(f32[64,384]{1,0:T(8,128)S(1)} %copy-done.6, f32[64,384]{1,0:T(8,128)S(1)} %copy-done.7, f32[64,896]{1,0:T(8,128)S(1)} %bitcast.4, f32[64,896]{1,0:T(8,128)S(1)} %bitcast.5, f32[80,64]{1,0:T(8,128)S(1)} %get-tuple-element.26.refs_0_, f32[80,64]{1,0:T(8,128)S(1)} %collective-permute-done.6.refs_1_, ...), custom_call_target="tpu_custom_call" | custom-call | flops 7000000000 | bytes 1048576 | tf_op jit(solution)/shard_map/top/pallas_call | solution.py:628
  34.3 0.0 collective-permute-done.4.twin
  34.3 0.0 collective-permute-done.5.beside
  34.4 3.3 %couple.1 = f32[16,1024]{1,0:T(8,128)} custom-call(s32[16]{0:T(128)S(1)} %get-tuple-element.20.near_partner_in, s32[1,30]{1,0:T(1,128)S(1)} %get-tuple-element.21.far_partner_in, f32[16,2944]{1,0:T(8,128)S(1)} %get-tuple-element.24.own, f32[16,2944]{1,0:T(8,128)S(1)} %collective-permute-done.4.twin, f32[16,2944]{1,0:T(8,128)S(1)} %collective-permute-done.5.beside, ...), custom_call_target="tpu_custom_call" | custom-call | flops 3000000000 | bytes 1048576 | tf_op jit(solution)/shard_map/couple/pallas_call | solution.py:647
  (10 shorter events, 0.0 us)
Async XLA Ops:
  0.6 4.6 %copy-start.4 = (f32[1,64,896]{2,1,0:T(8,128)S(1)}, f32[1,64,896]{2,1,0:T(8,128)}, u32[]{:S(2)}) copy-start(f32[1,64,896]{2,1,0:T(8,128)} %param.18) | copy-start | bytes 688132
  3.9 1.3 %collective-permute-start = (f32[80,64]{1,0:T(8,128)S(1)}, f32[80,64]{1,0:T(8,128)S(1)}, u32[]{:S(2)}, u32[]{:S(2)}) collective-permute-start(f32[80,64]{1,0:T(8,128)S(1)} %get-tuple-element.18.refs_0_), channel_id=1, source_target_pairs={{0,1},{1,0},{2,3},{3,2},{4,5},{5,4},{6,7},{7,6},{8,9},{9,8},{10,11... | collective-permute-start | bytes 61448 | tf_op jit(solution)/shard_map/ppermute | solution.py:509
  5.2 4.9 %copy-start.8 = (f32[16,1024]{1,0:T(8,128)S(1)}, f32[16,1024]{1,0:T(8,128)}, u32[]{:S(2)}) copy-start(f32[16,1024]{1,0:T(8,128)} %rhs.1) | copy-start | bytes 196612
  5.6 10.5 %collective-permute-start.1 = (f32[80,64]{1,0:T(8,128)S(1)}, f32[80,64]{1,0:T(8,128)S(1)}, u32[]{:S(2)}, u32[]{:S(2)}) collective-permute-start(f32[80,64]{1,0:T(8,128)S(1)} %get-tuple-element.22.refs_0_), channel_id=1, source_target_pairs={{0,2},{1,3},{2,0},{3,1},{4,6},{5,7},{6,4},{7,5},{8,10},{9,11},{10,... | collective-permute-start | bytes 61448 | tf_op jit(solution)/shard_map/ppermute | solution.py:509
  7.2 8.9 %collective-permute-start.2 = (f32[80,64]{1,0:T(8,128)S(1)}, f32[80,64]{1,0:T(8,128)S(1)}, u32[]{:S(2)}, u32[]{:S(2)}) collective-permute-start(f32[80,64]{1,0:T(8,128)S(1)} %get-tuple-element.22.refs_0_), channel_id=1, source_target_pairs={{0,4},{1,5},{2,6},{3,7},{4,0},{5,1},{6,2},{7,3},{8,12},{9,13},{10,... | collective-permute-start | bytes 61448 | tf_op jit(solution)/shard_map/ppermute | solution.py:509
  9.8 6.3 %collective-permute-start.3 = (f32[80,64]{1,0:T(8,128)S(1)}, f32[80,64]{1,0:T(8,128)S(1)}, u32[]{:S(2)}, u32[]{:S(2)}) collective-permute-start(f32[80,64]{1,0:T(8,128)S(1)} %get-tuple-element.22.refs_0_), channel_id=1, source_target_pairs={{0,6},{1,7},{2,4},{3,5},{4,2},{5,3},{6,0},{7,1},{8,14},{9,15},{10,... | collective-permute-start | bytes 61448 | tf_op jit(solution)/shard_map/ppermute | solution.py:509
  16.1 11.1 %copy-start.5 = (f32[1,64,896]{2,1,0:T(8,128)S(1)}, f32[1,64,896]{2,1,0:T(8,128)}, u32[]{:S(2)}) copy-start(f32[1,64,896]{2,1,0:T(8,128)} %param.19) | copy-start | bytes 688132
  16.2 11.1 %copy-start.6 = (f32[64,384]{1,0:T(8,128)S(1)}, f32[64,384]{1,0:T(8,128)}, u32[]{:S(2)}) copy-start(f32[64,384]{1,0:T(8,128)} %grp_transfer.1) | copy-start | bytes 294916
  16.2 11.1 %copy-start.7 = (f32[64,384]{1,0:T(8,128)S(1)}, f32[64,384]{1,0:T(8,128)}, u32[]{:S(2)}) copy-start(f32[64,384]{1,0:T(8,128)} %grp_coupling.1) | copy-start | bytes 294916
  17.0 10.2 %collective-permute-start.6 = (f32[80,64]{1,0:T(8,128)S(1)}, f32[80,64]{1,0:T(8,128)S(1)}, u32[]{:S(2)}, u32[]{:S(2)}) collective-permute-start(f32[80,64]{1,0:T(8,128)S(1)} %get-tuple-element.26.refs_0_), channel_id=1, source_target_pairs={{0,8},{8,0},{16,24},{24,16},{1,9},{9,1},{17,25},{25,17},{2,10},{10... | collective-permute-start | bytes 61448 | tf_op jit(solution)/shard_map/ppermute | solution.py:509
  18.5 8.7 %collective-permute-start.7 = (f32[80,64]{1,0:T(8,128)S(1)}, f32[80,64]{1,0:T(8,128)S(1)}, u32[]{:S(2)}, u32[]{:S(2)}) collective-permute-start(f32[80,64]{1,0:T(8,128)S(1)} %get-tuple-element.26.refs_0_), channel_id=1, source_target_pairs={{0,16},{8,24},{16,0},{24,8},{1,17},{9,25},{17,1},{25,9},{2,18},{10... | collective-permute-start | bytes 61448 | tf_op jit(solution)/shard_map/ppermute | solution.py:509
  19.0 8.2 %collective-permute-start.8 = (f32[80,64]{1,0:T(8,128)S(1)}, f32[80,64]{1,0:T(8,128)S(1)}, u32[]{:S(2)}, u32[]{:S(2)}) collective-permute-start(f32[80,64]{1,0:T(8,128)S(1)} %get-tuple-element.26.refs_0_), channel_id=1, source_target_pairs={{0,24},{8,16},{16,8},{24,0},{1,25},{9,17},{17,9},{25,1},{2,26},{10... | collective-permute-start | bytes 61448 | tf_op jit(solution)/shard_map/ppermute | solution.py:509
  20.5 13.8 %collective-permute-start.4 = (f32[16,2944]{1,0:T(8,128)S(1)}, f32[16,2944]{1,0:T(8,128)S(1)}, u32[]{:S(2)}, u32[]{:S(2)}) collective-permute-start(f32[16,2944]{1,0:T(8,128)S(1)} %get-tuple-element.24.own), channel_id=1, source_target_pairs={{0,1},{1,0},{2,3},{3,2},{4,5},{5,4},{6,7},{7,6},{8,9},{9,8},{10,11... | collective-permute-start | bytes 565256 | tf_op jit(solution)/shard_map/ppermute | solution.py:614
  20.5 13.8 %collective-permute-start.5 = (f32[16,2944]{1,0:T(8,128)S(1)}, f32[16,2944]{1,0:T(8,128)S(1)}, u32[]{:S(2)}, u32[]{:S(2)}) collective-permute-start(f32[16,2944]{1,0:T(8,128)S(1)} %get-tuple-element.24.own), channel_id=1, source_target_pairs={{1,2},{3,4},{5,6},{7,8},{9,10},{11,12},{13,14},{15,16},{17,18},{19... | collective-permute-start | bytes 565256 | tf_op jit(solution)/shard_map/ppermute | solution.py:616
  27.2 7.1 %copy-start = (f32[64,2048]{1,0:T(8,128)S(1)}, f32[64,2048]{1,0:T(8,128)}, u32[]{:S(2)}) copy-start(f32[64,2048]{1,0:T(8,128)} %near.1) | copy-start | bytes 1572868
  27.3 7.1 %copy-start.1 = (f32[64,1920]{1,0:T(8,128)S(1)}, f32[64,1920]{1,0:T(8,128)}, u32[]{:S(2)}) copy-start(f32[64,1920]{1,0:T(8,128)} %transfer.1) | copy-start | bytes 1474564
  27.3 7.1 %copy-start.2 = (f32[64,1920]{1,0:T(8,128)S(1)}, f32[64,1920]{1,0:T(8,128)}, u32[]{:S(2)}) copy-start(f32[64,1920]{1,0:T(8,128)} %coupling.1) | copy-start | bytes 1474564
  27.3 7.1 %copy-start.3 = (f32[64,1024]{1,0:T(8,128)S(1)}, f32[64,1024]{1,0:T(8,128)}, u32[]{:S(2)}) copy-start(f32[64,1024]{1,0:T(8,128)} %basis.1) | copy-start | bytes 786436
